TPU v7x, 512 devices: a whole 4x8x8 slice. The times are simulated.
512 devices in a mesh: leaf: 128 (over z, y, core), vec: 4 (over x).
Axes of the slice: x: 4, y: 8, z: 8, core: 2. Of those that a mesh axis runs over, the one named last changes fastest.
Arguments:
- vectors: bfloat16 [64, 131072], P('vec', 'leaf'), may hold values from -6 to 6
- points: float32 [3, 131072], P(None, 'leaf'), may hold values from 0 to 1
- near_cols: int32 [12, 2048], P(None, 'leaf'), may hold values from 0 to 2047, as said below
- near_count: int32 [2048], P('leaf'), may hold values from 3 to 12, as said below
- basis: bfloat16 [32, 131072], P(None, 'leaf'), may hold values from -0.75 to 0.75
- xfer_low: bfloat16 [3840, 1024], P('leaf'), may hold values from -0.75 to 0.75
- couple_low: bfloat16 [3, 3968, 1024], P(None, 'leaf'), may hold values from -0.4375 to 0.4375
- xfer_top: bfloat16 [254, 1024], replicated, may hold values from -0.75 to 0.75
- couple_top: bfloat16 [3, 124, 1024], replicated, may hold values from -0.4375 to 0.4375
Outputs:
- result: bfloat16 [64, 131072], P('vec', 'leaf')
Inputs may be any that keep to these rules, and one draw needn't show every extreme that they name: `near_cols`: entries of leaf i name leaves within 8 of i; entries 0, 1 and 2 of leaf i are i, min(i + 8, 2047) and max(i - 8, 0). Entries 0 to near_count[i] - 1 of leaf i are live; some leaf has 12.
All inputs are finite; a program needn't handle non-finite values.
Results may differ from a plain program's by a relative error of at most 0.0034.
Values may be sent and summed in bfloat16 or wider, within the bound.
No kernel may reach another device: no remote copies, remote signals or barrier semaphores. Data moves between devices by JAX's collectives and lax.ppermute only.
A program may use at most 64 MiB of HBM per device.

v0:
```python
import math

import jax
import jax.numpy as jnp
from jax import lax
from jax.sharding import PartitionSpec as P

MATVECS = 2
HALO = 8


KERNEL_LENGTH = 0.25
SOFTEN = 0.01
HIGHEST = lax.Precision.HIGHEST


def with_halo(cells, sides, width):
    for axis, dim in sides:
        count = lax.axis_size(axis)
        ends = count - 1
        head = lax.slice_in_dim(cells, 0, width, axis=dim)
        tail = lax.slice_in_dim(cells, cells.shape[dim] - width, cells.shape[dim], axis=dim)
        cells = jnp.concatenate(
            [
                lax.ppermute(tail, axis, [(i, (i + 1) % count) for i in range(ends)]),
                cells,
                lax.ppermute(head, axis, [((i + 1) % count, i) for i in range(ends)]),
            ],
            axis=dim,
        )
    return cells


def kernel_block(target, source, active, kernel_gain):
    squares = jnp.zeros((target.shape[1], target.shape[2], source.shape[2]), jnp.float32)
    for coord in range(3):
        spread = target[coord][:, :, None] - source[coord][:, None, :]
        squares = squares + spread * spread
    values = kernel_gain * jnp.exp(-jnp.sqrt(squares + SOFTEN) / KERNEL_LENGTH)
    return jnp.where(active[:, None, None], values, 0.0).astype(jnp.bfloat16)


def square_table(xfer, rank_size):
    return xfer.astype(jnp.float32).reshape(xfer.shape[:-1] + (rank_size, rank_size))


def raise_level(children, xfer):
    weights = square_table(xfer, children.shape[1])
    terms = jnp.einsum("vsn,nsr->vrn", children, weights, precision=HIGHEST)
    return terms.reshape(terms.shape[0], terms.shape[1], terms.shape[2] // 2, 2).sum(axis=3)


def lower_level(parents, xfer):
    widened = jnp.repeat(parents, 2, axis=2)
    weights = square_table(xfer, parents.shape[1])
    return jnp.einsum("vrn,nsr->vsn", widened, weights, precision=HIGHEST)


def interact(padded, table, first_node):
    node_count = table.shape[1]
    parity = (jnp.arange(node_count, dtype=jnp.int32) + first_node) % 2
    minus_three = padded[:, :, 0:node_count]
    minus_two = padded[:, :, 1 : 1 + node_count]
    plus_two = padded[:, :, 5 : 5 + node_count]
    plus_three = padded[:, :, 6 : 6 + node_count]
    third = jnp.where((parity == 0)[None, None, :], plus_three, minus_three)
    weights = square_table(table, padded.shape[1])
    result = jnp.einsum("vsn,nrs->vrn", minus_two, weights[0], precision=HIGHEST)
    result = result + jnp.einsum("vsn,nrs->vrn", plus_two, weights[1], precision=HIGHEST)
    return result + jnp.einsum("vsn,nrs->vrn", third, weights[2], precision=HIGHEST)


def pad_nodes(values):
    return jnp.pad(values, ((0, 0), (0, 0), (3, 3)))


def local_slice(table, leaf_dev, height):
    node_count = leaf_dev >> height
    first_node = 2 * leaf_dev - 2 * node_count
    return table[..., first_node : first_node + node_count, :]


def near_field(signal_ext, points, point_ext, local_cols, near_count, kernel_gain):
    vector_count = signal_ext.shape[0]
    leaf_dev = near_count.shape[0]
    leaf_size = points.shape[1] // leaf_dev
    sources = signal_ext.reshape(vector_count, -1, leaf_size)
    source_places = point_ext.reshape(3, -1, leaf_size)
    targets = points.reshape(3, leaf_dev, leaf_size)

    def one_slot(carry, inputs):
        columns, slot_index = inputs
        gathered = jnp.take(sources, columns, axis=1)
        kernel_tile = kernel_block(
            targets, jnp.take(source_places, columns, axis=1), slot_index < near_count, kernel_gain
        )
        update = jnp.einsum(
            "nab,vnb->vna", kernel_tile, gathered, preferred_element_type=jnp.float32
        )
        return (carry + update, None)

    initial = jnp.zeros((vector_count, leaf_dev, leaf_size), jnp.float32)
    slot_ids = jnp.arange(local_cols.shape[0], dtype=jnp.int32)
    result, _ = lax.scan(one_slot, initial, (local_cols, slot_ids))
    return result.reshape(vector_count, leaf_dev * leaf_size)


def padded_lower(upward, levels_dev):
    padded_list = []
    for height in range(levels_dev - 1):
        padded_list.append(with_halo(upward[height], (("leaf", 2),), 3))
    return padded_list


def far_field(signal, basis, xfer_low, couple_low, xfer_top, couple_top, place, leaf_dev):
    vector_count = signal.shape[0]
    rank_size = basis.shape[0]
    leaf_size = basis.shape[1] // leaf_dev
    levels_dev = leaf_dev.bit_length() - 1
    devices = lax.axis_size("leaf")
    levels_top = devices.bit_length() - 1
    blocks = signal.reshape(vector_count, leaf_dev, leaf_size)
    basis_blocks = basis.reshape(rank_size, leaf_dev, leaf_size)
    upward = [jnp.einsum("vnp,rnp->vrn", blocks, basis_blocks, preferred_element_type=jnp.float32)]
    for height in range(levels_dev):
        upward.append(raise_level(upward[height], local_slice(xfer_low, leaf_dev, height)))
    padded_list = padded_lower(upward, levels_dev)
    couplings = []
    for height in range(levels_dev - 1):
        node_count = leaf_dev >> height
        couplings.append(
            interact(
                padded_list[height], local_slice(couple_low, leaf_dev, height), place * node_count
            )
        )
    pairs = upward[levels_dev - 1]
    roots = upward[levels_dev]
    all_pairs, all_roots = (
        lax.all_gather(pairs, "leaf", axis=2, tiled=True),
        lax.all_gather(roots, "leaf", axis=2, tiled=True),
    )
    pair_pad = lax.dynamic_slice_in_dim(pad_nodes(all_pairs), 2 * place, 8, 2)
    couplings.append(
        interact(pair_pad, local_slice(couple_low, leaf_dev, levels_dev - 1), 2 * place)
    )
    root_pad = lax.dynamic_slice_in_dim(pad_nodes(all_roots), place, 7, 2)
    couplings.append(interact(root_pad, local_slice(couple_low, leaf_dev, levels_dev), place))
    summary = [all_roots]
    for height in range(levels_top):
        node_count = devices >> height
        first_node = 2 * devices - 2 * node_count
        summary.append(raise_level(summary[height], xfer_top[first_node : first_node + node_count]))
    downward = jnp.zeros((vector_count, rank_size, 1), jnp.float32)
    for height in range(levels_top - 1, 0, -1):
        node_count = devices >> height
        first_node = 2 * devices - 2 * node_count
        downward = lower_level(downward, xfer_top[first_node : first_node + node_count])
        if height <= levels_top - 2:
            couple_first = devices - 2 * node_count
            table = couple_top[:, couple_first : couple_first + node_count]
            downward = downward + interact(pad_nodes(summary[height]), table, 0)
    parent = lax.dynamic_slice_in_dim(downward, place // 2, 1, 2)
    own_xfer = square_table(lax.dynamic_slice_in_dim(xfer_top, place, 1, 0), rank_size)
    lowered = jnp.einsum("vrn,nsr->vsn", parent, own_xfer, precision=HIGHEST)
    downward = couplings[levels_dev] + lowered
    for height in range(levels_dev - 1, -1, -1):
        downward = couplings[height] + lower_level(
            downward, local_slice(xfer_low, leaf_dev, height)
        )
    basis_wide = basis_blocks.astype(jnp.float32)
    result = jnp.einsum("vrn,rnp->vnp", downward, basis_wide, precision=HIGHEST)
    return result.reshape(vector_count, leaf_dev * leaf_size)


def body(vectors, points, near_cols, near_count, basis, xfer_low, couple_low, xfer_top, couple_top):
    leaf_dev = near_count.shape[0]
    leaf_size = points.shape[1] // leaf_dev
    reach = HALO
    place = lax.axis_index("leaf")
    point_ext = with_halo(points, (("leaf", 1),), reach * leaf_size)
    local_cols = near_cols - (place * leaf_dev - reach)
    kernel_gain = 4.0 / math.sqrt(leaf_size * near_cols.shape[0])
    signal = vectors
    for repeat in range(MATVECS):
        signal_ext = with_halo(signal, (("leaf", 1),), reach * leaf_size)
        near_part = near_field(signal_ext, points, point_ext, local_cols, near_count, kernel_gain)
        far_part = far_field(
            signal, basis, xfer_low, couple_low, xfer_top, couple_top, place, leaf_dev
        )
        signal = (near_part + far_part).astype(jnp.bfloat16)
    return signal


def solution(mesh):
    placed = (
        P("vec", "leaf"),
        P(None, "leaf"),
        P(None, "leaf"),
        P("leaf"),
        P(None, "leaf"),
        P("leaf", None),
        P(None, "leaf", None),
        P(),
        P(),
    )
    return jax.shard_map(
        body, mesh=mesh, in_specs=placed, out_specs=P("vec", "leaf"), check_vma=False
    )
```

profile of v0, /device:TPU:249, one launch (start us, length us, event | category | flops | bytes accessed | tf_op | source)
XLA Modules:
  0.0 505.0 jit_solution(8998861083362565271)
XLA Ops:
  5.1 5.0 collective-permute-start.8
  10.1 1.9 collective-permute-start.9
  12.6 7.0 %collective-permute-start.6 = (f32[16,32,3]{1,0,2:T(8,128)}, f32[16,32,3]{1,0,2:T(8,128)}, u32[]{:S(2)}, u32[]{:S(2)}) collective-permute-start(f32[16,32,3]{1,0,2:T(8,128)} %get-tuple-element.274), channel_id=1, source_target_pairs={{0,4},{4,8},{8,12},{12,16},{16,20},{20,24},{24,28},{28,32},{32,36}... | collective-permute-start | bytes 18440 | tf_op jit(solution)/shard_map/ppermute | solution.py:25
  19.6 1.9 collective-permute-start.7
  22.2 7.0 %collective-permute-start.4 = (f32[16,32,3]{1,0,2:T(8,128)}, f32[16,32,3]{1,0,2:T(8,128)}, u32[]{:S(2)}, u32[]{:S(2)}) collective-permute-start(f32[16,32,3]{1,0,2:T(8,128)} %get-tuple-element.270), channel_id=1, source_target_pairs={{0,4},{4,8},{8,12},{12,16},{16,20},{20,24},{24,28},{28,32},{32,36}... | collective-permute-start | bytes 18440 | tf_op jit(solution)/shard_map/ppermute | solution.py:25
  45.4 47.9 %all_gather.12 = f32[16,32,256]{1,0,2:T(8,128)S(1)} all-gather(f32[16,32,2]{1,0,2:T(8,128)S(1)} %bitcast_reduce_fusion.15), channel_id=1, replica_groups=mesh['leaf'=128,'vec'=4] {'leaf'}, dimensions={2}, use_global_device_ids=true | all-gather | bytes 528384 | tf_op jit(solution)/shard_map/all_gather | solution.py:139
  93.6 48.0 %all_gather.13 = f32[16,32,128]{1,0,2:T(8,128)S(1)} all-gather(f32[16,32,1]{1,0,2:T(8,128)S(1)} %fusion.339), channel_id=1, replica_groups=mesh['leaf'=128,'vec'=4] {'leaf'}, dimensions={2}, use_global_device_ids=true | all-gather | bytes 264192 | tf_op jit(solution)/shard_map/all_gather | solution.py:140
  142.7 2.3 copy.77
  158.9 2.3 bitcast_reduce_fusion.1
  178.1 1.9 fusion.358
  185.1 2.3 fusion.359
  195.3 2.2 fusion.343
  202.8 2.5 copy.86
  207.0 2.5 copy.82
  209.4 2.9 fusion.360
  214.1 2.5 copy.84
  216.6 2.9 fusion.361
  220.2 2.4 fusion.97
  230.0 2.1 collective-permute-start.5
  232.9 6.8 %collective-permute-start.2 = (f32[3,512]{1,0:T(4,128)S(1)}, f32[3,512]{1,0:T(4,128)S(1)}, u32[]{:S(2)}, u32[]{:S(2)}) collective-permute-start(f32[3,512]{1,0:T(4,128)S(1)} %get-tuple-element.283), channel_id=1, source_target_pairs={{0,4},{4,8},{8,12},{12,16},{16,20},{20,24},{24,28},{28,32},{32,36}... | collective-permute-start | bytes 18440 | tf_op jit(solution)/shard_map/ppermute | solution.py:25
  244.8 7.0 %collective-permute-start = (bf16[16,512]{1,0:T(8,128)(2,1)S(1)}, bf16[16,512]{1,0:T(8,128)(2,1)S(1)}, u32[]{:S(2)}, u32[]{:S(2)}) collective-permute-start(bf16[16,512]{1,0:T(8,128)(2,1)S(1)} %copy-done.75), channel_id=1, source_target_pairs={{0,4},{4,8},{8,12},{12,16},{16,20},{20,24},{24,28},{28,32},{32,36}... | collective-permute-start | bytes 49160 | tf_op jit(solution)/shard_map/ppermute | solution.py:25
  258.8 3.7 collective-permute-done.1
  262.8 42.7 %while.22 = (s32[]{:T(128)}, f32[16,16,64]{2,0,1:T(8,128)S(1)}, s32[12,16]{1,0:T(8,128)S(1)}, bf16[16,32,64]{2,0,1:T(8,128)(2,1)S(1)}, s32[12]{0:T(128)S(1)}, /*...) while((s32[]{:T(128)}, f32[16,16,64]{2,0,1:T(8,128)S(1)}, ...), condition=%wide.region_1.0_spmd.clone, body=%wide.region_0.3_spmd.clone.sunk | while | flops 3068019 | bytes 356947 | solution.py:104
  306.7 47.7 %all_gather.15 = f32[16,32,128]{1,0,2:T(8,128)S(1)} all-gather(f32[16,32,1]{1,0,2:T(8,128)S(1)} %fusion.347), channel_id=1, replica_groups=mesh['leaf'=128,'vec'=4] {'leaf'}, dimensions={2}, use_global_device_ids=true | all-gather | bytes 264192 | tf_op jit(solution)/shard_map/all_gather | solution.py:140
  363.1 49.7 %all_gather.14 = f32[16,32,256]{1,0,2:T(8,128)S(1)} all-gather(f32[16,32,2]{1,0,2:T(8,128)S(1)} %bitcast_reduce_fusion.14), channel_id=1, replica_groups=mesh['leaf'=128,'vec'=4] {'leaf'}, dimensions={2}, use_global_device_ids=true | all-gather | bytes 528384 | tf_op jit(solution)/shard_map/all_gather | solution.py:139
  413.1 2.1 collective-permute-start.13
  415.2 6.8 %collective-permute-start.12 = (f32[16,32,3]{1,0,2:T(8,128)S(1)}, f32[16,32,3]{1,0,2:T(8,128)}, u32[]{:S(2)}, u32[]{:S(2)}) collective-permute-start(f32[16,32,3]{1,0,2:T(8,128)S(1)} %get-tuple-element.268), channel_id=1, source_target_pairs={{0,4},{4,8},{8,12},{12,16},{16,20},{20,24},{24,28},{28,32},{32,36}... | collective-permute-start | bytes 18440 | tf_op jit(solution)/shard_map/ppermute | solution.py:25
  423.9 7.0 %collective-permute-start.14 = (f32[16,32,3]{1,0,2:T(8,128)S(1)}, f32[16,32,3]{1,0,2:T(8,128)S(1)}, u32[]{:S(2)}, u32[]{:S(2)}) collective-permute-start(f32[16,32,3]{1,0,2:T(8,128)S(1)} %get-tuple-element.272), channel_id=1, source_target_pairs={{0,4},{4,8},{8,12},{12,16},{16,20},{20,24},{24,28},{28,32},{32,36}... | collective-permute-start | bytes 18440 | tf_op jit(solution)/shard_map/ppermute | solution.py:25
  439.4 5.4 %collective-permute-start.16 = (f32[16,32,3]{1,0,2:T(8,128)S(1)}, f32[16,32,3]{1,0,2:T(8,128)S(1)}, u32[]{:S(2)}, u32[]{:S(2)}) collective-permute-start(f32[16,32,3]{1,0,2:T(8,128)S(1)} %get-tuple-element.276), channel_id=1, source_target_pairs={{0,4},{4,8},{8,12},{12,16},{16,20},{20,24},{24,28},{28,32},{32,36}... | collective-permute-start | bytes 18440 | tf_op jit(solution)/shard_map/ppermute | solution.py:25
  445.7 7.5 %collective-permute-start.10 = (bf16[16,512]{1,0:T(8,128)(2,1)S(1)}, bf16[16,512]{1,0:T(8,128)(2,1)S(1)}, u32[]{:S(2)}, u32[]{:S(2)}) collective-permute-start(bf16[16,512]{1,0:T(8,128)(2,1)S(1)} %get-tuple-element.277), channel_id=1, source_target_pairs={{0,4},{4,8},{8,12},{12,16},{16,20},{20,24},{24,28},{28,32},{32,36}... | collective-permute-start | bytes 49160 | tf_op jit(solution)/shard_map/ppermute | solution.py:25
  460.2 2.1 collective-permute-done.11
  462.5 41.2 %while.23 = (s32[]{:T(128)}, f32[16,16,64]{2,0,1:T(8,128)S(1)}, s32[12,16]{1,0:T(8,128)S(1)}, bf16[16,32,64]{2,0,1:T(8,128)(2,1)S(1)}, s32[12]{0:T(128)S(1)}, /*...) while((s32[]{:T(128)}, f32[16,16,64]{2,0,1:T(8,128)S(1)}, ...), condition=%wide.region_11.14_spmd.clone, body=%wide.region_10.13_spmd.clone.sunk | while | flops 3068019 | bytes 356947 | solution.py:104
  (645 shorter events, 208.4 us)
Async XLA Ops:
  0.0 31.5 %copy-start.33 = (bf16[254,1024]{1,0:T(8,128)(2,1)S(1)}, bf16[254,1024]{1,0:T(8,128)(2,1)}, u32[]{:S(2)}) copy-start(bf16[254,1024]{1,0:T(8,128)(2,1)} %param.24) | copy-start | bytes 1560580
  0.0 35.2 %copy-start.28 = (bf16[3,124,1024]{2,1,0:T(8,128)(2,1)S(1)}, bf16[3,124,1024]{2,1,0:T(8,128)(2,1)}, u32[]{:S(2)}) copy-start(bf16[3,124,1024]{2,1,0:T(8,128)(2,1)} %param.25) | copy-start | bytes 2285572
  2.6 38.8 %copy-start.48 = (bf16[3,31,1024]{2,1,0:T(8,128)(2,1)S(1)}, bf16[3,31,1024]{2,1,0:T(8,128)(2,1)}, u32[]{:S(2)}) copy-start(bf16[3,31,1024]{2,1,0:T(8,128)(2,1)} %param.23) | copy-start | bytes 571396
  3.7 40.8 %copy-start.6 = (bf16[16,32,32]{2,1,0:T(8,128)(2,1)}, bf16[16,32,32]{2,1,0:T(8,128)(2,1)S(1)}, u32[]{:S(2)}) copy-start(bf16[16,32,32]{2,1,0:T(8,128)(2,1)S(1)} %reshape.504) | copy-start | bytes 98308
  3.7 40.8 %copy-start.40 = (bf16[16,1024]{1,0:T(8,128)(2,1)S(1)}, bf16[16,1024]{1,0:T(8,128)(2,1)}, u32[]{:S(2)}) copy-start(bf16[16,1024]{1,0:T(8,128)(2,1)} %param.17) | copy-start | bytes 98308
  3.8 41.3 %copy-start.14 = (bf16[8,32,32]{2,1,0:T(8,128)(2,1)}, bf16[8,32,32]{2,1,0:T(8,128)(2,1)S(1)}, u32[]{:S(2)}) copy-start(bf16[8,32,32]{2,1,0:T(8,128)(2,1)S(1)} %reshape.506) | copy-start | bytes 49156
  3.8 41.3 %slice-start.1 = ((bf16[30,1024]{1,0:T(8,128)(2,1)}), bf16[4,1024]{1,0:T(4,128)(2,1)S(1)}, s32[]{:S(2)}) async-start(bf16[30,1024]{1,0:T(8,128)(2,1)} %param.22), calls=%async_computation.1 | async-start | bytes 16384 | tf_op jit(solution)/shard_map/slice | solution.py:80
  4.5 88.9 %copy-start.20 = (f32[16,32,4]{1,0,2:T(8,128)}, f32[16,32,4]{1,0,2:T(8,128)S(1)}, u32[]{:S(2)}) copy-start(f32[16,32,4]{1,0,2:T(8,128)S(1)} %bitcast_reduce_fusion.13) | copy-start | bytes 24580
  5.1 227.8 %collective-permute-start.8 = (f32[16,32,3]{1,0,2:T(8,128)}, f32[16,32,3]{1,0,2:T(8,128)}, u32[]{:S(2)}, u32[]{:S(2)}) collective-permute-start(f32[16,32,3]{1,0,2:T(8,128)} %get-tuple-element.280), channel_id=1, source_target_pairs={{0,4},{4,8},{8,12},{12,16},{16,20},{20,24},{24,28},{28,32},{32,36}... | collective-permute-start | bytes 18440 | tf_op jit(solution)/shard_map/ppermute | solution.py:25
  10.1 219.9 %collective-permute-start.9 = (f32[16,32,3]{1,0,2:T(8,128)}, f32[16,32,3]{1,0,2:T(8,128)}, u32[]{:S(2)}, u32[]{:S(2)}) collective-permute-start(f32[16,32,3]{1,0,2:T(8,128)} %get-tuple-element.279), channel_id=1, source_target_pairs={{4,0},{8,4},{12,8},{16,12},{20,16},{24,20},{28,24},{32,28},{36,32}... | collective-permute-start | bytes 18440 | tf_op jit(solution)/shard_map/ppermute | solution.py:27
  12.6 232.2 %collective-permute-start.6 = (f32[16,32,3]{1,0,2:T(8,128)}, f32[16,32,3]{1,0,2:T(8,128)}, u32[]{:S(2)}, u32[]{:S(2)}) collective-permute-start(f32[16,32,3]{1,0,2:T(8,128)} %get-tuple-element.274), channel_id=1, source_target_pairs={{0,4},{4,8},{8,12},{12,16},{16,20},{20,24},{24,28},{28,32},{32,36}... | collective-permute-start | bytes 18440 | tf_op jit(solution)/shard_map/ppermute | solution.py:25
  19.6 222.3 %collective-permute-start.7 = (f32[16,32,3]{1,0,2:T(8,128)}, f32[16,32,3]{1,0,2:T(8,128)}, u32[]{:S(2)}, u32[]{:S(2)}) collective-permute-start(f32[16,32,3]{1,0,2:T(8,128)} %get-tuple-element.273), channel_id=1, source_target_pairs={{4,0},{8,4},{12,8},{16,12},{20,16},{24,20},{28,24},{32,28},{36,32}... | collective-permute-start | bytes 18440 | tf_op jit(solution)/shard_map/ppermute | solution.py:27
  22.2 234.2 %collective-permute-start.4 = (f32[16,32,3]{1,0,2:T(8,128)}, f32[16,32,3]{1,0,2:T(8,128)}, u32[]{:S(2)}, u32[]{:S(2)}) collective-permute-start(f32[16,32,3]{1,0,2:T(8,128)} %get-tuple-element.270), channel_id=1, source_target_pairs={{0,4},{4,8},{8,12},{12,16},{16,20},{20,24},{24,28},{28,32},{32,36}... | collective-permute-start | bytes 18440 | tf_op jit(solution)/shard_map/ppermute | solution.py:25
  45.2 48.4 %copy-start.26 = (bf16[4,32,32]{2,1,0:T(8,128)(2,1)}, bf16[4,32,32]{2,1,0:T(8,128)(2,1)S(1)}, u32[]{:S(2)}) copy-start(bf16[4,32,32]{2,1,0:T(8,128)(2,1)S(1)} %reshape.508) | copy-start | bytes 24580
  45.4 48.1 %copy-start.34 = (bf16[2,32,32]{2,1,0:T(8,128)(2,1)}, bf16[2,32,32]{2,1,0:T(8,128)(2,1)S(1)}, u32[]{:S(2)}) copy-start(bf16[2,32,32]{2,1,0:T(8,128)(2,1)S(1)} %reshape.510) | copy-start | bytes 12292
  93.6 56.7 %slice-start = ((bf16[254,1024]{1,0:T(8,128)(2,1)}), bf16[8,1024]{1,0:T(8,128)(2,1)S(1)}, s32[]{:S(2)}) async-start(bf16[254,1024]{1,0:T(8,128)(2,1)} %param.24), calls=%async_computation | async-start | bytes 32768 | tf_op jit(solution)/shard_map/slice | solution.py:157
  230.0 24.1 %collective-permute-start.5 = (f32[16,32,3]{1,0,2:T(8,128)S(1)}, f32[16,32,3]{1,0,2:T(8,128)S(1)}, u32[]{:S(2)}, u32[]{:S(2)}) collective-permute-start(f32[16,32,3]{1,0,2:T(8,128)S(1)} %copy-done.73), channel_id=1, source_target_pairs={{4,0},{8,4},{12,8},{16,12},{20,16},{24,20},{28,24},{32,28},{36,32}... | collective-permute-start | bytes 18440 | tf_op jit(solution)/shard_map/ppermute | solution.py:27
  232.9 25.6 %collective-permute-start.2 = (f32[3,512]{1,0:T(4,128)S(1)}, f32[3,512]{1,0:T(4,128)S(1)}, u32[]{:S(2)}, u32[]{:S(2)}) collective-permute-start(f32[3,512]{1,0:T(4,128)S(1)} %get-tuple-element.283), channel_id=1, source_target_pairs={{0,4},{4,8},{8,12},{12,16},{16,20},{20,24},{24,28},{28,32},{32,36}... | collective-permute-start | bytes 18440 | tf_op jit(solution)/shard_map/ppermute | solution.py:25
  241.9 16.7 %collective-permute-start.3 = (f32[3,512]{1,0:T(4,128)S(1)}, f32[3,512]{1,0:T(4,128)S(1)}, u32[]{:S(2)}, u32[]{:S(2)}) collective-permute-start(f32[3,512]{1,0:T(4,128)S(1)} %get-tuple-element.284), channel_id=1, source_target_pairs={{4,0},{8,4},{12,8},{16,12},{20,16},{24,20},{28,24},{32,28},{36,32}... | collective-permute-start | bytes 18440 | tf_op jit(solution)/shard_map/ppermute | solution.py:27
  244.8 14.0 %collective-permute-start = (bf16[16,512]{1,0:T(8,128)(2,1)S(1)}, bf16[16,512]{1,0:T(8,128)(2,1)S(1)}, u32[]{:S(2)}, u32[]{:S(2)}) collective-permute-start(bf16[16,512]{1,0:T(8,128)(2,1)S(1)} %copy-done.75), channel_id=1, source_target_pairs={{0,4},{4,8},{8,12},{12,16},{16,20},{20,24},{24,28},{28,32},{32,36}... | collective-permute-start | bytes 49160 | tf_op jit(solution)/shard_map/ppermute | solution.py:25
  254.1 8.4 %collective-permute-start.1 = (bf16[16,512]{1,0:T(8,128)(2,1)S(1)}, bf16[16,512]{1,0:T(8,128)(2,1)S(1)}, u32[]{:S(2)}, u32[]{:S(2)}) collective-permute-start(bf16[16,512]{1,0:T(8,128)(2,1)S(1)} %copy-done.74), channel_id=1, source_target_pairs={{4,0},{8,4},{12,8},{16,12},{20,16},{24,20},{28,24},{32,28},{36,32}... | collective-permute-start | bytes 49160 | tf_op jit(solution)/shard_map/ppermute | solution.py:27
  305.4 48.9 %copy-start.3 = (bf16[128,32,32]{2,1,0:T(8,128)(2,1)S(1)}, bf16[128,32,32]{2,1,0:T(8,128)(2,1)}, u32[]{:S(2)}) copy-start(bf16[128,32,32]{2,1,0:T(8,128)(2,1)} %copy.77) | copy-start | bytes 786436
  306.1 49.3 %copy-start.2 = (bf16[64,32,32]{2,1,0:T(8,128)(2,1)S(1)}, bf16[64,32,32]{2,1,0:T(8,128)(2,1)}, u32[]{:S(2)}) copy-start(bf16[64,32,32]{2,1,0:T(8,128)(2,1)} %copy.79) | copy-start | bytes 393220
  363.1 49.7 %copy-start.84 = (pred[2]{0:T(512)(128)(4,1)S(1)}, pred[2]{0:T(512)(128)(4,1)}, u32[]{:S(2)}) copy-start(pred[2]{0:T(512)(128)(4,1)} %fusion.272) | copy-start | bytes 10
  413.1 43.8 %collective-permute-start.13 = (f32[16,32,3]{1,0,2:T(8,128)S(1)}, f32[16,32,3]{1,0,2:T(8,128)}, u32[]{:S(2)}, u32[]{:S(2)}) collective-permute-start(f32[16,32,3]{1,0,2:T(8,128)S(1)} %get-tuple-element.267), channel_id=1, source_target_pairs={{4,0},{8,4},{12,8},{16,12},{20,16},{24,20},{28,24},{32,28},{36,32}... | collective-permute-start | bytes 18440 | tf_op jit(solution)/shard_map/ppermute | solution.py:27
  415.2 42.8 %collective-permute-start.12 = (f32[16,32,3]{1,0,2:T(8,128)S(1)}, f32[16,32,3]{1,0,2:T(8,128)}, u32[]{:S(2)}, u32[]{:S(2)}) collective-permute-start(f32[16,32,3]{1,0,2:T(8,128)S(1)} %get-tuple-element.268), channel_id=1, source_target_pairs={{0,4},{4,8},{8,12},{12,16},{16,20},{20,24},{24,28},{28,32},{32,36}... | collective-permute-start | bytes 18440 | tf_op jit(solution)/shard_map/ppermute | solution.py:25
  422.0 31.9 %collective-permute-start.15 = (f32[16,32,3]{1,0,2:T(8,128)S(1)}, f32[16,32,3]{1,0,2:T(8,128)S(1)}, u32[]{:S(2)}, u32[]{:S(2)}) collective-permute-start(f32[16,32,3]{1,0,2:T(8,128)S(1)} %get-tuple-element.271), channel_id=1, source_target_pairs={{4,0},{8,4},{12,8},{16,12},{20,16},{24,20},{28,24},{32,28},{36,32}... | collective-permute-start | bytes 18440 | tf_op jit(solution)/shard_map/ppermute | solution.py:27
  423.9 32.1 %collective-permute-start.14 = (f32[16,32,3]{1,0,2:T(8,128)S(1)}, f32[16,32,3]{1,0,2:T(8,128)S(1)}, u32[]{:S(2)}, u32[]{:S(2)}) collective-permute-start(f32[16,32,3]{1,0,2:T(8,128)S(1)} %get-tuple-element.272), channel_id=1, source_target_pairs={{0,4},{4,8},{8,12},{12,16},{16,20},{20,24},{24,28},{28,32},{32,36}... | collective-permute-start | bytes 18440 | tf_op jit(solution)/shard_map/ppermute | solution.py:25
  430.9 8.5 %collective-permute-start.17 = (f32[16,32,3]{1,0,2:T(8,128)S(1)}, f32[16,32,3]{1,0,2:T(8,128)S(1)}, u32[]{:S(2)}, u32[]{:S(2)}) collective-permute-start(f32[16,32,3]{1,0,2:T(8,128)S(1)} %get-tuple-element.275), channel_id=1, source_target_pairs={{4,0},{8,4},{12,8},{16,12},{20,16},{24,20},{28,24},{32,28},{36,32}... | collective-permute-start | bytes 18440 | tf_op jit(solution)/shard_map/ppermute | solution.py:27
  439.4 6.3 %collective-permute-start.16 = (f32[16,32,3]{1,0,2:T(8,128)S(1)}, f32[16,32,3]{1,0,2:T(8,128)S(1)}, u32[]{:S(2)}, u32[]{:S(2)}) collective-permute-start(f32[16,32,3]{1,0,2:T(8,128)S(1)} %get-tuple-element.276), channel_id=1, source_target_pairs={{0,4},{4,8},{8,12},{12,16},{16,20},{20,24},{24,28},{28,32},{32,36}... | collective-permute-start | bytes 18440 | tf_op jit(solution)/shard_map/ppermute | solution.py:25
  445.7 14.4 %collective-permute-start.10 = (bf16[16,512]{1,0:T(8,128)(2,1)S(1)}, bf16[16,512]{1,0:T(8,128)(2,1)S(1)}, u32[]{:S(2)}, u32[]{:S(2)}) collective-permute-start(bf16[16,512]{1,0:T(8,128)(2,1)S(1)} %get-tuple-element.277), channel_id=1, source_target_pairs={{0,4},{4,8},{8,12},{12,16},{16,20},{20,24},{24,28},{28,32},{32,36}... | collective-permute-start | bytes 49160 | tf_op jit(solution)/shard_map/ppermute | solution.py:25
  453.9 8.4 %collective-permute-start.11 = (bf16[16,512]{1,0:T(8,128)(2,1)S(1)}, bf16[16,512]{1,0:T(8,128)(2,1)S(1)}, u32[]{:S(2)}, u32[]{:S(2)}) collective-permute-start(bf16[16,512]{1,0:T(8,128)(2,1)S(1)} %get-tuple-element.278), channel_id=1, source_target_pairs={{4,0},{8,4},{12,8},{16,12},{20,16},{24,20},{28,24},{32,28},{36,32}... | collective-permute-start | bytes 49160 | tf_op jit(solution)/shard_map/ppermute | solution.py:27
  (83 other events, 590.5 us)
where the time goes:
time: 513 us; the launch traced here: 505 us
  blocking collectives  193 us (38%)
  local copies, waits for them, and re-layouts  116 us (23%)
  matrix products  85.2 us (17%)
  starting transfers between devices  76.9 us (15%)
  other arithmetic  21.9 us (4%)
  waiting for transfers between devices  8.23 us (2%)
    all_gather x2, blocking collectives, far_field(): lax.all_gather(pairs, 'leaf', axis=2, tiled=True)  97.6 us
    all_gather x2, blocking collectives, far_field(): lax.all_gather(roots, 'leaf', axis=2, tiled=True)  95.7 us
    ppermute x9, starting transfers between devices, with_halo(): lax.ppermute(tail, axis, [(i, (i + 1) % count) for i in range(ends)])  59.4 us
    dot_general x24, matrix products, one_slot(): jnp.einsum('nab,vnb->vna', kernel_tile, gathered, preferred_element_type=...  20.9 us
    ppermute x9, starting transfers between devices, with_halo(): lax.ppermute(head, axis, [((i + 1) % count, i) for i in range(ends)])  17.6 us
    dot_general x20, matrix products, interact(): jnp.einsum('vsn,nrs->vrn', minus_two, weights[0], precision=HIGHEST)  16.5 us
    and x24, other arithmetic, one_slot(): gathered = jnp.take(sources, columns, axis=1)  16.3 us
    dot_general x20, matrix products, interact(): jnp.einsum('vsn,nrs->vrn', third, weights[2], precision=HIGHEST)  15.7 us
  transfers between devices with their start and end apart: 18, of which 4 were waited for; matrix products, arithmetic and copies ran while one was open for 24% of the time, Pallas kernels for 0%

commit v1 on v0

v1 whole, which is shorter than its diff:
```python
import math

import jax
import jax.numpy as jnp
from jax import lax
from jax.experimental import pallas as pl
from jax.experimental.pallas import tpu as pltpu
from jax.sharding import PartitionSpec as P

F32 = jnp.float32
BF16 = jnp.bfloat16
HALO = 8
LEAF_DEV = 16
RANK = 32
NEAR = 12
VEC = 16
DEVICES = 128
CHUNKS = 8
LOW = (0, 16, 24, 28, 30)
NODES = (16, 8, 4, 2)
TOP_XFER = (0, 128, 192, 224, 240, 248)
TOP_COUPLE = (0, 0, 64, 96, 112, 120)
SCALE = 4.0 * math.log2(math.e)
SOFT = 0.01 * SCALE * SCALE
LOG_GAIN = math.log2(4.0 / math.sqrt(64 * NEAR))
VMEM_LIMIT = 48 * 1024 * 1024


def nn(a, b):
    return lax.dot_general(a, b, (((1,), (0,)), ((), ())), preferred_element_type=F32)


def nt(a, b):
    return lax.dot_general(a, b, (((1,), (1,)), ((), ())), preferred_element_type=F32)


def tn(a, b):
    return lax.dot_general(a, b, (((0,), (0,)), ((), ())), preferred_element_type=F32)


def halves(x):
    high = x.astype(BF16)
    return high, (x - high.astype(F32)).astype(BF16)


def lanes_in(rows, lo, size, dtype):
    lane = lax.broadcasted_iota(jnp.int32, (rows, 128), 1)
    return ((lane >= lo) & (lane < lo + size)).astype(F32).astype(dtype)


class Masks:
    def __init__(self):
        self.group = [lanes_in(16, 32 * g, 32, BF16) for g in range(4)]
        self.groupf = [lanes_in(16, 32 * g, 32, F32) for g in range(4)]
        self.half = [lanes_in(16, 64 * g, 64, BF16) for g in range(2)]
        self.halff = [lanes_in(16, 64 * g, 64, F32) for g in range(2)]


def spread_matrix():
    row = lax.broadcasted_iota(jnp.int32, (128, 512), 0)
    col = lax.broadcasted_iota(jnp.int32, (128, 512), 1)
    return (row == ((col >> 7) << 5) + (col & 31)).astype(F32).astype(BF16)


def spread_table(table, spread, out, first):
    count = table.shape[0]
    for c in range(8):
        wide = nn(table[:, 128 * c : 128 * c + 128], spread)
        for q in range(4):
            out[pl.ds(first * 32 + 4 * c + q, count, stride=32), :] = wide[:, 128 * q : 128 * q + 128]


def up_pass(signal, basis, xfer, m):
    total = [0.0] * 4
    for c in range(CHUNKS):
        wide = jnp.concatenate([basis[:, 128 * c : 128 * c + 128]] * 4, axis=0)
        both = nt(jnp.concatenate([signal[c] * m.half[0], signal[c] * m.half[1]], axis=0), wide)
        g = (2 * c) % 4
        total[c // 2] = total[c // 2] + both[:16] * m.groupf[g] + both[16:] * m.groupf[g + 1]
    heights = []
    for h in range(4):
        split = [halves(t) for t in total]
        heights.append(split)
        first = LOW[h] * 32
        if h == 3:
            both = nn(jnp.concatenate(split[0], axis=0), xfer[first : first + 128, :])
            return heights, both[:16] + both[16:]
        count = NODES[h] // 4
        total = [0.0] * max(1, count // 2)
        for t in range(count):
            high, low = split[t]
            left = jnp.concatenate(
                [high * m.half[0], high * m.half[1], low * m.half[0], low * m.half[1]], axis=0
            )
            both = nn(left, xfer[first + 128 * t : first + 128 * t + 128, :])
            both = both[:32] + both[32:]
            g = (2 * t) % 4
            total[t // 2] = total[t // 2] + both[:16] * m.groupf[g] + both[16:] * m.groupf[g + 1]


def write_sends(signal, heights, root, left, right, gather, m):
    for c in range(4):
        left[16 * c : 16 * c + 16, :] = signal[c]
        right[16 * c : 16 * c + 16, :] = signal[c + 4]
    for h in range(4):
        for part in range(2):
            at = 64 * (part + 1) + 16 * h
            left[at : at + 16, :] = heights[h][0][part]
            right[at : at + 16, :] = heights[h][-1][part]
    packed = root[0:4] * m.groupf[0][0:4]
    for g in range(1, 4):
        packed = packed + root[4 * g : 4 * g + 4] * m.groupf[g][0:4]
    block = jnp.concatenate([packed] * 4, axis=0).astype(BF16)
    for q in range(DEVICES // 4):
        gather[16 * q : 16 * q + 16, :] = block


def couple_low(heights, from_left, from_right, table, m):
    result = []
    for h in range(4):
        nodes = NODES[h]
        own = heights[h]
        before = [from_left[at : at + 16, :] for at in (64 + 16 * h, 128 + 16 * h)]
        after = [from_right[at : at + 16, :] for at in (64 + 16 * h, 128 + 16 * h)]

        def node(n, part):
            if n < 0:
                return before[part] * m.group[(nodes + n) % 4]
            if n >= nodes:
                return after[part] * m.group[n - nodes]
            return own[n // 4][part] * m.group[n % 4]

        chunks = []
        for t in range(max(1, nodes // 4)):
            targets = range(4 * t, min(4 * t + 4, nodes))
            thirds = [j + 3 if j % 2 == 0 else j - 3 for j in targets]
            left = [
                jnp.concatenate([node(n, part) for part in range(2) for n in slot], axis=0)
                for slot in ([j - 2 for j in targets], [j + 2 for j in targets], thirds)
            ]
            rows = [(31 * k + LOW[h] + 4 * t) * 32 for k in range(3)]
            right = [table[r : r + 128, :] for r in rows]
            wide = nt(jnp.concatenate(left, axis=1), jnp.concatenate(right, axis=1))
            wide = wide[: 16 * len(targets)] + wide[16 * len(targets) :]
            chunk = wide[0:16] * m.groupf[0]
            for j in range(1, len(targets)):
                chunk = chunk + wide[16 * j : 16 * j + 16] * m.groupf[j]
            chunks.append(chunk)
        result.append(chunks)
    return result


def top_apply(gathered, table, m):
    left = []
    for g in range(4):
        left.append(jnp.concatenate([gathered[16 * c : 16 * c + 16, :] * m.group[g] for c in range(32)], axis=1))
    right = [
        jnp.concatenate([table[at + 32 * (c // 4) : at + 32 * (c // 4) + 32, :] for c in range(128)], axis=0)
        for at in (0, 1024)
    ]
    wide = nn(jnp.concatenate(left, axis=0), jnp.concatenate(right, axis=1))
    wide = wide[:, :128] + wide[:, 128:]
    row = lax.broadcasted_iota(jnp.int32, (64, 128), 0)
    lane = lax.broadcasted_iota(jnp.int32, (64, 128), 1)
    wide = jnp.where(((row >> 2) & 3) == (lane >> 5), wide, 0.0)
    parts = []
    for g in range(4):
        block = wide[16 * g : 16 * g + 8] + wide[16 * g + 8 : 16 * g + 16]
        parts.append(block[0:4] + block[4:8])
    total = jnp.concatenate(parts, axis=0)
    total = total + pltpu.roll(total, 64, 1)
    return total + pltpu.roll(total, 32, 1)


def down_pass(root, couplings, xfer, m):
    high, low = halves(root)
    first = LOW[3] * 32
    both = nt(jnp.concatenate([high * m.group[0], low * m.group[0]], axis=0), xfer[first : first + 128, :])
    down = [couplings[3][0] + both[:16] + both[16:]]
    for h in (2, 1, 0):
        first = LOW[h] * 32
        split = [halves(d) for d in down]
        down = []
        for t in range(NODES[h] // 4):
            high, low = split[t // 2]
            g = (2 * t) % 4
            left = [high * m.group[g], high * m.group[g + 1], low * m.group[g], low * m.group[g + 1]]
            both = nt(jnp.concatenate(left, axis=0), xfer[first + 128 * t : first + 128 * t + 128, :])
            both = both[:32] + both[32:]
            down.append(couplings[h][t] + both[:16] * m.halff[0] + both[16:] * m.halff[1])
    return down


def build_top(place, xfer_top, own_couple, couple_top, spread, wide_xfer, wide_couple, levels, top, m):
    spread_table(xfer_top[...], spread, wide_xfer, 0)
    row = lax.broadcasted_iota(jnp.int32, (8, 124), 0)
    col = lax.broadcasted_iota(jnp.int32, (8, 124), 1)
    wanted = jnp.zeros((8, 124), jnp.int32) - 1
    for level in range(1, 6):
        wanted = jnp.where(row == level - 1, TOP_COUPLE[level] + (place >> level), wanted)
    pick = (col == wanted).astype(F32).astype(BF16)
    for k in range(3):
        spread_table(nn(pick, couple_top[k]).astype(BF16), spread, wide_couple, 8 * k)
    row = lax.broadcasted_iota(jnp.int32, (32, 128), 0)
    lane = lax.broadcasted_iota(jnp.int32, (32, 128), 1)
    path = (row == (lane & 31)).astype(F32)
    groupf = [lanes_in(32, 32 * g, 32, F32) for g in range(4)]
    slots = []
    for level in range(6):
        if level == 0:
            tables = [own_couple[(31 * k + 30) * 32 : (31 * k + 31) * 32, :].astype(F32) for k in range(3)]
        else:
            tables = [wide_couple[(8 * k + level - 1) * 32 : (8 * k + level) * 32, :] for k in range(3)]
        at = pl.multiple_of((TOP_XFER[level] + (place >> level)) * 32, 32)
        tables.append(wide_xfer[pl.ds(at, 32), :])
        left = tables[0] * groupf[0]
        for g in range(1, 4):
            left = left + tables[g] * groupf[g]
        left = left.astype(BF16)
        high, low = halves(path)
        both = tn(jnp.concatenate([left, left], axis=0), jnp.concatenate([high, low], axis=0))
        slots.append([both[32 * k : 32 * k + 32] for k in range(3)])
        path = both[96:128]
    row = lax.broadcasted_iota(jnp.int32, (256, 128), 0)
    lane = lax.broadcasted_iota(jnp.int32, (256, 128), 1)
    family = ((row >> 6) == (lane >> 5)).astype(F32)
    for level in range(5, -1, -1):
        here = levels[level]
        count = DEVICES >> level
        if level == 5:
            here[...] = jnp.zeros((128, 128), F32)
        else:
            for t in range(count // 8):
                first = (TOP_XFER[level] + 8 * t) * 32
                left = (wide_xfer[first : first + 256, :] * family).astype(BF16)
                high, low = halves(levels[level + 1][128 * t : 128 * t + 128, :])
                here[256 * t : 256 * t + 256, :] = nn(
                    jnp.concatenate([left, left], axis=1), jnp.concatenate([high, low], axis=0)
                )
        node = place >> level
        third = jnp.where(node % 2 == 0, node + 3, node - 3)
        for k, other in enumerate((node - 2, node + 2, third)):
            live = ((other >= 0) & (other < count)).astype(F32)
            at = pl.multiple_of(jnp.clip(other, 0, count - 1) * 32, 32)
            here[pl.ds(at, 32), :] = here[pl.ds(at, 32), :] + slots[level][k] * live
    for c in range(32):
        block = levels[0][128 * c : 128 * c + 32, :] * groupf[0]
        for g in range(1, 4):
            block = block + levels[0][128 * c + 32 * g : 128 * c + 32 * g + 32, :] * groupf[g]
        top[32 * c : 32 * c + 32, :], top[1024 + 32 * c : 1056 + 32 * c, :] = halves(block)


def point_parts(points):
    high = points.astype(BF16).astype(F32)
    rest = points - high
    mid = rest.astype(BF16).astype(F32)
    low = rest - mid
    return jnp.concatenate([high, mid, low, jnp.zeros((7, points.shape[1]), F32)], axis=0).astype(BF16)


def build_tiles(place, parts, cols, counts, from_left, from_right, near_left, near_right, tiles):
    half = lanes_in(8, 0, 64, F32)
    other = 1.0 - half
    blocks = [from_left[192 + 16 * c : 208 + 16 * c, :] for c in range(4)]
    blocks += [parts[:, 128 * c : 128 * c + 128] for c in range(CHUNKS)]
    blocks += [from_right[192 + 16 * c : 208 + 16 * c, :] for c in range(4)]
    row = lax.broadcasted_iota(jnp.int32, (8, 16), 0)
    col = lax.broadcasted_iota(jnp.int32, (8, 16), 1)
    adder = ((col % 3 == row) & (col < 9) & (row < 3)).astype(F32).astype(BF16)
    for c in range(16):
        joined = nn(adder, blocks[c]) * SCALE
        turned = pltpu.roll(joined, 64, 1)
        near_left[2 * c] = joined * half
        near_right[2 * c + 1] = joined * other
        near_left[2 * c + 1] = turned * half
        near_right[2 * c] = turned * other
    row = lax.broadcasted_iota(jnp.int32, (16, 384), 0)
    col = lax.broadcasted_iota(jnp.int32, (16, 384), 1)
    column = ((row % 3 == (col >> 7)) & (row < 9)).astype(F32).astype(BF16)
    lane = lax.broadcasted_iota(jnp.int32, (1, 128), 1)
    base = place * LEAF_DEV - HALO
    for c in range(CHUNKS):
        targets = tn(parts[:, 128 * c : 128 * c + 128], column) * SCALE
        for e in range(2):
            leaf = 2 * c + e
            count = counts[leaf]
            mine = [targets[64 * e : 64 * e + 64, 128 * x : 128 * x + 128] for x in range(3)]
            for pair in range(NEAR // 2):
                first = cols[2 * pair, leaf] - base
                second = cols[2 * pair + 1, leaf] - base
                source = near_left[first] + near_right[second]
                squares = SOFT
                for x in range(3):
                    gap = mine[x] - source[x : x + 1, :]
                    squares = squares + gap * gap
                slot = jnp.where(lane < 64, 2 * pair, 2 * pair + 1)
                gain = jnp.where(slot < count, LOG_GAIN, -2000.0)
                value = jnp.exp2(gain - squares * lax.rsqrt(squares))
                tiles[64 * leaf : 64 * leaf + 64, 128 * pair : 128 * pair + 128] = value.astype(BF16)


def finish(place, signal, from_left, from_right, cols, tiles, down, basis, near_left, near_right, m):
    chunks = [from_left[16 * c : 16 * c + 16, :] for c in range(4)]
    chunks += signal
    chunks += [from_right[16 * c : 16 * c + 16, :] for c in range(4)]
    for c in range(16):
        turned = pltpu.roll(chunks[c].astype(F32), 64, 1).astype(BF16)
        near_left[2 * c] = chunks[c] * m.half[0]
        near_right[2 * c + 1] = chunks[c] * m.half[1]
        near_left[2 * c + 1] = turned * m.half[0]
        near_right[2 * c] = turned * m.half[1]
    base = place * LEAF_DEV - HALO
    result = []
    split = [halves(d) for d in down]
    for c in range(CHUNKS):
        rows = []
        for leaf in (2 * c, 2 * c + 1):
            parts = []
            for pair in range(NEAR // 2):
                first = cols[2 * pair, leaf] - base
                second = cols[2 * pair + 1, leaf] - base
                parts.append(near_left[first] + near_right[second])
            rows.append(jnp.concatenate(parts, axis=1))
        both = nt(jnp.concatenate(rows, axis=0), tiles[128 * c : 128 * c + 128, :])
        high, low = split[c // 2]
        g = (2 * c) % 4
        left = [high * m.group[g], high * m.group[g + 1], low * m.group[g], low * m.group[g + 1]]
        wide = jnp.concatenate([basis[:, 128 * c : 128 * c + 128]] * 4, axis=0)
        far = nn(jnp.concatenate(left, axis=0), wide)
        both = both + far[:32] + far[32:]
        result.append((both[:16] * m.halff[0] + both[16:] * m.halff[1]).astype(BF16))
    return result


def first_kernel(vectors, points, basis, xfer_low, left, right, gather, heights_out, xfer_out, wide):
    m = Masks()
    spread = spread_matrix()
    wide[960:1024, :] = jnp.zeros((64, 128), F32)
    spread_table(xfer_low[...], spread, wide, 0)
    xfer_out[...] = wide[...].astype(BF16)
    signal = [vectors[:, 128 * c : 128 * c + 128] for c in range(CHUNKS)]
    heights, root = up_pass(signal, basis, xfer_out, m)
    write_sends(signal, heights, root, left, right, gather, m)
    parts = point_parts(points[...])
    for c in range(4):
        left[192 + 16 * c : 208 + 16 * c, :] = parts[:, 128 * c : 128 * c + 128]
        right[192 + 16 * c : 208 + 16 * c, :] = parts[:, 512 + 128 * c : 640 + 128 * c]
    store_heights(heights, heights_out)


def store_heights(heights, out):
    at = 0
    for chunks in heights:
        for high, low in chunks:
            out[at : at + 16, :] = high
            out[at + 128 : at + 144, :] = low
            at += 16


def load_heights(source):
    heights, at = [], 0
    for count in (4, 2, 1, 1):
        heights.append(
            [(source[b : b + 16, :], source[b + 128 : b + 144, :]) for b in range(at, at + 16 * count, 16)]
        )
        at += 16 * count
    return heights


def second_kernel(
    cols, counts, vectors, points, basis, xfer, couple, xfer_top, couple_top, heights_in, from_left, from_right, gathered,
    left, right, gather, signal_out, heights_out, tiles, couple_out, top,
    wide, wide_xfer, wide_couple, places_left, places_right, near_left, near_right, *levels,
):
    m = Masks()
    place = lax.axis_index("leaf")
    spread = spread_matrix()
    wide[93 * 32 :, :] = jnp.zeros((96, 128), F32)
    for k in range(3):
        spread_table(couple[k], spread, wide, 31 * k)
    couple_out[...] = wide[...].astype(BF16)
    build_tiles(
        place, point_parts(points[...]), cols, counts, from_left, from_right, places_left, places_right, tiles
    )
    build_top(place, xfer_top, couple_out, couple_top, spread, wide_xfer, wide_couple, levels, top, m)
    heights = load_heights(heights_in)
    signal = [vectors[:, 128 * c : 128 * c + 128] for c in range(CHUNKS)]
    couplings = couple_low(heights, from_left, from_right, couple_out, m)
    down = down_pass(top_apply(gathered, top, m), couplings, xfer, m)
    signal = finish(place, signal, from_left, from_right, cols, tiles, down, basis, near_left, near_right, m)
    for c in range(CHUNKS):
        signal_out[:, 128 * c : 128 * c + 128] = signal[c]
    heights, root = up_pass(signal, basis, xfer, m)
    write_sends(signal, heights, root, left, right, gather, m)
    store_heights(heights, heights_out)


def third_kernel(
    cols, vectors, basis, xfer, couple, top, tiles, heights_in, from_left, from_right, gathered, out, near_left, near_right
):
    m = Masks()
    place = lax.axis_index("leaf")
    heights = load_heights(heights_in)
    signal = [vectors[:, 128 * c : 128 * c + 128] for c in range(CHUNKS)]
    couplings = couple_low(heights, from_left, from_right, couple, m)
    down = down_pass(top_apply(gathered, top, m), couplings, xfer, m)
    signal = finish(place, signal, from_left, from_right, cols, tiles, down, basis, near_left, near_right, m)
    for c in range(CHUNKS):
        out[:, 128 * c : 128 * c + 128] = signal[c]


def call(kernel, name, inputs, scalars, outputs, scratch):
    in_specs = [pl.BlockSpec(memory_space=pltpu.SMEM)] * scalars
    in_specs += [pl.BlockSpec(memory_space=pltpu.VMEM)] * (len(inputs) - scalars)
    return pl.pallas_call(
        kernel,
        out_shape=[jax.ShapeDtypeStruct(shape, BF16) for shape in outputs],
        in_specs=in_specs,
        out_specs=[pl.BlockSpec(memory_space=pltpu.VMEM)] * len(outputs),
        scratch_shapes=scratch,
        compiler_params=pltpu.CompilerParams(vmem_limit_bytes=VMEM_LIMIT),
        name=name,
    )(*inputs)


def exchange(left, right, gather):
    count = lax.axis_size("leaf")
    from_right = lax.ppermute(left, "leaf", [(i + 1, i) for i in range(count - 1)])
    from_left = lax.ppermute(right, "leaf", [(i, i + 1) for i in range(count - 1)])
    blocks = gather.reshape(count, 4, 128)
    gathered = lax.all_to_all(blocks, "leaf", 0, 0, tiled=True)
    return from_left, from_right, gathered.reshape(count * 4, 128)


def body(vectors, points, near_cols, near_count, basis, xfer_low, couple, xfer_top, couple_top):
    left, right, gather, heights, xfer = call(
        first_kernel, "up_first", (vectors, points, basis, xfer_low), 0,
        [(256, 128), (256, 128), (512, 128), (256, 128), (1024, 128)],
        [pltpu.VMEM((1024, 128), F32)],
    )
    from_left, from_right, gathered = exchange(left, right, gather)
    blocks = [pltpu.VMEM((32, 16, 128), BF16)] * 2
    left, right, gather, signal, heights, tiles, couple, top = call(
        second_kernel, "down_up",
        (near_cols, near_count, vectors, points, basis, xfer, couple, xfer_top, couple_top, heights, from_left, from_right,
         gathered), 2,
        [(192, 128), (192, 128), (512, 128), (16, 1024), (256, 128), (1024, 768), (3072, 128), (2048, 128)],
        [pltpu.VMEM((3072, 128), F32), pltpu.VMEM((8128, 128), F32), pltpu.VMEM((768, 128), F32)]
        + [pltpu.VMEM((32, 8, 128), F32)] * 2 + blocks
        + [pltpu.VMEM((4096 >> level, 128), F32) for level in range(6)],
    )
    from_left, from_right, gathered = exchange(left, right, gather)
    (result,) = call(
        third_kernel, "down_last",
        (near_cols, signal, basis, xfer, couple, top, tiles, heights, from_left, from_right, gathered), 1,
        [(16, 1024)], blocks,
    )
    return result


def solution(mesh):
    placed = (
        P("vec", "leaf"),
        P(None, "leaf"),
        P(None, "leaf"),
        P("leaf"),
        P(None, "leaf"),
        P("leaf", None),
        P(None, "leaf", None),
        P(),
        P(),
    )
    return jax.shard_map(body, mesh=mesh, in_specs=placed, out_specs=P("vec", "leaf"), check_vma=False)
```

time: 513 us -> 89.6 us (0.17)
  the two profiles are of different devices: /device:TPU:249 before, /device:TPU:1 now
where the time goes in v1:
time: 89.6 us; the launch traced here: 88.6 us
  starting transfers between devices  40.3 us (45%)
  Pallas kernels  20.5 us (23%)
  local copies, waits for them, and re-layouts  14 us (16%)
  waiting for transfers between devices  13.7 us (15%)
    all_to_all x2, starting transfers between devices, exchange(): gathered = lax.all_to_all(blocks, 'leaf', 0, 0, tiled=True)  29.2 us
    pallas_call x3, Pallas kernels, call(): pl.pallas_call(kernel, out_shape=[jax.ShapeDtypeStruct(shape, BF16) for s...  20.5 us
    unnamed x40, local copies, waits for them, and re-layouts  14 us
    ppermute x2, waiting for transfers between devices, exchange(): lax.ppermute(left, 'leaf', [(i + 1, i) for i in range(count - 1)])  7.74 us
    ppermute x2, starting transfers between devices, exchange(): lax.ppermute(right, 'leaf', [(i, i + 1) for i in range(count - 1)])  7.08 us
    all_to_all x2, waiting for transfers between devices, exchange(): gathered = lax.all_to_all(blocks, 'leaf', 0, 0, tiled=True)  5.96 us
    ppermute x2, starting transfers between devices, exchange(): lax.ppermute(left, 'leaf', [(i + 1, i) for i in range(count - 1)])  4.02 us
  transfers between devices with their start and end apart: 6, of which 4 were waited for; matrix products, arithmetic and copies ran while one was open for 0% of the time, Pallas kernels for 0%

profile of v1, /device:TPU:1, one launch (start us, length us, event | category | flops | bytes accessed | tf_op | source)
XLA Modules:
  0.0 88.6 jit_solution(3362386179748239107)
XLA Ops:
  0.0 0.8 copy-done.1
  0.8 0.8 copy-done.6
  1.6 0.7 copy-done.8
  2.3 0.8 copy-done.12
  3.2 1.7 %up_first.1 = (bf16[256,128]{1,0:T(8,128)(2,1)S(1)}, bf16[256,128]{1,0:T(8,128)(2,1)S(1)}, bf16[512,128]{1,0:T(8,128)(2,1)}, bf16[256,128]{1,0:T(8,128)(2,1)S(1)}, bf16[1024,128]{1,0:T(8,128)(2,1)S(1)}) custom-call(bf16[16,1024]{1,0:T(8,128)(2,1)S(1)} %copy-done.6, f32[3,1024]{1,0:T(4,128)S(1)} %copy-done.8, bf16[32,1024]{1,0:T(8,128)(2,1)S(1)} %copy-done.1, ...), custom_call_target="tpu_custom_call" | custom-call | tf_op jit(solution)/shard_map/up_first/pallas_call | solution.py:415
  4.9 18.4 %all-to-all-start = ((bf16[128,4,128]{2,1,0:T(4,128)(2,1)}), bf16[128,4,128]{2,1,0:T(4,128)(2,1)S(1)}, u32[]{:S(2)}, u32[]{:S(2)}) async-start(bf16[128,4,128]{2,1,0:T(4,128)(2,1)} %bitcast), calls=%async_computation | async-start | bytes 262144 | tf_op jit(solution)/shard_map/all_to_all | solution.py:431
  23.3 3.5 %collective-permute-start = (bf16[256,128]{1,0:T(8,128)(2,1)S(1)}, bf16[256,128]{1,0:T(8,128)(2,1)S(1)}, u32[]{:S(2)}, u32[]{:S(2)}) collective-permute-start(bf16[256,128]{1,0:T(8,128)(2,1)S(1)} %get-tuple-element.20), channel_id=1, source_target_pairs={{0,4},{4,8},{8,12},{12,16},{16,20},{20,24},{24,28},{28,32},{32,36}... | collective-permute-start | bytes 196616 | tf_op jit(solution)/shard_map/ppermute | solution.py:429
  26.9 2.1 %collective-permute-start.1 = (bf16[256,128]{1,0:T(8,128)(2,1)S(1)}, bf16[256,128]{1,0:T(8,128)(2,1)S(1)}, u32[]{:S(2)}, u32[]{:S(2)}) collective-permute-start(bf16[256,128]{1,0:T(8,128)(2,1)S(1)} %get-tuple-element.21), channel_id=1, source_target_pairs={{4,0},{8,4},{12,8},{16,12},{20,16},{24,20},{28,24},{32,28},{36,32}... | collective-permute-start | bytes 196616 | tf_op jit(solution)/shard_map/ppermute | solution.py:428
  29.0 0.0 collective-permute-done.from_left
  29.0 3.8 %collective-permute-done.1.from_right = bf16[256,128]{1,0:T(8,128)(2,1)S(1)} collective-permute-done((bf16[256,128]{1,0:T(8,128)(2,1)S(1)}, bf16[256,128]{1,0:T(8,128)(2,1)S(1)}, u32[]{:S(2)}, u32[]{:S(2)}) %collective-permute-start.1) | collective-permute-done | bytes 65568 | tf_op jit(solution)/shard_map/ppermute | solution.py:428
  32.8 0.6 copy-done.10
  33.4 2.7 %all-to-all-done = bf16[128,4,128]{2,1,0:T(4,128)(2,1)S(1)} async-done(((bf16[128,4,128]{2,1,0:T(4,128)(2,1)}), bf16[128,4,128]{2,1,0:T(4,128)(2,1)S(1)}, u32[]{:S(2)}, u32[]{:S(2)}) %all-to-all-start) | async-done | bytes 131104 | tf_op jit(solution)/shard_map/all_to_all | solution.py:431
  36.1 1.1 %copy-done = bf16[3,124,1024]{2,1,0:T(8,128)(2,1)S(1)} copy-done((bf16[3,124,1024]{2,1,0:T(8,128)(2,1)S(1)}, bf16[3,124,1024]{2,1,0:T(8,128)(2,1)}, u32[]{:S(2)}) %copy-start) | copy-done | bytes 761880
  37.2 0.8 copy-done.2
  38.0 1.0 %copy-done.4 = bf16[254,1024]{1,0:T(8,128)(2,1)S(1)} copy-done((bf16[254,1024]{1,0:T(8,128)(2,1)S(1)}, bf16[254,1024]{1,0:T(8,128)(2,1)}, u32[]{:S(2)}) %copy-start.4) | copy-done | bytes 520216
  39.1 0.9 %copy-done.5 = bf16[3,31,1024]{2,1,0:T(8,128)(2,1)S(1)} copy-done((bf16[3,31,1024]{2,1,0:T(8,128)(2,1)S(1)}, bf16[3,31,1024]{2,1,0:T(8,128)(2,1)}, u32[]{:S(2)}) %copy-start.5) | copy-done | bytes 190488
  40.0 0.8 copy-done.7
  40.8 0.7 copy-done.9
  41.5 0.8 copy-done.11
  42.3 0.7 copy-done.15
  43.0 0.7 copy-done.17
  43.7 15.1 %down_up.1 = (bf16[192,128]{1,0:T(8,128)(2,1)S(1)}, bf16[192,128]{1,0:T(8,128)(2,1)S(1)}, bf16[512,128]{1,0:T(8,128)(2,1)}, bf16[16,1024]{1,0:T(8,128)(2,1)S(1)}...) custom-call(s32[12,16]{1,0:T(8,128)S(1)} %copy-done.15, ...), custom_call_target="tpu_custom_call" | custom-call | tf_op jit(solution)/shard_map/down_up/pallas_call | solution.py:415
  58.8 0.6 copy-done.13
  59.4 0.6 copy-done.18
  60.0 0.6 copy-done.19
  60.6 10.8 %all-to-all-start.1 = ((bf16[128,4,128]{2,1,0:T(4,128)(2,1)}), bf16[128,4,128]{2,1,0:T(4,128)(2,1)S(1)}, u32[]{:S(2)}, u32[]{:S(2)}) async-start(bf16[128,4,128]{2,1,0:T(4,128)(2,1)} %bitcast.2), calls=%async_computation.1 | async-start | bytes 262144 | tf_op jit(solution)/shard_map/all_to_all | solution.py:431
  71.5 3.5 %collective-permute-start.2 = (bf16[192,128]{1,0:T(8,128)(2,1)}, bf16[192,128]{1,0:T(8,128)(2,1)S(1)}, u32[]{:S(2)}, u32[]{:S(2)}) collective-permute-start(bf16[192,128]{1,0:T(8,128)(2,1)} %copy-done.19), channel_id=1, source_target_pairs={{0,4},{4,8},{8,12},{12,16},{16,20},{20,24},{24,28},{28,32},{32,36}... | collective-permute-start | bytes 147464 | tf_op jit(solution)/shard_map/ppermute | solution.py:429
  75.0 1.9 %collective-permute-start.3 = (bf16[192,128]{1,0:T(8,128)(2,1)}, bf16[192,128]{1,0:T(8,128)(2,1)S(1)}, u32[]{:S(2)}, u32[]{:S(2)}) collective-permute-start(bf16[192,128]{1,0:T(8,128)(2,1)} %copy-done.18), channel_id=1, source_target_pairs={{4,0},{8,4},{12,8},{16,12},{20,16},{24,20},{28,24},{32,28},{36,32}... | collective-permute-start | bytes 147464 | tf_op jit(solution)/shard_map/ppermute | solution.py:428
  76.9 4.0 %collective-permute-done.3.from_right = bf16[192,128]{1,0:T(8,128)(2,1)S(1)} collective-permute-done((bf16[192,128]{1,0:T(8,128)(2,1)}, bf16[192,128]{1,0:T(8,128)(2,1)S(1)}, u32[]{:S(2)}, u32[]{:S(2)}) %collective-permute-start.3) | collective-permute-done | bytes 49184 | tf_op jit(solution)/shard_map/ppermute | solution.py:428
  80.9 3.3 %all-to-all-done.1 = bf16[128,4,128]{2,1,0:T(4,128)(2,1)S(1)} async-done(((bf16[128,4,128]{2,1,0:T(4,128)(2,1)}), bf16[128,4,128]{2,1,0:T(4,128)(2,1)S(1)}, u32[]{:S(2)}, u32[]{:S(2)}) %all-to-all-start.1) | async-done | bytes 131104 | tf_op jit(solution)/shard_map/all_to_all | solution.py:431
  84.2 0.8 copy-done.14
  85.0 3.7 %down_last.1 = bf16[16,1024]{1,0:T(8,128)(2,1)} custom-call(s32[12,16]{1,0:T(8,128)S(1)} %copy-done.16, bf16[16,1024]{1,0:T(8,128)(2,1)S(1)} %copy-done.14, bf16[32,1024]{1,0:T(8,128)(2,1)S(1)} %copy-done.3, bf16[1024,128]{1,0:T(8,128)(2,1)S(1)} %get-tuple-element.18.xfer, bf16[3072,128]{1,0:T(8,128)(2,1)S(1)} %get-tuple-element.24.couple, ...), custom_call_target="tpu_custom_call" | custom-call | tf_op jit(solution)/shard_map/down_last/pallas_call | solution.py:415
  (23 shorter events, 0.0 us)
Async XLA Ops:
  0.0 0.8 copy-start.1
  0.8 0.8 copy-start.6
  1.6 0.7 copy-start.8
  2.3 0.8 copy-start.12
  3.2 81.0 %copy-start.3 = (bf16[32,1024]{1,0:T(8,128)(2,1)S(1)}, bf16[32,1024]{1,0:T(8,128)(2,1)}, u32[]{:S(2)}) copy-start(bf16[32,1024]{1,0:T(8,128)(2,1)} %basis.5) | copy-start | bytes 196612
  3.2 81.0 %copy-start.16 = (s32[12,16]{1,0:T(8,128)S(1)}, s32[12,16]{1,0:T(8,128)}, u32[]{:S(2)}) copy-start(s32[12,16]{1,0:T(8,128)} %cols.3) | copy-start | bytes 2308
  4.9 31.2 %all-to-all-start = ((bf16[128,4,128]{2,1,0:T(4,128)(2,1)}), bf16[128,4,128]{2,1,0:T(4,128)(2,1)S(1)}, u32[]{:S(2)}, u32[]{:S(2)}) async-start(bf16[128,4,128]{2,1,0:T(4,128)(2,1)} %bitcast), calls=%async_computation | async-start | bytes 262144 | tf_op jit(solution)/shard_map/all_to_all | solution.py:431
  23.3 5.7 %collective-permute-start = (bf16[256,128]{1,0:T(8,128)(2,1)S(1)}, bf16[256,128]{1,0:T(8,128)(2,1)S(1)}, u32[]{:S(2)}, u32[]{:S(2)}) collective-permute-start(bf16[256,128]{1,0:T(8,128)(2,1)S(1)} %get-tuple-element.20), channel_id=1, source_target_pairs={{0,4},{4,8},{8,12},{12,16},{16,20},{20,24},{24,28},{28,32},{32,36}... | collective-permute-start | bytes 196616 | tf_op jit(solution)/shard_map/ppermute | solution.py:429
  26.9 5.9 %collective-permute-start.1 = (bf16[256,128]{1,0:T(8,128)(2,1)S(1)}, bf16[256,128]{1,0:T(8,128)(2,1)S(1)}, u32[]{:S(2)}, u32[]{:S(2)}) collective-permute-start(bf16[256,128]{1,0:T(8,128)(2,1)S(1)} %get-tuple-element.21), channel_id=1, source_target_pairs={{4,0},{8,4},{12,8},{16,12},{20,16},{24,20},{28,24},{32,28},{36,32}... | collective-permute-start | bytes 196616 | tf_op jit(solution)/shard_map/ppermute | solution.py:428
  32.7 0.6 copy-start.10
  36.1 1.1 %copy-start = (bf16[3,124,1024]{2,1,0:T(8,128)(2,1)S(1)}, bf16[3,124,1024]{2,1,0:T(8,128)(2,1)}, u32[]{:S(2)}) copy-start(bf16[3,124,1024]{2,1,0:T(8,128)(2,1)} %couple_top.1) | copy-start | bytes 2285572
  37.2 0.8 copy-start.2
  38.0 1.0 %copy-start.4 = (bf16[254,1024]{1,0:T(8,128)(2,1)S(1)}, bf16[254,1024]{1,0:T(8,128)(2,1)}, u32[]{:S(2)}) copy-start(bf16[254,1024]{1,0:T(8,128)(2,1)} %xfer_top.1) | copy-start | bytes 1560580
  39.1 0.9 %copy-start.5 = (bf16[3,31,1024]{2,1,0:T(8,128)(2,1)S(1)}, bf16[3,31,1024]{2,1,0:T(8,128)(2,1)}, u32[]{:S(2)}) copy-start(bf16[3,31,1024]{2,1,0:T(8,128)(2,1)} %couple.1) | copy-start | bytes 571396
  40.0 0.8 copy-start.7
  40.8 0.7 copy-start.9
  41.5 0.8 copy-start.11
  42.3 0.7 copy-start.15
  43.0 0.7 copy-start.17
  58.8 0.6 copy-start.13
  59.4 0.6 copy-start.18
  60.0 0.6 copy-start.19
  60.6 23.6 %all-to-all-start.1 = ((bf16[128,4,128]{2,1,0:T(4,128)(2,1)}), bf16[128,4,128]{2,1,0:T(4,128)(2,1)S(1)}, u32[]{:S(2)}, u32[]{:S(2)}) async-start(bf16[128,4,128]{2,1,0:T(4,128)(2,1)} %bitcast.2), calls=%async_computation.1 | async-start | bytes 262144 | tf_op jit(solution)/shard_map/all_to_all | solution.py:431
  71.5 5.5 %collective-permute-start.2 = (bf16[192,128]{1,0:T(8,128)(2,1)}, bf16[192,128]{1,0:T(8,128)(2,1)S(1)}, u32[]{:S(2)}, u32[]{:S(2)}) collective-permute-start(bf16[192,128]{1,0:T(8,128)(2,1)} %copy-done.19), channel_id=1, source_target_pairs={{0,4},{4,8},{8,12},{12,16},{16,20},{20,24},{24,28},{28,32},{32,36}... | collective-permute-start | bytes 147464 | tf_op jit(solution)/shard_map/ppermute | solution.py:429
  75.0 5.9 %collective-permute-start.3 = (bf16[192,128]{1,0:T(8,128)(2,1)}, bf16[192,128]{1,0:T(8,128)(2,1)S(1)}, u32[]{:S(2)}, u32[]{:S(2)}) collective-permute-start(bf16[192,128]{1,0:T(8,128)(2,1)} %copy-done.18), channel_id=1, source_target_pairs={{4,0},{8,4},{12,8},{16,12},{20,16},{24,20},{28,24},{32,28},{36,32}... | collective-permute-start | bytes 147464 | tf_op jit(solution)/shard_map/ppermute | solution.py:428
  84.2 0.8 copy-start.14

commit v2 on v1

--- a/solution.py
+++ b/solution.py
@@ -24,6 +24,7 @@
 SOFT = 0.01 * SCALE * SCALE
 LOG_GAIN = math.log2(4.0 / math.sqrt(64 * NEAR))
 VMEM_LIMIT = 48 * 1024 * 1024
+VMEM_MOST = 60 * 1024 * 1024
 
 
 def nn(a, b):
@@ -191,8 +192,10 @@
     return down
 
 
-def build_top(place, xfer_top, own_couple, couple_top, spread, wide_xfer, wide_couple, levels, top, m):
+def build_top(place, xfer_top, couple, couple_top, spread, wide_xfer, wide_own, wide_couple, levels, top, m):
     spread_table(xfer_top[...], spread, wide_xfer, 0)
+    for k in range(3):
+        spread_table(couple[k, 30:31, :], spread, wide_own, k)
     row = lax.broadcasted_iota(jnp.int32, (8, 124), 0)
     col = lax.broadcasted_iota(jnp.int32, (8, 124), 1)
     wanted = jnp.zeros((8, 124), jnp.int32) - 1
@@ -208,7 +211,7 @@
     slots = []
     for level in range(6):
         if level == 0:
-            tables = [own_couple[(31 * k + 30) * 32 : (31 * k + 31) * 32, :].astype(F32) for k in range(3)]
+            tables = [wide_own[32 * k : 32 * k + 32, :] for k in range(3)]
         else:
             tables = [wide_couple[(8 * k + level - 1) * 32 : (8 * k + level) * 32, :] for k in range(3)]
         at = pl.multiple_of((TOP_XFER[level] + (place >> level)) * 32, 32)
@@ -299,7 +302,7 @@
                 tiles[64 * leaf : 64 * leaf + 64, 128 * pair : 128 * pair + 128] = value.astype(BF16)
 
 
-def finish(place, signal, from_left, from_right, cols, tiles, down, basis, near_left, near_right, m):
+def near_field(place, signal, from_left, from_right, cols, tiles, near_left, near_right, m):
     chunks = [from_left[16 * c : 16 * c + 16, :] for c in range(4)]
     chunks += signal
     chunks += [from_right[16 * c : 16 * c + 16, :] for c in range(4)]
@@ -311,7 +314,6 @@
         near_right[2 * c] = turned * m.half[1]
     base = place * LEAF_DEV - HALO
     result = []
-    split = [halves(d) for d in down]
     for c in range(CHUNKS):
         rows = []
         for leaf in (2 * c, 2 * c + 1):
@@ -322,30 +324,23 @@
                 parts.append(near_left[first] + near_right[second])
             rows.append(jnp.concatenate(parts, axis=1))
         both = nt(jnp.concatenate(rows, axis=0), tiles[128 * c : 128 * c + 128, :])
+        result.append(both[:16] * m.halff[0] + both[16:] * m.halff[1])
+    return result
+
+
+def far_field(down, basis, near, m):
+    result = []
+    split = [halves(d) for d in down]
+    for c in range(CHUNKS):
         high, low = split[c // 2]
         g = (2 * c) % 4
         left = [high * m.group[g], high * m.group[g + 1], low * m.group[g], low * m.group[g + 1]]
         wide = jnp.concatenate([basis[:, 128 * c : 128 * c + 128]] * 4, axis=0)
         far = nn(jnp.concatenate(left, axis=0), wide)
-        both = both + far[:32] + far[32:]
-        result.append((both[:16] * m.halff[0] + both[16:] * m.halff[1]).astype(BF16))
+        far = far[:32] + far[32:]
+        far = far[:16] * m.halff[0] + far[16:] * m.halff[1]
+        result.append((near[:, 128 * c : 128 * c + 128] + far).astype(BF16))
     return result
-
-
-def first_kernel(vectors, points, basis, xfer_low, left, right, gather, heights_out, xfer_out, wide):
-    m = Masks()
-    spread = spread_matrix()
-    wide[960:1024, :] = jnp.zeros((64, 128), F32)
-    spread_table(xfer_low[...], spread, wide, 0)
-    xfer_out[...] = wide[...].astype(BF16)
-    signal = [vectors[:, 128 * c : 128 * c + 128] for c in range(CHUNKS)]
-    heights, root = up_pass(signal, basis, xfer_out, m)
-    write_sends(signal, heights, root, left, right, gather, m)
-    parts = point_parts(points[...])
-    for c in range(4):
-        left[192 + 16 * c : 208 + 16 * c, :] = parts[:, 128 * c : 128 * c + 128]
-        right[192 + 16 * c : 208 + 16 * c, :] = parts[:, 512 + 128 * c : 640 + 128 * c]
-    store_heights(heights, heights_out)
 
 
 def store_heights(heights, out):
@@ -367,27 +362,124 @@
     return heights
 
 
-def second_kernel(
-    cols, counts, vectors, points, basis, xfer, couple, xfer_top, couple_top, heights_in, from_left, from_right, gathered,
-    left, right, gather, signal_out, heights_out, tiles, couple_out, top,
-    wide, wide_xfer, wide_couple, places_left, places_right, near_left, near_right, *levels,
+def store_local(near, couplings, near_out, couplings_out):
+    for c in range(CHUNKS):
+        near_out[:, 128 * c : 128 * c + 128] = near[c]
+    at = 0
+    for chunks in couplings:
+        for chunk in chunks:
+            couplings_out[at : at + 16, :] = chunk
+            at += 16
+
+
+def load_couplings(source):
+    couplings, at = [], 0
+    for count in (4, 2, 1, 1):
+        couplings.append([source[b : b + 16, :] for b in range(at, at + 16 * count, 16)])
+        at += 16 * count
+    return couplings
+
+
+def chunks_of(signal):
+    return [signal[:, 128 * c : 128 * c + 128] for c in range(CHUNKS)]
+
+
+def fetch(sources, targets, sems):
+    copies = [pltpu.make_async_copy(s, t, sems.at[i]) for i, (s, t) in enumerate(zip(sources, targets, strict=True))]
+    for copy in copies:
+        copy.start()
+    return copies
+
+
+def first_kernel(
+    vectors_hbm, points_hbm, basis_hbm, xfer_hbm, left, right, gather, heights_out, xfer_out,
+    vectors, points, basis, xfer_low, wide, sems,
 ):
+    copies = fetch((xfer_hbm, vectors_hbm, basis_hbm, points_hbm), (xfer_low, vectors, basis, points), sems)
+    m = Masks()
+    spread = spread_matrix()
+    wide[960:1024, :] = jnp.zeros((64, 128), F32)
+    copies[0].wait()
+    spread_table(xfer_low[...], spread, wide, 0)
+    xfer_out[...] = wide[...].astype(BF16)
+    copies[1].wait()
+    copies[2].wait()
+    signal = chunks_of(vectors)
+    heights, root = up_pass(signal, basis, xfer_out, m)
+    write_sends(signal, heights, root, left, right, gather, m)
+    store_heights(heights, heights_out)
+    copies[3].wait()
+    parts = point_parts(points[...])
+    for c in range(4):
+        left[192 + 16 * c : 208 + 16 * c, :] = parts[:, 128 * c : 128 * c + 128]
+        right[192 + 16 * c : 208 + 16 * c, :] = parts[:, 512 + 128 * c : 640 + 128 * c]
+
+
+def table_kernel(
+    xfer_hbm, couple_top_hbm, couple_hbm, after, top,
+    xfer_top, couple_top, couple, wide, wide_xfer, wide_couple, sems, *levels,
+):
+    del after
+    copies = fetch((xfer_hbm, couple_top_hbm, couple_hbm), (xfer_top, couple_top, couple), sems)
     m = Masks()
     place = lax.axis_index("leaf")
+    for copy in copies:
+        copy.wait()
+    build_top(place, xfer_top, couple, couple_top, spread_matrix(), wide_xfer, wide, wide_couple, levels, top, m)
+
+
+def local_first_kernel(
+    cols_hbm, counts_hbm, vectors_hbm, points_hbm, couple_hbm, from_left, from_right, heights_in,
+    tiles, near_out, couplings_out,
+    cols, counts, vectors, points, couple, wide, couple_wide, places_left, places_right, near_left, near_right, sems,
+):
+    copies = fetch(
+        (cols_hbm, counts_hbm, vectors_hbm, points_hbm, couple_hbm), (cols, counts, vectors, points, couple), sems
+    )
+    m = Masks()
+    place = lax.axis_index("leaf")
+    for copy in copies:
+        copy.wait()
+    build_tiles(
+        place, point_parts(points[...]), cols, counts, from_left, from_right, places_left, places_right, tiles
+    )
+    spread_couple(couple, wide, couple_wide)
+    couplings = couple_low(load_heights(heights_in), from_left, from_right, couple_wide, m)
+    near = near_field(place, chunks_of(vectors), from_left, from_right, cols, tiles, near_left, near_right, m)
+    store_local(near, couplings, near_out, couplings_out)
+
+
+def spread_couple(couple, wide, out):
     spread = spread_matrix()
     wide[93 * 32 :, :] = jnp.zeros((96, 128), F32)
     for k in range(3):
         spread_table(couple[k], spread, wide, 31 * k)
-    couple_out[...] = wide[...].astype(BF16)
-    build_tiles(
-        place, point_parts(points[...]), cols, counts, from_left, from_right, places_left, places_right, tiles
-    )
-    build_top(place, xfer_top, couple_out, couple_top, spread, wide_xfer, wide_couple, levels, top, m)
-    heights = load_heights(heights_in)
-    signal = [vectors[:, 128 * c : 128 * c + 128] for c in range(CHUNKS)]
-    couplings = couple_low(heights, from_left, from_right, couple_out, m)
-    down = down_pass(top_apply(gathered, top, m), couplings, xfer, m)
-    signal = finish(place, signal, from_left, from_right, cols, tiles, down, basis, near_left, near_right, m)
+    out[...] = wide[...].astype(BF16)
+
+
+def local_next_kernel(
+    cols_hbm, couple_hbm, vectors, tiles, from_left, from_right, heights_in, near_out, couplings_out,
+    cols, couple, wide, couple_wide, near_left, near_right, sems,
+):
+    copies = fetch((couple_hbm, cols_hbm), (couple, cols), sems)
+    m = Masks()
+    place = lax.axis_index("leaf")
+    copies[0].wait()
+    spread_couple(couple, wide, couple_wide)
+    couplings = couple_low(load_heights(heights_in), from_left, from_right, couple_wide, m)
+    copies[1].wait()
+    near = near_field(place, chunks_of(vectors), from_left, from_right, cols, tiles, near_left, near_right, m)
+    store_local(near, couplings, near_out, couplings_out)
+
+
+def down_up_kernel(
+    basis_hbm, gathered, top, xfer, near, couplings, left, right, gather, signal_out, heights_out, basis, sems
+):
+    copies = fetch((basis_hbm,), (basis,), sems)
+    m = Masks()
+    down = down_pass(top_apply(gathered, top, m), load_couplings(couplings), xfer, m)
+    copies[0].wait()
+    signal = far_field(down, basis, near, m)
     for c in range(CHUNKS):
         signal_out[:, 128 * c : 128 * c + 128] = signal[c]
     heights, root = up_pass(signal, basis, xfer, m)
@@ -395,65 +487,79 @@
     store_heights(heights, heights_out)
 
 
-def third_kernel(
-    cols, vectors, basis, xfer, couple, top, tiles, heights_in, from_left, from_right, gathered, out, near_left, near_right
-):
+def down_last_kernel(basis_hbm, gathered, top, xfer, near, couplings, out, basis, sems):
+    copies = fetch((basis_hbm,), (basis,), sems)
     m = Masks()
-    place = lax.axis_index("leaf")
-    heights = load_heights(heights_in)
-    signal = [vectors[:, 128 * c : 128 * c + 128] for c in range(CHUNKS)]
-    couplings = couple_low(heights, from_left, from_right, couple, m)
-    down = down_pass(top_apply(gathered, top, m), couplings, xfer, m)
-    signal = finish(place, signal, from_left, from_right, cols, tiles, down, basis, near_left, near_right, m)
+    down = down_pass(top_apply(gathered, top, m), load_couplings(couplings), xfer, m)
+    copies[0].wait()
+    signal = far_field(down, basis, near, m)
     for c in range(CHUNKS):
         out[:, 128 * c : 128 * c + 128] = signal[c]
 
 
-def call(kernel, name, inputs, scalars, outputs, scratch):
-    in_specs = [pl.BlockSpec(memory_space=pltpu.SMEM)] * scalars
-    in_specs += [pl.BlockSpec(memory_space=pltpu.VMEM)] * (len(inputs) - scalars)
+def call(kernel, name, arguments, arrays, outputs, scratch, flops, limit=VMEM_LIMIT):
+    inputs = tuple(arguments) + tuple(arrays)
+    in_specs = [pl.BlockSpec(memory_space=pltpu.HBM)] * len(arguments)
+    in_specs += [pl.BlockSpec(memory_space=pltpu.VMEM)] * len(arrays)
     return pl.pallas_call(
         kernel,
-        out_shape=[jax.ShapeDtypeStruct(shape, BF16) for shape in outputs],
+        out_shape=[jax.ShapeDtypeStruct(shape, dtype) for shape, dtype in outputs],
         in_specs=in_specs,
         out_specs=[pl.BlockSpec(memory_space=pltpu.VMEM)] * len(outputs),
         scratch_shapes=scratch,
-        compiler_params=pltpu.CompilerParams(vmem_limit_bytes=VMEM_LIMIT),
+        compiler_params=pltpu.CompilerParams(vmem_limit_bytes=limit),
+        cost_estimate=pl.CostEstimate(flops=flops, bytes_accessed=1 << 20, transcendentals=0),
         name=name,
     )(*inputs)
 
 
 def exchange(left, right, gather):
     count = lax.axis_size("leaf")
+    blocks = gather.reshape(count, 4, 128)
+    gathered = lax.all_to_all(blocks, "leaf", 0, 0, tiled=True)
     from_right = lax.ppermute(left, "leaf", [(i + 1, i) for i in range(count - 1)])
     from_left = lax.ppermute(right, "leaf", [(i, i + 1) for i in range(count - 1)])
-    blocks = gather.reshape(count, 4, 128)
-    gathered = lax.all_to_all(blocks, "leaf", 0, 0, tiled=True)
     return from_left, from_right, gathered.reshape(count * 4, 128)
 
 
 def body(vectors, points, near_cols, near_count, basis, xfer_low, couple, xfer_top, couple_top):
+    vm, sm = pltpu.VMEM, pltpu.SMEM
+    sems = pltpu.SemaphoreType.DMA
+    signal_buf, basis_buf, points_buf = vm((16, 1024), BF16), vm((32, 1024), BF16), vm((3, 1024), F32)
+    couple_buf = [vm((3, 31, 1024), BF16), vm((3072, 128), F32)]
+    blocks = [vm((32, 16, 128), BF16)] * 2
+    sends = [((512, 128), BF16), ((256, 128), BF16)]
+    local = [((16, 1024), F32), ((128, 128), F32)]
     left, right, gather, heights, xfer = call(
-        first_kernel, "up_first", (vectors, points, basis, xfer_low), 0,
-        [(256, 128), (256, 128), (512, 128), (256, 128), (1024, 128)],
-        [pltpu.VMEM((1024, 128), F32)],
+        first_kernel, "up_first", (vectors, points, basis, xfer_low), (),
+        [((256, 128), BF16)] * 2 + sends + [((1024, 128), BF16)],
+        [signal_buf, points_buf, basis_buf, vm((30, 1024), BF16), vm((1024, 128), F32), sems((4,))], 1 << 20, VMEM_MOST,
     )
     from_left, from_right, gathered = exchange(left, right, gather)
-    blocks = [pltpu.VMEM((32, 16, 128), BF16)] * 2
-    left, right, gather, signal, heights, tiles, couple, top = call(
-        second_kernel, "down_up",
-        (near_cols, near_count, vectors, points, basis, xfer, couple, xfer_top, couple_top, heights, from_left, from_right,
-         gathered), 2,
-        [(192, 128), (192, 128), (512, 128), (16, 1024), (256, 128), (1024, 768), (3072, 128), (2048, 128)],
-        [pltpu.VMEM((3072, 128), F32), pltpu.VMEM((8128, 128), F32), pltpu.VMEM((768, 128), F32)]
-        + [pltpu.VMEM((32, 8, 128), F32)] * 2 + blocks
-        + [pltpu.VMEM((4096 >> level, 128), F32) for level in range(6)],
+    (top,) = call(
+        table_kernel, "tables", (xfer_top, couple_top, couple, heights), (), [((2048, 128), BF16)],
+        [vm((254, 1024), BF16), vm((3, 124, 1024), BF16), vm((3, 31, 1024), BF16), vm((96, 128), F32),
+         vm((8128, 128), F32), vm((768, 128), F32), sems((3,))] + [vm((4096 >> level, 128), F32) for level in range(6)],
+        1 << 32, VMEM_MOST,
+    )
+    tiles, near, couplings = call(
+        local_first_kernel, "local_first", (near_cols, near_count, vectors, points, couple),
+        (from_left, from_right, heights), [((1024, 768), BF16)] + local,
+        [sm((12, 16), jnp.int32), sm((16,), jnp.int32), signal_buf, points_buf] + couple_buf + [vm((3072, 128), BF16)]
+        + [vm((32, 8, 128), F32)] * 2 + blocks + [sems((5,))], 1 << 32,
+    )
+    left, right, gather, signal, heights = call(
+        down_up_kernel, "down_up", (basis,), (gathered, top, xfer, near, couplings),
+        [((192, 128), BF16)] * 2 + [sends[0], ((16, 1024), BF16), sends[1]], [basis_buf, sems((1,))], 1 << 20,
     )
     from_left, from_right, gathered = exchange(left, right, gather)
+    near, couplings = call(
+        local_next_kernel, "local_next", (near_cols, couple), (signal, tiles, from_left, from_right, heights), local,
+        [sm((12, 16), jnp.int32)] + couple_buf + [vm((3072, 128), BF16)] + blocks + [sems((2,))], 1 << 32,
+    )
     (result,) = call(
-        third_kernel, "down_last",
-        (near_cols, signal, basis, xfer, couple, top, tiles, heights, from_left, from_right, gathered), 1,
-        [(16, 1024)], blocks,
+        down_last_kernel, "down_last", (basis,), (gathered, top, xfer, near, couplings), [((16, 1024), BF16)],
+        [basis_buf, sems((1,))], 1 << 20,
     )
     return result
 

time: 89.6 us -> 81.6 us (0.911)
  local copies, waits for them, and re-layouts: 14 us -> 0.05 us
  starting transfers between devices: 40.3 us -> 45.9 us
  Pallas kernels: 20.5 us -> 24.7 us
  waiting for transfers between devices: 13.7 us -> 10.1 us
    unnamed x40 -> x18, local copies, waits for them, and re-layouts: 14 us -> 0.05 us
    ppermute x2, waiting for transfers between devices: 7.74 us -> 0.01 us  [exchange(): lax.ppermute(left, 'leaf', [(i + 1, i) for i in range(count - 1)])]
    all_to_all x2, starting transfers between devices: 29.2 us -> 34.7 us  [exchange(): gathered = lax.all_to_all(blocks, 'leaf', 0, 0, tiled=True)]
    pallas_call x3 -> x6, Pallas kernels: 20.5 us -> 24.7 us  [call(): pl.pallas_call(kernel, out_shape=[jax.ShapeDtypeStruct(shape, dtype) for...]
    all_to_all x2, waiting for transfers between devices: 5.96 us -> 10.1 us  [exchange(): gathered = lax.all_to_all(blocks, 'leaf', 0, 0, tiled=True)]
  transfers between devices with their start and end apart: 6 -> 6, of which waited for: 4 -> 1; matrix products, arithmetic and copies ran while one was open for 0% -> 0% of each run, Pallas kernels for 0% -> 20%
where the time goes in v2:
time: 81.6 us; the launch traced here: 81.2 us
  starting transfers between devices  45.9 us (56%)
  Pallas kernels  24.7 us (30%)
  waiting for transfers between devices  10.1 us (12%)
    all_to_all x2, starting transfers between devices, exchange(): gathered = lax.all_to_all(blocks, 'leaf', 0, 0, tiled=True)  34.7 us
    pallas_call x6, Pallas kernels, call(): pl.pallas_call(kernel, out_shape=[jax.ShapeDtypeStruct(shape, dtype) for...  24.7 us
    all_to_all x2, waiting for transfers between devices, exchange(): gathered = lax.all_to_all(blocks, 'leaf', 0, 0, tiled=True)  10.1 us
    ppermute x2, starting transfers between devices, exchange(): lax.ppermute(right, 'leaf', [(i, i + 1) for i in range(count - 1)])  7.18 us
    ppermute x2, starting transfers between devices, exchange(): lax.ppermute(left, 'leaf', [(i + 1, i) for i in range(count - 1)])  4.02 us
  transfers between devices with their start and end apart: 6, of which 1 were waited for; matrix products, arithmetic and copies ran while one was open for 0% of the time, Pallas kernels for 20%

profile of v2, /device:TPU:1, one launch (start us, length us, event | category | flops | bytes accessed | tf_op | source)
XLA Modules:
  0.0 81.2 jit_solution(8893950115434121118)
XLA Ops:
  0.0 2.9 %up_first.1 = (bf16[256,128]{1,0:T(8,128)(2,1)}, bf16[256,128]{1,0:T(8,128)(2,1)}, bf16[512,128]{1,0:T(8,128)(2,1)}, bf16[256,128]{1,0:T(8,128)(2,1)}, bf16[1024,128]{1,0:T(8,128)(2,1)}) custom-call(bf16[16,1024]{1,0:T(8,128)(2,1)} %vectors_hbm.3, f32[3,1024]{1,0:T(4,128)} %points_hbm.3, bf16[32,1024]{1,0:T(8,128)(2,1)} %basis_hbm.5, bf16[30,1024]{1,0:T(8,128)(2,1)} %xfer_hbm.2), custom_call_target="tpu_custom_call" | custom-call | flops 1048576 | bytes 1048576 | tf_op jit(solution)/shard_map/up_first/pallas_call | solution.py:504
  2.9 18.4 %all-to-all-start = ((bf16[128,4,128]{2,1,0:T(4,128)(2,1)}), bf16[128,4,128]{2,1,0:T(4,128)(2,1)S(1)}, u32[]{:S(2)}, u32[]{:S(2)}) async-start(bf16[128,4,128]{2,1,0:T(4,128)(2,1)} %bitcast.6), calls=%async_computation | async-start | bytes 262144 | tf_op jit(solution)/shard_map/all_to_all | solution.py:519
  21.4 3.5 %collective-permute-start = (bf16[256,128]{1,0:T(8,128)(2,1)}, bf16[256,128]{1,0:T(8,128)(2,1)S(1)}, u32[]{:S(2)}, u32[]{:S(2)}) collective-permute-start(bf16[256,128]{1,0:T(8,128)(2,1)} %get-tuple-element.23), channel_id=1, source_target_pairs={{0,4},{4,8},{8,12},{12,16},{16,20},{20,24},{24,28},{28,32},{32,36}... | collective-permute-start | bytes 196616 | tf_op jit(solution)/shard_map/ppermute | solution.py:521
  24.9 2.1 %collective-permute-start.1 = (bf16[256,128]{1,0:T(8,128)(2,1)}, bf16[256,128]{1,0:T(8,128)(2,1)S(1)}, u32[]{:S(2)}, u32[]{:S(2)}) collective-permute-start(bf16[256,128]{1,0:T(8,128)(2,1)} %get-tuple-element.24), channel_id=1, source_target_pairs={{4,0},{8,4},{12,8},{16,12},{20,16},{24,20},{28,24},{32,28},{36,32}... | collective-permute-start | bytes 196616 | tf_op jit(solution)/shard_map/ppermute | solution.py:520
  27.0 0.0 copy-start.3
  27.0 0.0 copy-start.4
  27.0 0.0 copy-start.5
  27.1 0.0 copy-start.6
  27.1 0.0 copy-start.7
  27.1 0.0 copy-start.8
  27.1 9.0 %tables.1.top = bf16[2048,128]{1,0:T(8,128)(2,1)} custom-call(bf16[254,1024]{1,0:T(8,128)(2,1)} %xfer_hbm.3, bf16[3,124,1024]{2,1,0:T(8,128)(2,1)} %couple_top_hbm.1, bf16[3,31,1024]{2,1,0:T(8,128)(2,1)} %couple_hbm.5, bf16[256,128]{1,0:T(8,128)(2,1)} %get-tuple-element.21.after.heights_in), custom_call_target="tpu_custom_call" | custom-call | flops 4294967296 | bytes 1048576 | tf_op jit(solution)/shard_map/tables/pallas_call | solution.py:504
  36.1 0.0 copy-start
  36.1 0.0 copy-start.1
  36.1 0.0 copy-start.2
  36.1 0.0 collective-permute-done.from_left
  36.1 0.0 collective-permute-done.1.from_right
  36.1 0.0 copy-done.3
  36.1 0.0 copy-done.4
  36.2 0.0 copy-done.5
  36.2 0.0 copy-done.6
  36.2 0.0 copy-done.7
  36.2 4.7 %local_first.1 = (bf16[1024,768]{1,0:T(8,128)(2,1)S(1)}, f32[16,1024]{1,0:T(8,128)S(1)}, f32[128,128]{1,0:T(8,128)S(1)}) custom-call(s32[12,16]{1,0:T(8,128)S(1)} %copy-done.7, s32[16]{0:T(128)S(1)} %copy-done.8, bf16[16,1024]{1,0:T(8,128)(2,1)S(1)} %copy-done.3, f32[3,1024]{1,0:T(4,128)S(1)} %copy-done.4, bf16[3,31,1024]{2,1,0:T(8,128)(2,1)S(1)} %copy-done.5, ...), custom_call_target="tpu_custom_call" | custom-call | flops 4294967296 | bytes 1048576 | tf_op jit(solution)/shard_map/local_first/pallas_call | solution.py:504
  40.9 0.0 all-to-all-done
  40.9 3.2 %down_up.1 = (bf16[192,128]{1,0:T(8,128)(2,1)S(1)}, bf16[192,128]{1,0:T(8,128)(2,1)S(1)}, bf16[512,128]{1,0:T(8,128)(2,1)}, bf16[16,1024]{1,0:T(8,128)(2,1)S(1)}, bf16[256,128]{1,0:T(8,128)(2,1)S(1)}) custom-call(bf16[32,1024]{1,0:T(8,128)(2,1)S(1)} %copy-done.2, bf16[512,128]{1,0:T(8,128)(2,1)S(1)} %bitcast.4, bf16[2048,128]{1,0:T(8,128)(2,1)S(1)} %copy-done, ...), custom_call_target="tpu_custom_call" | custom-call | flops 1048576 | bytes 1048576 | tf_op jit(solution)/shard_map/down_up/pallas_call | solution.py:504
  44.1 3.6 %collective-permute-start.2 = (bf16[192,128]{1,0:T(8,128)(2,1)S(1)}, bf16[192,128]{1,0:T(8,128)(2,1)S(1)}, u32[]{:S(2)}, u32[]{:S(2)}) collective-permute-start(bf16[192,128]{1,0:T(8,128)(2,1)S(1)} %get-tuple-element.30), channel_id=1, source_target_pairs={{0,4},{4,8},{8,12},{12,16},{16,20},{20,24},{24,28},{28,32},{32,36}... | collective-permute-start | bytes 147464 | tf_op jit(solution)/shard_map/ppermute | solution.py:521
  47.8 1.9 %collective-permute-start.3 = (bf16[192,128]{1,0:T(8,128)(2,1)S(1)}, bf16[192,128]{1,0:T(8,128)(2,1)S(1)}, u32[]{:S(2)}, u32[]{:S(2)}) collective-permute-start(bf16[192,128]{1,0:T(8,128)(2,1)S(1)} %get-tuple-element.31), channel_id=1, source_target_pairs={{4,0},{8,4},{12,8},{16,12},{20,16},{24,20},{28,24},{32,28},{36,32}... | collective-permute-start | bytes 147464 | tf_op jit(solution)/shard_map/ppermute | solution.py:520
  49.7 16.3 %all-to-all-start.1 = ((bf16[128,4,128]{2,1,0:T(4,128)(2,1)}), bf16[128,4,128]{2,1,0:T(4,128)(2,1)S(1)}, u32[]{:S(2)}, u32[]{:S(2)}) async-start(bf16[128,4,128]{2,1,0:T(4,128)(2,1)} %bitcast.2), calls=%async_computation.1 | async-start | bytes 262144 | tf_op jit(solution)/shard_map/all_to_all | solution.py:519
  66.0 0.0 collective-permute-done.2.from_left
  66.0 0.0 collective-permute-done.3.from_right
  66.0 2.6 %local_next.1 = (f32[16,1024]{1,0:T(8,128)S(1)}, f32[128,128]{1,0:T(8,128)S(1)}) custom-call(s32[12,16]{1,0:T(8,128)S(1)} %copy-done.7, bf16[3,31,1024]{2,1,0:T(8,128)(2,1)S(1)} %copy-done.5, bf16[16,1024]{1,0:T(8,128)(2,1)S(1)} %get-tuple-element.28.vectors, bf16[1024,768]{1,0:T(8,128)(2,1)S(1)} %get-tuple-element.29.tiles, ...), custom_call_target="tpu_custom_call" | custom-call | flops 4294967296 | bytes 1048576 | tf_op jit(solution)/shard_map/local_next/pallas_call | solution.py:504
  68.6 10.1 %all-to-all-done.1 = bf16[128,4,128]{2,1,0:T(4,128)(2,1)S(1)} async-done(((bf16[128,4,128]{2,1,0:T(4,128)(2,1)}), bf16[128,4,128]{2,1,0:T(4,128)(2,1)S(1)}, u32[]{:S(2)}, u32[]{:S(2)}) %all-to-all-start.1) | async-done | bytes 131104 | tf_op jit(solution)/shard_map/all_to_all | solution.py:519
  78.7 2.3 %down_last.1 = bf16[16,1024]{1,0:T(8,128)(2,1)} custom-call(bf16[32,1024]{1,0:T(8,128)(2,1)S(1)} %copy-done.2, bf16[512,128]{1,0:T(8,128)(2,1)S(1)} %bitcast.5, bf16[2048,128]{1,0:T(8,128)(2,1)S(1)} %copy-done, bf16[1024,128]{1,0:T(8,128)(2,1)S(1)} %copy-done.1, f32[16,1024]{1,0:T(8,128)S(1)} %get-tuple-element.33.near, ...), custom_call_target="tpu_custom_call" | custom-call | flops 1048576 | bytes 1048576 | tf_op jit(solution)/shard_map/down_last/pallas_call | solution.py:504
  (4 shorter events, 0.0 us)
Async XLA Ops:
  2.9 37.9 %all-to-all-start = ((bf16[128,4,128]{2,1,0:T(4,128)(2,1)}), bf16[128,4,128]{2,1,0:T(4,128)(2,1)S(1)}, u32[]{:S(2)}, u32[]{:S(2)}) async-start(bf16[128,4,128]{2,1,0:T(4,128)(2,1)} %bitcast.6), calls=%async_computation | async-start | bytes 262144 | tf_op jit(solution)/shard_map/all_to_all | solution.py:519
  21.4 14.7 %collective-permute-start = (bf16[256,128]{1,0:T(8,128)(2,1)}, bf16[256,128]{1,0:T(8,128)(2,1)S(1)}, u32[]{:S(2)}, u32[]{:S(2)}) collective-permute-start(bf16[256,128]{1,0:T(8,128)(2,1)} %get-tuple-element.23), channel_id=1, source_target_pairs={{0,4},{4,8},{8,12},{12,16},{16,20},{20,24},{24,28},{28,32},{32,36}... | collective-permute-start | bytes 196616 | tf_op jit(solution)/shard_map/ppermute | solution.py:521
  24.9 11.2 %collective-permute-start.1 = (bf16[256,128]{1,0:T(8,128)(2,1)}, bf16[256,128]{1,0:T(8,128)(2,1)S(1)}, u32[]{:S(2)}, u32[]{:S(2)}) collective-permute-start(bf16[256,128]{1,0:T(8,128)(2,1)} %get-tuple-element.24), channel_id=1, source_target_pairs={{4,0},{8,4},{12,8},{16,12},{20,16},{24,20},{28,24},{32,28},{36,32}... | collective-permute-start | bytes 196616 | tf_op jit(solution)/shard_map/ppermute | solution.py:520
  27.0 9.1 %copy-start.3 = (bf16[16,1024]{1,0:T(8,128)(2,1)S(1)}, bf16[16,1024]{1,0:T(8,128)(2,1)}, u32[]{:S(2)}) copy-start(bf16[16,1024]{1,0:T(8,128)(2,1)} %vectors_hbm.3) | copy-start | bytes 98308
  27.0 9.1 %copy-start.4 = (f32[3,1024]{1,0:T(4,128)S(1)}, f32[3,1024]{1,0:T(4,128)}, u32[]{:S(2)}) copy-start(f32[3,1024]{1,0:T(4,128)} %points_hbm.3) | copy-start | bytes 36868
  27.0 9.1 %copy-start.5 = (bf16[3,31,1024]{2,1,0:T(8,128)(2,1)S(1)}, bf16[3,31,1024]{2,1,0:T(8,128)(2,1)}, u32[]{:S(2)}) copy-start(bf16[3,31,1024]{2,1,0:T(8,128)(2,1)} %couple_hbm.5) | copy-start | bytes 571396
  27.1 9.1 %copy-start.6 = (bf16[256,128]{1,0:T(8,128)(2,1)S(1)}, bf16[256,128]{1,0:T(8,128)(2,1)}, u32[]{:S(2)}) copy-start(bf16[256,128]{1,0:T(8,128)(2,1)} %get-tuple-element.21.after.heights_in) | copy-start | bytes 196612
  27.1 9.1 %copy-start.7 = (s32[12,16]{1,0:T(8,128)S(1)}, s32[12,16]{1,0:T(8,128)}, u32[]{:S(2)}) copy-start(s32[12,16]{1,0:T(8,128)} %cols_hbm.3) | copy-start | bytes 2308
  27.1 9.1 %copy-start.8 = (s32[16]{0:T(128)S(1)}, s32[16]{0:T(128)}, u32[]{:S(2)}) copy-start(s32[16]{0:T(128)} %counts_hbm.1) | copy-start | bytes 196
  36.1 4.8 %copy-start = (bf16[2048,128]{1,0:T(8,128)(2,1)S(1)}, bf16[2048,128]{1,0:T(8,128)(2,1)}, u32[]{:S(2)}) copy-start(bf16[2048,128]{1,0:T(8,128)(2,1)} %tables.1.top) | copy-start | bytes 1572868
  36.1 4.8 %copy-start.1 = (bf16[1024,128]{1,0:T(8,128)(2,1)S(1)}, bf16[1024,128]{1,0:T(8,128)(2,1)}, u32[]{:S(2)}) copy-start(bf16[1024,128]{1,0:T(8,128)(2,1)} %get-tuple-element.22.xfer) | copy-start | bytes 786436
  36.1 4.8 %copy-start.2 = (bf16[32,1024]{1,0:T(8,128)(2,1)S(1)}, bf16[32,1024]{1,0:T(8,128)(2,1)}, u32[]{:S(2)}) copy-start(bf16[32,1024]{1,0:T(8,128)(2,1)} %basis_hbm.5) | copy-start | bytes 196612
  44.1 21.9 %collective-permute-start.2 = (bf16[192,128]{1,0:T(8,128)(2,1)S(1)}, bf16[192,128]{1,0:T(8,128)(2,1)S(1)}, u32[]{:S(2)}, u32[]{:S(2)}) collective-permute-start(bf16[192,128]{1,0:T(8,128)(2,1)S(1)} %get-tuple-element.30), channel_id=1, source_target_pairs={{0,4},{4,8},{8,12},{12,16},{16,20},{20,24},{24,28},{28,32},{32,36}... | collective-permute-start | bytes 147464 | tf_op jit(solution)/shard_map/ppermute | solution.py:521
  47.8 18.2 %collective-permute-start.3 = (bf16[192,128]{1,0:T(8,128)(2,1)S(1)}, bf16[192,128]{1,0:T(8,128)(2,1)S(1)}, u32[]{:S(2)}, u32[]{:S(2)}) collective-permute-start(bf16[192,128]{1,0:T(8,128)(2,1)S(1)} %get-tuple-element.31), channel_id=1, source_target_pairs={{4,0},{8,4},{12,8},{16,12},{20,16},{24,20},{28,24},{32,28},{36,32}... | collective-permute-start | bytes 147464 | tf_op jit(solution)/shard_map/ppermute | solution.py:520
  49.7 29.0 %all-to-all-start.1 = ((bf16[128,4,128]{2,1,0:T(4,128)(2,1)}), bf16[128,4,128]{2,1,0:T(4,128)(2,1)S(1)}, u32[]{:S(2)}, u32[]{:S(2)}) async-start(bf16[128,4,128]{2,1,0:T(4,128)(2,1)} %bitcast.2), calls=%async_computation.1 | async-start | bytes 262144 | tf_op jit(solution)/shard_map/all_to_all | solution.py:519

commit v3 on v2

--- a/solution.py
+++ b/solution.py
@@ -57,18 +57,30 @@
         self.halff = [lanes_in(16, 64 * g, 64, F32) for g in range(2)]
 
 
-def spread_matrix():
-    row = lax.broadcasted_iota(jnp.int32, (128, 512), 0)
-    col = lax.broadcasted_iota(jnp.int32, (128, 512), 1)
-    return (row == ((col >> 7) << 5) + (col & 31)).astype(F32).astype(BF16)
-
-
-def spread_table(table, spread, out, first):
+def repeat_matrix():
+    row = lax.broadcasted_iota(jnp.int32, (128, 128), 0)
+    col = lax.broadcasted_iota(jnp.int32, (128, 128), 1)
+    return ((row & 31) == (col & 31)).astype(F32).astype(BF16)
+
+
+def spread_table(table, out, first=0):
+    table = table.astype(F32)
+    row = lax.broadcasted_iota(jnp.int32, (8, 128), 0)
+    lane = lax.broadcasted_iota(jnp.int32, (8, 128), 1)
+    mine = ((row & 3) == (lane >> 5)).astype(F32)
+    upper = row < 4
+    repeat = repeat_matrix()
     count = table.shape[0]
-    for c in range(8):
-        wide = nn(table[:, 128 * c : 128 * c + 128], spread)
-        for q in range(4):
-            out[pl.ds(first * 32 + 4 * c + q, count, stride=32), :] = wide[:, 128 * q : 128 * q + 128]
+    for n in range(0, count, 4):
+        parts = []
+        for node in range(n, min(n + 4, count)):
+            for j in range(4):
+                one = table[node : node + 1, 256 * j : 256 * j + 128]
+                two = table[node : node + 1, 256 * j + 128 : 256 * j + 256]
+                parts.append(jnp.where(upper, one, two) * mine)
+        wide = nn(jnp.concatenate(parts, axis=0).astype(BF16), repeat)
+        at = (first + n) * 32
+        out[at : at + wide.shape[0], :] = wide.astype(out.dtype)
 
 
 def up_pass(signal, basis, xfer, m):
@@ -192,65 +204,94 @@
     return down
 
 
-def build_top(place, xfer_top, couple, couple_top, spread, wide_xfer, wide_own, wide_couple, levels, top, m):
-    spread_table(xfer_top[...], spread, wide_xfer, 0)
-    for k in range(3):
-        spread_table(couple[k, 30:31, :], spread, wide_own, k)
+def one_hot(wanted, count):
+    col = lax.broadcasted_iota(jnp.int32, wanted.shape, 1)
+    return (col == wanted).astype(F32).astype(BF16)
+
+
+def pack_matrix():
+    row = lax.broadcasted_iota(jnp.int32, (512, 512), 0)
+    col = lax.broadcasted_iota(jnp.int32, (512, 512), 1)
+    same = ((row >> 7) == ((col >> 5) & 3)) & (((row >> 5) & 3) == (col >> 7)) & ((row & 31) == (col & 31))
+    return same.astype(F32).astype(BF16)
+
+
+def pack_xfer(xfer_top, wide_xfer):
+    row = lax.broadcasted_iota(jnp.int32, (256, 254), 0)
+    at = row & 63
+    wanted = jnp.zeros((256, 254), jnp.int32) - 1
+    for level in range(4, -1, -1):
+        first = 64 - (64 >> level)
+        node = TOP_XFER[level] + (row >> 6) * (32 >> level) + at - first
+        wanted = jnp.where((at >= first) & (at < first + (32 >> level)), node, wanted)
+    packed = nn(one_hot(wanted, 254), xfer_top[...]).astype(BF16)
+    pack = pack_matrix()
+    for c in range(8):
+        left = jnp.concatenate([packed[64 * g : 64 * g + 64, 128 * c : 128 * c + 128] for g in range(4)], axis=1)
+        wide = nn(left, pack)
+        for q in range(4):
+            wide_xfer[pl.ds(4 * c + q, 64, stride=32), :] = wide[:, 128 * q : 128 * q + 128]
+
+
+def build_top(place, xfer_top, couple, couple_top, wide_xfer, wide_path, levels, top):
+    row = lax.broadcasted_iota(jnp.int32, (8, 254), 0)
+    wanted = jnp.zeros((8, 254), jnp.int32) - 1
+    for level in range(5):
+        wanted = jnp.where(row == level, TOP_XFER[level] + (place >> level), wanted)
+    rows = [nn(one_hot(wanted, 254), xfer_top[...])]
     row = lax.broadcasted_iota(jnp.int32, (8, 124), 0)
-    col = lax.broadcasted_iota(jnp.int32, (8, 124), 1)
     wanted = jnp.zeros((8, 124), jnp.int32) - 1
     for level in range(1, 6):
-        wanted = jnp.where(row == level - 1, TOP_COUPLE[level] + (place >> level), wanted)
-    pick = (col == wanted).astype(F32).astype(BF16)
+        wanted = jnp.where(row == level, TOP_COUPLE[level] + (place >> level), wanted)
+    pick = one_hot(wanted, 124)
+    row = lax.broadcasted_iota(jnp.int32, (8, 31), 0)
+    pick_own = one_hot(jnp.where(row == 0, LOW[4], -1), 31)
     for k in range(3):
-        spread_table(nn(pick, couple_top[k]).astype(BF16), spread, wide_couple, 8 * k)
+        rows.append(nn(pick, couple_top[k]) + nn(pick_own, couple[k]))
+    spread_table(jnp.concatenate(rows, axis=0), wide_path)
+
     row = lax.broadcasted_iota(jnp.int32, (32, 128), 0)
     lane = lax.broadcasted_iota(jnp.int32, (32, 128), 1)
-    path = (row == (lane & 31)).astype(F32)
+    repeat = (row == (lane & 31)).astype(F32).astype(BF16)
+    repeat = jnp.concatenate([repeat, repeat], axis=0)
     groupf = [lanes_in(32, 32 * g, 32, F32) for g in range(4)]
+    path = (lax.broadcasted_iota(jnp.int32, (32, 32), 0) == lax.broadcasted_iota(jnp.int32, (32, 32), 1)).astype(F32)
     slots = []
     for level in range(6):
-        if level == 0:
-            tables = [wide_own[32 * k : 32 * k + 32, :] for k in range(3)]
-        else:
-            tables = [wide_couple[(8 * k + level - 1) * 32 : (8 * k + level) * 32, :] for k in range(3)]
-        at = pl.multiple_of((TOP_XFER[level] + (place >> level)) * 32, 32)
-        tables.append(wide_xfer[pl.ds(at, 32), :])
-        left = tables[0] * groupf[0]
+        at = [level, 8 + level, 16 + level, 24 + level]
+        right = wide_path[32 * at[0] : 32 * at[0] + 32, :] * groupf[0]
         for g in range(1, 4):
-            left = left + tables[g] * groupf[g]
-        left = left.astype(BF16)
-        high, low = halves(path)
-        both = tn(jnp.concatenate([left, left], axis=0), jnp.concatenate([high, low], axis=0))
-        slots.append([both[32 * k : 32 * k + 32] for k in range(3)])
-        path = both[96:128]
-    row = lax.broadcasted_iota(jnp.int32, (256, 128), 0)
-    lane = lax.broadcasted_iota(jnp.int32, (256, 128), 1)
-    family = ((row >> 6) == (lane >> 5)).astype(F32)
+            right = right + wide_path[32 * at[g] : 32 * at[g] + 32, :] * groupf[g]
+        both = nn(jnp.concatenate(halves(path), axis=0), right.astype(BF16))
+        both = both[:32] + both[32:]
+        path = both[:, 0:32]
+        turned = tn(jnp.concatenate(halves(both), axis=0), repeat)
+        slots.append([turned[32 * k + 32 : 32 * k + 64] for k in range(3)])
+
+    row = lax.broadcasted_iota(jnp.int32, (128, 128), 0)
+    diagonal = ((row >> 5) == (lax.broadcasted_iota(jnp.int32, (128, 128), 1) >> 5)).astype(F32).astype(BF16)
     for level in range(5, -1, -1):
         here = levels[level]
-        count = DEVICES >> level
+        blocks = 32 >> level
         if level == 5:
-            here[...] = jnp.zeros((128, 128), F32)
+            here[...] = jnp.zeros((32, 128), F32)
         else:
-            for t in range(count // 8):
-                first = (TOP_XFER[level] + 8 * t) * 32
-                left = (wide_xfer[first : first + 256, :] * family).astype(BF16)
-                high, low = halves(levels[level + 1][128 * t : 128 * t + 128, :])
-                here[256 * t : 256 * t + 256, :] = nn(
-                    jnp.concatenate([left, left], axis=1), jnp.concatenate([high, low], axis=0)
+            first = 64 - (64 >> level)
+            for b in range(blocks // 2):
+                high, low = halves(levels[level + 1][32 * b : 32 * b + 32, :])
+                right = [jnp.concatenate([part] * 4, axis=0) * diagonal for part in (high, low)]
+                left = wide_xfer[(first + 2 * b) * 32 : (first + 2 * b + 2) * 32, :].astype(BF16)
+                here[64 * b : 64 * b + 64, :] = nn(
+                    jnp.concatenate([left, left], axis=1), jnp.concatenate(right, axis=0)
                 )
         node = place >> level
         third = jnp.where(node % 2 == 0, node + 3, node - 3)
         for k, other in enumerate((node - 2, node + 2, third)):
-            live = ((other >= 0) & (other < count)).astype(F32)
-            at = pl.multiple_of(jnp.clip(other, 0, count - 1) * 32, 32)
-            here[pl.ds(at, 32), :] = here[pl.ds(at, 32), :] + slots[level][k] * live
-    for c in range(32):
-        block = levels[0][128 * c : 128 * c + 32, :] * groupf[0]
-        for g in range(1, 4):
-            block = block + levels[0][128 * c + 32 * g : 128 * c + 32 * g + 32, :] * groupf[g]
-        top[32 * c : 32 * c + 32, :], top[1024 + 32 * c : 1056 + 32 * c, :] = halves(block)
+            other = jnp.where((other >= 0) & (other < 4 * blocks), other, -blocks)
+            at = pl.multiple_of((other & (blocks - 1)) * 32, 32)
+            mine = jnp.where((lane >> 5) == (other >> (5 - level)), slots[level][k], 0.0)
+            here[pl.ds(at, 32), :] = here[pl.ds(at, 32), :] + mine
+    top[:1024, :], top[1024:, :] = halves(levels[0][...])
 
 
 def point_parts(points):
@@ -393,15 +434,13 @@
 
 def first_kernel(
     vectors_hbm, points_hbm, basis_hbm, xfer_hbm, left, right, gather, heights_out, xfer_out,
-    vectors, points, basis, xfer_low, wide, sems,
+    vectors, points, basis, xfer_low, sems,
 ):
     copies = fetch((xfer_hbm, vectors_hbm, basis_hbm, points_hbm), (xfer_low, vectors, basis, points), sems)
     m = Masks()
-    spread = spread_matrix()
-    wide[960:1024, :] = jnp.zeros((64, 128), F32)
+    xfer_out[960:1024, :] = jnp.zeros((64, 128), BF16)
     copies[0].wait()
-    spread_table(xfer_low[...], spread, wide, 0)
-    xfer_out[...] = wide[...].astype(BF16)
+    spread_table(xfer_low[...], xfer_out)
     copies[1].wait()
     copies[2].wait()
     signal = chunks_of(vectors)
@@ -417,21 +456,21 @@
 
 def table_kernel(
     xfer_hbm, couple_top_hbm, couple_hbm, after, top,
-    xfer_top, couple_top, couple, wide, wide_xfer, wide_couple, sems, *levels,
+    xfer_top, couple_top, couple, wide_xfer, wide_path, sems, *levels,
 ):
     del after
-    copies = fetch((xfer_hbm, couple_top_hbm, couple_hbm), (xfer_top, couple_top, couple), sems)
-    m = Masks()
-    place = lax.axis_index("leaf")
-    for copy in copies:
-        copy.wait()
-    build_top(place, xfer_top, couple, couple_top, spread_matrix(), wide_xfer, wide, wide_couple, levels, top, m)
+    copies = fetch((xfer_hbm, couple_hbm, couple_top_hbm), (xfer_top, couple, couple_top), sems)
+    copies[0].wait()
+    pack_xfer(xfer_top, wide_xfer)
+    copies[1].wait()
+    copies[2].wait()
+    build_top(lax.axis_index("leaf"), xfer_top, couple, couple_top, wide_xfer, wide_path, levels, top)
 
 
 def local_first_kernel(
     cols_hbm, counts_hbm, vectors_hbm, points_hbm, couple_hbm, from_left, from_right, heights_in,
     tiles, near_out, couplings_out,
-    cols, counts, vectors, points, couple, wide, couple_wide, places_left, places_right, near_left, near_right, sems,
+    cols, counts, vectors, points, couple, couple_wide, places_left, places_right, near_left, near_right, sems,
 ):
     copies = fetch(
         (cols_hbm, counts_hbm, vectors_hbm, points_hbm, couple_hbm), (cols, counts, vectors, points, couple), sems
@@ -443,31 +482,33 @@
     build_tiles(
         place, point_parts(points[...]), cols, counts, from_left, from_right, places_left, places_right, tiles
     )
-    spread_couple(couple, wide, couple_wide)
+    spread_couple(couple, couple_wide)
     couplings = couple_low(load_heights(heights_in), from_left, from_right, couple_wide, m)
     near = near_field(place, chunks_of(vectors), from_left, from_right, cols, tiles, near_left, near_right, m)
     store_local(near, couplings, near_out, couplings_out)
 
 
-def spread_couple(couple, wide, out):
-    spread = spread_matrix()
-    wide[93 * 32 :, :] = jnp.zeros((96, 128), F32)
+def spread_couple(couple, out):
+    out[93 * 32 :, :] = jnp.zeros((96, 128), BF16)
     for k in range(3):
-        spread_table(couple[k], spread, wide, 31 * k)
-    out[...] = wide[...].astype(BF16)
+        spread_table(couple[k], out, 31 * k)
+
+
+def spread_kernel(couple_hbm, after, out, couple, sems):
+    del after
+    fetch((couple_hbm,), (couple,), sems)[0].wait()
+    spread_couple(couple, out)
 
 
 def local_next_kernel(
-    cols_hbm, couple_hbm, vectors, tiles, from_left, from_right, heights_in, near_out, couplings_out,
-    cols, couple, wide, couple_wide, near_left, near_right, sems,
+    cols_hbm, couple_wide, vectors, tiles, from_left, from_right, heights_in, near_out, couplings_out,
+    cols, near_left, near_right, sems,
 ):
-    copies = fetch((couple_hbm, cols_hbm), (couple, cols), sems)
+    copies = fetch((cols_hbm,), (cols,), sems)
     m = Masks()
     place = lax.axis_index("leaf")
+    couplings = couple_low(load_heights(heights_in), from_left, from_right, couple_wide, m)
     copies[0].wait()
-    spread_couple(couple, wide, couple_wide)
-    couplings = couple_low(load_heights(heights_in), from_left, from_right, couple_wide, m)
-    copies[1].wait()
     near = near_field(place, chunks_of(vectors), from_left, from_right, cols, tiles, near_left, near_right, m)
     store_local(near, couplings, near_out, couplings_out)
 
@@ -516,7 +557,9 @@
 def exchange(left, right, gather):
     count = lax.axis_size("leaf")
     blocks = gather.reshape(count, 4, 128)
-    gathered = lax.all_to_all(blocks, "leaf", 0, 0, tiled=True)
+    quarter = count // 4
+    order = [g * quarter + b for b in range(quarter) for g in range(4)]
+    gathered = lax.all_to_all(blocks, "leaf", 0, 0, tiled=True, axis_index_groups=[order])
     from_right = lax.ppermute(left, "leaf", [(i + 1, i) for i in range(count - 1)])
     from_left = lax.ppermute(right, "leaf", [(i, i + 1) for i in range(count - 1)])
     return from_left, from_right, gathered.reshape(count * 4, 128)
@@ -526,20 +569,20 @@
     vm, sm = pltpu.VMEM, pltpu.SMEM
     sems = pltpu.SemaphoreType.DMA
     signal_buf, basis_buf, points_buf = vm((16, 1024), BF16), vm((32, 1024), BF16), vm((3, 1024), F32)
-    couple_buf = [vm((3, 31, 1024), BF16), vm((3072, 128), F32)]
+    couple_buf = [vm((3, 31, 1024), BF16)]
     blocks = [vm((32, 16, 128), BF16)] * 2
     sends = [((512, 128), BF16), ((256, 128), BF16)]
     local = [((16, 1024), F32), ((128, 128), F32)]
     left, right, gather, heights, xfer = call(
         first_kernel, "up_first", (vectors, points, basis, xfer_low), (),
         [((256, 128), BF16)] * 2 + sends + [((1024, 128), BF16)],
-        [signal_buf, points_buf, basis_buf, vm((30, 1024), BF16), vm((1024, 128), F32), sems((4,))], 1 << 20, VMEM_MOST,
+        [signal_buf, points_buf, basis_buf, vm((30, 1024), BF16), sems((4,))], 1 << 20, VMEM_MOST,
     )
     from_left, from_right, gathered = exchange(left, right, gather)
     (top,) = call(
         table_kernel, "tables", (xfer_top, couple_top, couple, heights), (), [((2048, 128), BF16)],
-        [vm((254, 1024), BF16), vm((3, 124, 1024), BF16), vm((3, 31, 1024), BF16), vm((96, 128), F32),
-         vm((8128, 128), F32), vm((768, 128), F32), sems((3,))] + [vm((4096 >> level, 128), F32) for level in range(6)],
+        [vm((254, 1024), BF16), vm((3, 124, 1024), BF16), vm((3, 31, 1024), BF16), vm((2048, 128), F32),
+         vm((1024, 128), F32), sems((3,))] + [vm((1024 >> level, 128), F32) for level in range(6)],
         1 << 32, VMEM_MOST,
     )
     tiles, near, couplings = call(
@@ -553,9 +596,13 @@
         [((192, 128), BF16)] * 2 + [sends[0], ((16, 1024), BF16), sends[1]], [basis_buf, sems((1,))], 1 << 20,
     )
     from_left, from_right, gathered = exchange(left, right, gather)
+    (couple_wide,) = call(
+        spread_kernel, "spread", (couple, heights), (), [((3072, 128), BF16)], couple_buf + [sems((1,))], 1 << 32
+    )
     near, couplings = call(
-        local_next_kernel, "local_next", (near_cols, couple), (signal, tiles, from_left, from_right, heights), local,
-        [sm((12, 16), jnp.int32)] + couple_buf + [vm((3072, 128), BF16)] + blocks + [sems((2,))], 1 << 32,
+        local_next_kernel, "local_next", (near_cols,),
+        (couple_wide, signal, tiles, from_left, from_right, heights), local,
+        [sm((12, 16), jnp.int32)] + blocks + [sems((1,))], 1 << 32,
     )
     (result,) = call(
         down_last_kernel, "down_last", (basis,), (gathered, top, xfer, near, couplings), [((16, 1024), BF16)],

time: 81.6 us -> 69.7 us (0.85)
  waiting for transfers between devices: 10.1 us -> 4.69 us
  Pallas kernels: 24.7 us -> 20.2 us
  starting transfers between devices: 45.9 us -> 44.1 us
    all_to_all x2, waiting for transfers between devices: 10.1 us -> 1.59 us  [exchange(): lax.all_to_all(blocks, 'leaf', 0, 0, tiled=True, axis_index_groups=[order])]
    pallas_call x6 -> x7, Pallas kernels: 24.7 us -> 20.2 us  [call(): pl.pallas_call(kernel, out_shape=[jax.ShapeDtypeStruct(shape, dtype) for...]
    ppermute x2, waiting for transfers between devices: 0.01 us -> 3.1 us  [exchange(): lax.ppermute(left, 'leaf', [(i + 1, i) for i in range(count - 1)])]
    all_to_all x2, starting transfers between devices: 34.7 us -> 33.2 us  [exchange(): lax.all_to_all(blocks, 'leaf', 0, 0, tiled=True, axis_index_groups=[order])]
  transfers between devices with their start and end apart: 6 -> 6, of which waited for: 1 -> 2; matrix products, arithmetic and copies ran while one was open for 0% -> 0% of each run, Pallas kernels for 20% -> 17%
where the time goes in v3:
time: 69.7 us; the launch traced here: 69.4 us
  starting transfers between devices  44.1 us (63%)
  Pallas kernels  20.2 us (29%)
  waiting for transfers between devices  4.69 us (7%)
    all_to_all x2, starting transfers between devices, exchange(): lax.all_to_all(blocks, 'leaf', 0, 0, tiled=True, axis_index_groups=[order])  33.2 us
    pallas_call x7, Pallas kernels, call(): pl.pallas_call(kernel, out_shape=[jax.ShapeDtypeStruct(shape, dtype) for...  20.2 us
    ppermute x2, starting transfers between devices, exchange(): lax.ppermute(right, 'leaf', [(i, i + 1) for i in range(count - 1)])  7.08 us
    ppermute x2, starting transfers between devices, exchange(): lax.ppermute(left, 'leaf', [(i + 1, i) for i in range(count - 1)])  3.84 us
    ppermute x2, waiting for transfers between devices, exchange(): lax.ppermute(left, 'leaf', [(i + 1, i) for i in range(count - 1)])  3.1 us
    all_to_all x2, waiting for transfers between devices, exchange(): lax.all_to_all(blocks, 'leaf', 0, 0, tiled=True, axis_index_groups=[order])  1.59 us
  transfers between devices with their start and end apart: 6, of which 2 were waited for; matrix products, arithmetic and copies ran while one was open for 0% of the time, Pallas kernels for 17%

profile of v3, /device:TPU:1, one launch (start us, length us, event | category | flops | bytes accessed | tf_op | source)
XLA Modules:
  0.0 69.4 jit_solution(12270918494935214995)
XLA Ops:
  0.0 2.7 %up_first.1 = (bf16[256,128]{1,0:T(8,128)(2,1)}, bf16[256,128]{1,0:T(8,128)(2,1)}, bf16[512,128]{1,0:T(8,128)(2,1)}, bf16[256,128]{1,0:T(8,128)(2,1)}, bf16[1024,128]{1,0:T(8,128)(2,1)}) custom-call(bf16[16,1024]{1,0:T(8,128)(2,1)} %vectors_hbm.3, f32[3,1024]{1,0:T(4,128)} %points_hbm.3, bf16[32,1024]{1,0:T(8,128)(2,1)} %basis_hbm.5, bf16[30,1024]{1,0:T(8,128)(2,1)} %xfer_hbm.2), custom_call_target="tpu_custom_call" | custom-call | flops 1048576 | bytes 1048576 | tf_op jit(solution)/shard_map/up_first/pallas_call | solution.py:545
  2.7 18.4 %all-to-all-start = ((bf16[128,4,128]{2,1,0:T(4,128)(2,1)}), bf16[128,4,128]{2,1,0:T(4,128)(2,1)S(1)}, u32[]{:S(2)}, u32[]{:S(2)}) async-start(bf16[128,4,128]{2,1,0:T(4,128)(2,1)} %bitcast.6), calls=%async_computation | async-start | bytes 262144 | tf_op jit(solution)/shard_map/all_to_all | solution.py:562
  21.2 3.5 %collective-permute-start = (bf16[256,128]{1,0:T(8,128)(2,1)}, bf16[256,128]{1,0:T(8,128)(2,1)S(1)}, u32[]{:S(2)}, u32[]{:S(2)}) collective-permute-start(bf16[256,128]{1,0:T(8,128)(2,1)} %get-tuple-element.23), channel_id=1, source_target_pairs={{0,4},{4,8},{8,12},{12,16},{16,20},{20,24},{24,28},{28,32},{32,36}... | collective-permute-start | bytes 196616 | tf_op jit(solution)/shard_map/ppermute | solution.py:564
  24.7 1.9 %collective-permute-start.1 = (bf16[256,128]{1,0:T(8,128)(2,1)}, bf16[256,128]{1,0:T(8,128)(2,1)S(1)}, u32[]{:S(2)}, u32[]{:S(2)}) collective-permute-start(bf16[256,128]{1,0:T(8,128)(2,1)} %get-tuple-element.24), channel_id=1, source_target_pairs={{4,0},{8,4},{12,8},{16,12},{20,16},{24,20},{28,24},{32,28},{36,32}... | collective-permute-start | bytes 196616 | tf_op jit(solution)/shard_map/ppermute | solution.py:563
  26.6 0.0 copy-start.3
  26.6 0.0 copy-start.4
  26.7 0.0 copy-start.5
  26.7 0.0 copy-start.6
  26.7 0.0 copy-start.7
  26.7 0.0 copy-start.8
  26.7 6.1 %tables.1.top = bf16[2048,128]{1,0:T(8,128)(2,1)} custom-call(bf16[254,1024]{1,0:T(8,128)(2,1)} %xfer_hbm.3, bf16[3,124,1024]{2,1,0:T(8,128)(2,1)} %couple_top_hbm.1, bf16[3,31,1024]{2,1,0:T(8,128)(2,1)} %couple_hbm.5, bf16[256,128]{1,0:T(8,128)(2,1)} %get-tuple-element.21.after.heights_in), custom_call_target="tpu_custom_call" | custom-call | flops 4294967296 | bytes 1048576 | tf_op jit(solution)/shard_map/tables/pallas_call | solution.py:545
  32.8 0.0 copy-start
  32.8 0.0 copy-start.1
  32.8 0.0 copy-start.2
  32.8 0.0 collective-permute-done.from_left
  32.8 0.0 collective-permute-done.1.from_right
  32.9 0.0 copy-done.3
  32.9 0.0 copy-done.4
  32.9 0.0 copy-done.5
  32.9 0.0 copy-done.6
  32.9 3.9 %local_first.1 = (bf16[1024,768]{1,0:T(8,128)(2,1)S(1)}, f32[16,1024]{1,0:T(8,128)S(1)}, f32[128,128]{1,0:T(8,128)S(1)}) custom-call(s32[12,16]{1,0:T(8,128)S(1)} %copy-done.7, s32[16]{0:T(128)S(1)} %copy-done.8, bf16[16,1024]{1,0:T(8,128)(2,1)S(1)} %copy-done.3, f32[3,1024]{1,0:T(4,128)S(1)} %copy-done.4, bf16[3,31,1024]{2,1,0:T(8,128)(2,1)S(1)} %copy-done.5, ...), custom_call_target="tpu_custom_call" | custom-call | flops 4294967296 | bytes 1048576 | tf_op jit(solution)/shard_map/local_first/pallas_call | solution.py:545
  36.8 0.0 all-to-all-done
  36.8 3.2 %down_up.1 = (bf16[192,128]{1,0:T(8,128)(2,1)S(1)}, bf16[192,128]{1,0:T(8,128)(2,1)S(1)}, bf16[512,128]{1,0:T(8,128)(2,1)}, bf16[16,1024]{1,0:T(8,128)(2,1)S(1)}, bf16[256,128]{1,0:T(8,128)(2,1)S(1)}) custom-call(bf16[32,1024]{1,0:T(8,128)(2,1)S(1)} %copy-done.2, bf16[512,128]{1,0:T(8,128)(2,1)S(1)} %bitcast.5, bf16[2048,128]{1,0:T(8,128)(2,1)S(1)} %copy-done, ...), custom_call_target="tpu_custom_call" | custom-call | flops 1048576 | bytes 1048576 | tf_op jit(solution)/shard_map/down_up/pallas_call | solution.py:545
  40.0 14.8 %all-to-all-start.1 = ((bf16[128,4,128]{2,1,0:T(4,128)(2,1)}), bf16[128,4,128]{2,1,0:T(4,128)(2,1)S(1)}, u32[]{:S(2)}, u32[]{:S(2)}) async-start(bf16[128,4,128]{2,1,0:T(4,128)(2,1)} %bitcast.2), calls=%async_computation.1 | async-start | bytes 262144 | tf_op jit(solution)/shard_map/all_to_all | solution.py:562
  54.8 3.5 %collective-permute-start.2 = (bf16[192,128]{1,0:T(8,128)(2,1)S(1)}, bf16[192,128]{1,0:T(8,128)(2,1)S(1)}, u32[]{:S(2)}, u32[]{:S(2)}) collective-permute-start(bf16[192,128]{1,0:T(8,128)(2,1)S(1)} %get-tuple-element.31), channel_id=1, source_target_pairs={{0,4},{4,8},{8,12},{12,16},{16,20},{20,24},{24,28},{28,32},{32,36}... | collective-permute-start | bytes 147464 | tf_op jit(solution)/shard_map/ppermute | solution.py:564
  58.4 1.9 %collective-permute-start.3 = (bf16[192,128]{1,0:T(8,128)(2,1)S(1)}, bf16[192,128]{1,0:T(8,128)(2,1)S(1)}, u32[]{:S(2)}, u32[]{:S(2)}) collective-permute-start(bf16[192,128]{1,0:T(8,128)(2,1)S(1)} %get-tuple-element.32), channel_id=1, source_target_pairs={{4,0},{8,4},{12,8},{16,12},{20,16},{24,20},{28,24},{32,28},{36,32}... | collective-permute-start | bytes 147464 | tf_op jit(solution)/shard_map/ppermute | solution.py:563
  60.3 0.7 spread.1.couple_wide
  61.0 0.0 collective-permute-done.2.from_left
  61.0 3.1 %collective-permute-done.3.from_right = bf16[192,128]{1,0:T(8,128)(2,1)S(1)} collective-permute-done((bf16[192,128]{1,0:T(8,128)(2,1)S(1)}, bf16[192,128]{1,0:T(8,128)(2,1)S(1)}, u32[]{:S(2)}, u32[]{:S(2)}) %collective-permute-start.3) | collective-permute-done | bytes 49184 | tf_op jit(solution)/shard_map/ppermute | solution.py:563
  64.1 1.3 %local_next.1 = (f32[16,1024]{1,0:T(8,128)S(1)}, f32[128,128]{1,0:T(8,128)S(1)}) custom-call(s32[12,16]{1,0:T(8,128)S(1)} %copy-done.7, bf16[3072,128]{1,0:T(8,128)(2,1)S(1)} %spread.1.couple_wide, bf16[16,1024]{1,0:T(8,128)(2,1)S(1)} %get-tuple-element.29.vectors, bf16[1024,768]{1,0:T(8,128)(2,1)S(1)} %get-tuple-element.30.tiles, ...), custom_call_target="tpu_custom_call" | custom-call | flops 4294967296 | bytes 1048576 | tf_op jit(solution)/shard_map/local_next/pallas_call | solution.py:545
  65.4 1.6 %all-to-all-done.1 = bf16[128,4,128]{2,1,0:T(4,128)(2,1)S(1)} async-done(((bf16[128,4,128]{2,1,0:T(4,128)(2,1)}), bf16[128,4,128]{2,1,0:T(4,128)(2,1)S(1)}, u32[]{:S(2)}, u32[]{:S(2)}) %all-to-all-start.1) | async-done | bytes 131104 | tf_op jit(solution)/shard_map/all_to_all | solution.py:562
  67.0 2.3 %down_last.1 = bf16[16,1024]{1,0:T(8,128)(2,1)} custom-call(bf16[32,1024]{1,0:T(8,128)(2,1)S(1)} %copy-done.2, bf16[512,128]{1,0:T(8,128)(2,1)S(1)} %bitcast.4, bf16[2048,128]{1,0:T(8,128)(2,1)S(1)} %copy-done, bf16[1024,128]{1,0:T(8,128)(2,1)S(1)} %copy-done.1, f32[16,1024]{1,0:T(8,128)S(1)} %get-tuple-element.33.near, ...), custom_call_target="tpu_custom_call" | custom-call | flops 1048576 | bytes 1048576 | tf_op jit(solution)/shard_map/down_last/pallas_call | solution.py:545
  (5 shorter events, 0.0 us)
Async XLA Ops:
  2.7 34.1 %all-to-all-start = ((bf16[128,4,128]{2,1,0:T(4,128)(2,1)}), bf16[128,4,128]{2,1,0:T(4,128)(2,1)S(1)}, u32[]{:S(2)}, u32[]{:S(2)}) async-start(bf16[128,4,128]{2,1,0:T(4,128)(2,1)} %bitcast.6), calls=%async_computation | async-start | bytes 262144 | tf_op jit(solution)/shard_map/all_to_all | solution.py:562
  21.2 11.7 %collective-permute-start = (bf16[256,128]{1,0:T(8,128)(2,1)}, bf16[256,128]{1,0:T(8,128)(2,1)S(1)}, u32[]{:S(2)}, u32[]{:S(2)}) collective-permute-start(bf16[256,128]{1,0:T(8,128)(2,1)} %get-tuple-element.23), channel_id=1, source_target_pairs={{0,4},{4,8},{8,12},{12,16},{16,20},{20,24},{24,28},{28,32},{32,36}... | collective-permute-start | bytes 196616 | tf_op jit(solution)/shard_map/ppermute | solution.py:564
  24.7 8.2 %collective-permute-start.1 = (bf16[256,128]{1,0:T(8,128)(2,1)}, bf16[256,128]{1,0:T(8,128)(2,1)S(1)}, u32[]{:S(2)}, u32[]{:S(2)}) collective-permute-start(bf16[256,128]{1,0:T(8,128)(2,1)} %get-tuple-element.24), channel_id=1, source_target_pairs={{4,0},{8,4},{12,8},{16,12},{20,16},{24,20},{28,24},{32,28},{36,32}... | collective-permute-start | bytes 196616 | tf_op jit(solution)/shard_map/ppermute | solution.py:563
  26.6 6.2 %copy-start.3 = (bf16[16,1024]{1,0:T(8,128)(2,1)S(1)}, bf16[16,1024]{1,0:T(8,128)(2,1)}, u32[]{:S(2)}) copy-start(bf16[16,1024]{1,0:T(8,128)(2,1)} %vectors_hbm.3) | copy-start | bytes 98308
  26.6 6.2 %copy-start.4 = (f32[3,1024]{1,0:T(4,128)S(1)}, f32[3,1024]{1,0:T(4,128)}, u32[]{:S(2)}) copy-start(f32[3,1024]{1,0:T(4,128)} %points_hbm.3) | copy-start | bytes 36868
  26.7 6.2 %copy-start.5 = (bf16[3,31,1024]{2,1,0:T(8,128)(2,1)S(1)}, bf16[3,31,1024]{2,1,0:T(8,128)(2,1)}, u32[]{:S(2)}) copy-start(bf16[3,31,1024]{2,1,0:T(8,128)(2,1)} %couple_hbm.5) | copy-start | bytes 571396
  26.7 6.2 %copy-start.6 = (bf16[256,128]{1,0:T(8,128)(2,1)S(1)}, bf16[256,128]{1,0:T(8,128)(2,1)}, u32[]{:S(2)}) copy-start(bf16[256,128]{1,0:T(8,128)(2,1)} %get-tuple-element.21.after.heights_in) | copy-start | bytes 196612
  26.7 6.2 %copy-start.7 = (s32[12,16]{1,0:T(8,128)S(1)}, s32[12,16]{1,0:T(8,128)}, u32[]{:S(2)}) copy-start(s32[12,16]{1,0:T(8,128)} %cols_hbm.3) | copy-start | bytes 2308
  26.7 6.2 %copy-start.8 = (s32[16]{0:T(128)S(1)}, s32[16]{0:T(128)}, u32[]{:S(2)}) copy-start(s32[16]{0:T(128)} %counts_hbm.1) | copy-start | bytes 196
  32.8 4.0 %copy-start = (bf16[2048,128]{1,0:T(8,128)(2,1)S(1)}, bf16[2048,128]{1,0:T(8,128)(2,1)}, u32[]{:S(2)}) copy-start(bf16[2048,128]{1,0:T(8,128)(2,1)} %tables.1.top) | copy-start | bytes 1572868
  32.8 4.0 %copy-start.1 = (bf16[1024,128]{1,0:T(8,128)(2,1)S(1)}, bf16[1024,128]{1,0:T(8,128)(2,1)}, u32[]{:S(2)}) copy-start(bf16[1024,128]{1,0:T(8,128)(2,1)} %get-tuple-element.22.xfer) | copy-start | bytes 786436
  32.8 4.0 %copy-start.2 = (bf16[32,1024]{1,0:T(8,128)(2,1)S(1)}, bf16[32,1024]{1,0:T(8,128)(2,1)}, u32[]{:S(2)}) copy-start(bf16[32,1024]{1,0:T(8,128)(2,1)} %basis_hbm.5) | copy-start | bytes 196612
  40.0 27.0 %all-to-all-start.1 = ((bf16[128,4,128]{2,1,0:T(4,128)(2,1)}), bf16[128,4,128]{2,1,0:T(4,128)(2,1)S(1)}, u32[]{:S(2)}, u32[]{:S(2)}) async-start(bf16[128,4,128]{2,1,0:T(4,128)(2,1)} %bitcast.2), calls=%async_computation.1 | async-start | bytes 262144 | tf_op jit(solution)/shard_map/all_to_all | solution.py:562
  54.8 6.2 %collective-permute-start.2 = (bf16[192,128]{1,0:T(8,128)(2,1)S(1)}, bf16[192,128]{1,0:T(8,128)(2,1)S(1)}, u32[]{:S(2)}, u32[]{:S(2)}) collective-permute-start(bf16[192,128]{1,0:T(8,128)(2,1)S(1)} %get-tuple-element.31), channel_id=1, source_target_pairs={{0,4},{4,8},{8,12},{12,16},{16,20},{20,24},{24,28},{28,32},{32,36}... | collective-permute-start | bytes 147464 | tf_op jit(solution)/shard_map/ppermute | solution.py:564
  58.4 5.7 %collective-permute-start.3 = (bf16[192,128]{1,0:T(8,128)(2,1)S(1)}, bf16[192,128]{1,0:T(8,128)(2,1)S(1)}, u32[]{:S(2)}, u32[]{:S(2)}) collective-permute-start(bf16[192,128]{1,0:T(8,128)(2,1)S(1)} %get-tuple-element.32), channel_id=1, source_target_pairs={{4,0},{8,4},{12,8},{16,12},{20,16},{24,20},{28,24},{32,28},{36,32}... | collective-permute-start | bytes 147464 | tf_op jit(solution)/shard_map/ppermute | solution.py:563

commit v4 on v2

v4 whole, which is shorter than its diff:
```python
import math

import jax
import jax.numpy as jnp
from jax import lax
from jax.experimental import pallas as pl
from jax.experimental.pallas import tpu as pltpu
from jax.sharding import PartitionSpec as P

F32 = jnp.float32
BF16 = jnp.bfloat16
HALO = 8
LEAF_DEV = 16
RANK = 32
NEAR = 12
VEC = 16
DEVICES = 128
CHUNKS = 8
LOW = (0, 16, 24, 28, 30)
NODES = (16, 8, 4, 2)
TOP_XFER = (0, 128, 192, 224, 240, 248)
TOP_COUPLE = (0, 0, 64, 96, 112, 120)
SCALE = 4.0 * math.log2(math.e)
SOFT = 0.01 * SCALE * SCALE
LOG_GAIN = math.log2(4.0 / math.sqrt(64 * NEAR))
VMEM_LIMIT = 48 * 1024 * 1024


def nn(a, b):
    return lax.dot_general(a, b, (((1,), (0,)), ((), ())), preferred_element_type=F32)


def nt(a, b):
    return lax.dot_general(a, b, (((1,), (1,)), ((), ())), preferred_element_type=F32)


def tn(a, b):
    return lax.dot_general(a, b, (((0,), (0,)), ((), ())), preferred_element_type=F32)


def halves(x):
    high = x.astype(BF16)
    return high, (x - high.astype(F32)).astype(BF16)


def lanes_in(rows, lo, size, dtype):
    lane = lax.broadcasted_iota(jnp.int32, (rows, 128), 1)
    return ((lane >= lo) & (lane < lo + size)).astype(F32).astype(dtype)


class Masks:
    def __init__(self):
        self.group = [lanes_in(16, 32 * g, 32, BF16) for g in range(4)]
        self.groupf = [lanes_in(16, 32 * g, 32, F32) for g in range(4)]
        self.half = [lanes_in(16, 64 * g, 64, BF16) for g in range(2)]
        self.halff = [lanes_in(16, 64 * g, 64, F32) for g in range(2)]


def repeat_matrix():
    row = lax.broadcasted_iota(jnp.int32, (128, 128), 0)
    col = lax.broadcasted_iota(jnp.int32, (128, 128), 1)
    return ((row & 31) == (col & 31)).astype(F32).astype(BF16)


def spread_rows(table, nodes):
    row = lax.broadcasted_iota(jnp.int32, (8, 128), 0)
    lane = lax.broadcasted_iota(jnp.int32, (8, 128), 1)
    mine = ((row & 3) == (lane >> 5)).astype(F32)
    parts = []
    for node in nodes:
        for j in range(4):
            one = table[node : node + 1, 256 * j : 256 * j + 128]
            two = table[node : node + 1, 256 * j + 128 : 256 * j + 256]
            parts.append(jnp.where(row < 4, one, two) * mine)
    return jnp.concatenate(parts, axis=0).astype(BF16)


def spread_table(table, out, first=0):
    table = table.astype(F32)
    repeat = repeat_matrix()
    count = table.shape[0]
    for n in range(0, count, 4):
        wide = nn(spread_rows(table, range(n, min(n + 4, count))), repeat)
        at = (first + n) * 32
        out[at : at + wide.shape[0], :] = wide.astype(out.dtype)


def spread_couple(couple, out):
    tables = [couple[k].astype(F32) for k in range(3)]
    row = lax.broadcasted_iota(jnp.int32, (384, 128), 0)
    col = lax.broadcasted_iota(jnp.int32, (384, 128), 1)
    fold = (((row & 31) == (col & 31)) & ((row >> 7) == (col >> 5))).astype(F32).astype(BF16)
    for n in range(0, 31, 4):
        nodes = range(n, min(n + 4, 31))
        wide = nn(jnp.concatenate([spread_rows(table, nodes) for table in tables], axis=1), fold)
        out[32 * n : 32 * n + wide.shape[0], :] = wide.astype(BF16)
    out[992:1024, :] = jnp.zeros((32, 128), BF16)


def up_pass(signal, basis, xfer, m):
    nodes = []
    for c in range(CHUNKS):
        wide = jnp.concatenate([basis[:, 128 * c : 128 * c + 128]] * 4, axis=0)
        both = nt(jnp.concatenate([signal[c] * m.half[0], signal[c] * m.half[1]], axis=0), wide)
        nodes += [both[:16], both[16:]]
    heights = []
    for h in range(4):
        split = [halves(node) for node in nodes]
        heights.append(split)
        nodes = []
        for t in range(0, NODES[h], 4):
            family = split[t : t + 4]
            left = [
                family[i][part] * m.group[i] + family[i + 1][part] * m.group[i + 1]
                for part in range(2)
                for i in range(0, len(family), 2)
            ]
            first = (LOW[h] + t) * 32
            both = nn(jnp.concatenate(left, axis=0), xfer[first : first + 128, :])
            size = 8 * len(family)
            both = both[:size] + both[size:]
            nodes += [both[i : i + 16] for i in range(0, size, 16)]
    return heights, nodes[0]


def exchange_rows(place, to_left, to_right, near, far, first):
    even = (place & 1) == 0
    for i, (one, two) in enumerate(zip(to_left, to_right, strict=True)):
        at = first + 16 * i
        near[at : at + 16, :] = jnp.where(even, two, one)
        far[at : at + 16, :] = jnp.where(even, one, two)


def sides(place, near, far, left, right):
    even = (place & 1) == 0
    for at in range(0, near.shape[0], 16):
        one, two = near[at : at + 16, :], far[at : at + 16, :]
        left[at : at + 16, :] = jnp.where(even, two, one)
        right[at : at + 16, :] = jnp.where(even, one, two)


def write_sends(place, signal, heights, root, weights, near, far, gather):
    exchange_rows(place, signal[:4], signal[4:], near, far, 0)
    to_left = [heights[h][i][part] for h in range(4) for i in (0, 1) for part in range(2)]
    to_right = [heights[h][i][part] for h in range(4) for i in (-2, -1) for part in range(2)]
    exchange_rows(place, to_left, to_right, near, far, 64)
    both = nn(jnp.concatenate([part[:, 0:64] for part in halves(root)], axis=0), weights[...])
    both = both[:16] + both[16:]
    row = lax.broadcasted_iota(jnp.int32, (16, 128), 0)
    mine = ((row >> 2) == (lax.broadcasted_iota(jnp.int32, (16, 128), 1) >> 5)).astype(F32)
    packed = []
    for level in range(6):
        one = both[:, 128 * level : 128 * level + 128] * mine
        one = one[0:8] + one[8:16]
        packed.append(one[0:4] + one[4:8])
    packed = jnp.concatenate(packed, axis=0)
    packed = jnp.concatenate([packed] * 3 + [jnp.zeros((56, 128), F32)], axis=0).astype(BF16)
    gather[...] = nn(relation(place), packed).astype(BF16)


def couple_low(heights, from_left, from_right, table, m):
    result = []
    for h in range(4):
        count = NODES[h]

        def node(n, part, h=h, count=count):
            if n < 0:
                at = 64 + (4 * h + 2 * (n + 2) + part) * 16
                return from_left[at : at + 16, :]
            if n >= count:
                at = 64 + (4 * h + 2 * (n - count) + part) * 16
                return from_right[at : at + 16, :]
            return heights[h][n][part]

        chunks = []
        for t in range(0, count, 4):
            targets = range(t, min(t + 4, count))
            left = []
            for part in range(2):
                for j in targets:
                    third = j + 3 if j % 2 == 0 else j - 3
                    slots = (node(j - 2, part), node(j + 2, part), node(third, part))
                    left.append(slots[0] * m.group[0] + slots[1] * m.group[1] + slots[2] * m.group[2])
            first = (LOW[h] + t) * 32
            wide = nt(jnp.concatenate(left, axis=0), table[first : first + 128, :])
            wide = wide[: 16 * len(targets)] + wide[16 * len(targets) :]
            chunk = wide[0:16] * m.groupf[0]
            for j in range(1, len(targets)):
                chunk = chunk + wide[16 * j : 16 * j + 16] * m.groupf[j]
            chunks.append(chunk)
        result.append(chunks)
    return result


def top_apply(place, gathered, top):
    sums = tn(relation(place), gathered[...])
    row = lax.broadcasted_iota(jnp.int32, (16, 128), 0)
    mine = ((row >> 2) == (lax.broadcasted_iota(jnp.int32, (16, 128), 1) >> 5)).astype(F32)
    left = [jnp.concatenate([sums[4 * i : 4 * i + 4]] * 4, axis=0) * mine for i in range(18)]
    left = halves(jnp.concatenate(left, axis=1))
    total = nt(jnp.concatenate(left, axis=0), top[...])
    total = jnp.concatenate([total[:16] + total[16:], jnp.zeros((16, 64), F32)], axis=1)
    total = total + pltpu.roll(total, 64, 1)
    return total + pltpu.roll(total, 32, 1)


def down_pass(root, couplings, xfer, m):
    high, low = halves(root)
    first = LOW[3] * 32
    both = nt(jnp.concatenate([high * m.group[0], low * m.group[0]], axis=0), xfer[first : first + 128, :])
    down = [couplings[3][0] + both[:16] + both[16:]]
    for h in (2, 1, 0):
        first = LOW[h] * 32
        split = [halves(d) for d in down]
        down = []
        for t in range(NODES[h] // 4):
            high, low = split[t // 2]
            g = (2 * t) % 4
            left = [high * m.group[g], high * m.group[g + 1], low * m.group[g], low * m.group[g + 1]]
            both = nt(jnp.concatenate(left, axis=0), xfer[first + 128 * t : first + 128 * t + 128, :])
            both = both[:32] + both[32:]
            down.append(couplings[h][t] + both[:16] * m.halff[0] + both[16:] * m.halff[1])
    return down


def one_hot(wanted, count):
    col = lax.broadcasted_iota(jnp.int32, wanted.shape, 1)
    return (col == wanted).astype(F32).astype(BF16)


def pick_rows(table, level_rows):
    count = table.shape[0]
    row = lax.broadcasted_iota(jnp.int32, (8, count), 0)
    col = lax.broadcasted_iota(jnp.int32, (8, count), 1)
    wanted = jnp.zeros((8, count), jnp.int32) - 1
    for level, at in level_rows.items():
        wanted = jnp.where(row == level, at, wanted)
    return nn((col == wanted).astype(F32).astype(BF16), table)


def build_paths(place, xfer_top, wide_path, paths, weights):
    rows = pick_rows(xfer_top[...], {level: TOP_XFER[level] + (place >> level) for level in range(5)})
    spread_table(rows[0:5], wide_path)
    row = lax.broadcasted_iota(jnp.int32, (32, 128), 0)
    lane = lax.broadcasted_iota(jnp.int32, (32, 128), 1)
    step = [wide_path[32 * level : 32 * level + 32, :] for level in range(5)]

    def times(left, right):
        both = nn(jnp.concatenate([part[:, 0:32] for part in halves(left)], axis=0), right)
        return both[:32] + both[32:]

    pair = halves(nn(step[2][:, 0:32], step[3]))
    second = nn(step[0][:, 0:32], step[1])
    fourth = times(second, jnp.concatenate(pair, axis=1))
    fourth = fourth[:, :128] + fourth[:, 128:]
    products = [(row == (lane & 31)).astype(F32), step[0].astype(F32), second, times(second, step[2]), fourth]
    products.append(times(fourth, step[4]))
    for level in range(6):
        paths[32 * level : 32 * level + 32, :] = products[level]
        high, low = halves(products[level])
        weights[0:32, 128 * level : 128 * level + 128] = high
        weights[32:64, 128 * level : 128 * level + 128] = low


def build_top(place, couple, couple_top, paths, wide_couple, top):
    at = {level: TOP_COUPLE[level] + (place >> level) for level in range(1, 6)}
    for k in range(3):
        rows = pick_rows(couple_top[k], at) + pick_rows(couple[k], {0: LOW[4]})
        spread_table(rows[0:6], wide_couple, 6 * k)
    for level in range(6):
        high, low = halves(paths[32 * level : 32 * level + 32, :])
        left = jnp.concatenate([high[:, 0:32], low[:, 0:32]], axis=0)
        right = [wide_couple[(6 * k + level) * 32 : (6 * k + level + 1) * 32, :] for k in range(3)]
        both = nn(left, jnp.concatenate(right, axis=1))
        high, low = halves(both[:32] + both[32:])
        for k in range(3):
            at = (6 * k + level) * 128
            top[0:32, at : at + 128] = high[:, 128 * k : 128 * k + 128]
            top[32:64, at : at + 128] = low[:, 128 * k : 128 * k + 128]


def relation(place):
    lane = lax.broadcasted_iota(jnp.int32, (1, 128), 1)
    k = (lane >= 24).astype(jnp.int32) + (lane >= 48).astype(jnp.int32) + (lane >= 72).astype(jnp.int32)
    level = (lane - 24 * k) >> 2
    node = place >> level
    third = jnp.where((node & 1) == 0, node + 3, node - 3)
    slot = jnp.where(k == 0, node - 2, jnp.where(k == 1, node + 2, jnp.where(k == 2, third, -1)))
    row = lax.broadcasted_iota(jnp.int32, (4 * DEVICES, 128), 0)
    match = (((row >> 2) >> level) == slot) & ((row & 3) == (lane & 3))
    return match.astype(F32).astype(BF16)


def point_parts(points):
    high = points.astype(BF16).astype(F32)
    rest = points - high
    mid = rest.astype(BF16).astype(F32)
    low = rest - mid
    return jnp.concatenate([high, mid, low, jnp.zeros((7, points.shape[1]), F32)], axis=0).astype(BF16)


def build_tiles(place, parts, cols, counts, from_left, from_right, near_left, near_right, tiles):
    half = lanes_in(8, 0, 64, F32)
    other = 1.0 - half
    blocks = [from_left[320 + 16 * c : 336 + 16 * c, :] for c in range(4)]
    blocks += [parts[:, 128 * c : 128 * c + 128] for c in range(CHUNKS)]
    blocks += [from_right[320 + 16 * c : 336 + 16 * c, :] for c in range(4)]
    row = lax.broadcasted_iota(jnp.int32, (8, 16), 0)
    col = lax.broadcasted_iota(jnp.int32, (8, 16), 1)
    adder = ((col % 3 == row) & (col < 9) & (row < 3)).astype(F32).astype(BF16)
    for c in range(16):
        joined = nn(adder, blocks[c]) * SCALE
        turned = pltpu.roll(joined, 64, 1)
        near_left[2 * c] = joined * half
        near_right[2 * c + 1] = joined * other
        near_left[2 * c + 1] = turned * half
        near_right[2 * c] = turned * other
    row = lax.broadcasted_iota(jnp.int32, (16, 384), 0)
    col = lax.broadcasted_iota(jnp.int32, (16, 384), 1)
    column = ((row % 3 == (col >> 7)) & (row < 9)).astype(F32).astype(BF16)
    lane = lax.broadcasted_iota(jnp.int32, (1, 128), 1)
    base = place * LEAF_DEV - HALO
    for c in range(CHUNKS):
        targets = tn(parts[:, 128 * c : 128 * c + 128], column) * SCALE
        for e in range(2):
            leaf = 2 * c + e
            count = counts[leaf]
            mine = [targets[64 * e : 64 * e + 64, 128 * x : 128 * x + 128] for x in range(3)]
            for pair in range(NEAR // 2):
                first = cols[2 * pair, leaf] - base
                second = cols[2 * pair + 1, leaf] - base
                source = near_left[first] + near_right[second]
                squares = SOFT
                for x in range(3):
                    gap = mine[x] - source[x : x + 1, :]
                    squares = squares + gap * gap
                slot = jnp.where(lane < 64, 2 * pair, 2 * pair + 1)
                gain = jnp.where(slot < count, LOG_GAIN, -2000.0)
                value = jnp.exp2(gain - squares * lax.rsqrt(squares))
                tiles[64 * leaf : 64 * leaf + 64, 128 * pair : 128 * pair + 128] = value.astype(BF16)


def near_field(place, signal, from_left, from_right, cols, tiles, near_left, near_right, m):
    chunks = [from_left[16 * c : 16 * c + 16, :] for c in range(4)]
    chunks += signal
    chunks += [from_right[16 * c : 16 * c + 16, :] for c in range(4)]
    for c in range(16):
        turned = pltpu.roll(chunks[c].astype(F32), 64, 1).astype(BF16)
        near_left[2 * c] = chunks[c] * m.half[0]
        near_right[2 * c + 1] = chunks[c] * m.half[1]
        near_left[2 * c + 1] = turned * m.half[0]
        near_right[2 * c] = turned * m.half[1]
    base = place * LEAF_DEV - HALO
    result = []
    for c in range(CHUNKS):
        rows = []
        for leaf in (2 * c, 2 * c + 1):
            parts = []
            for pair in range(NEAR // 2):
                first = cols[2 * pair, leaf] - base
                second = cols[2 * pair + 1, leaf] - base
                parts.append(near_left[first] + near_right[second])
            rows.append(jnp.concatenate(parts, axis=1))
        both = nt(jnp.concatenate(rows, axis=0), tiles[128 * c : 128 * c + 128, :])
        result.append(both[:16] * m.halff[0] + both[16:] * m.halff[1])
    return result


def far_field(down, basis, near, m):
    result = []
    split = [halves(d) for d in down]
    for c in range(CHUNKS):
        high, low = split[c // 2]
        g = (2 * c) % 4
        left = [high * m.group[g], high * m.group[g + 1], low * m.group[g], low * m.group[g + 1]]
        wide = jnp.concatenate([basis[:, 128 * c : 128 * c + 128]] * 4, axis=0)
        far = nn(jnp.concatenate(left, axis=0), wide)
        far = far[:32] + far[32:]
        far = far[:16] * m.halff[0] + far[16:] * m.halff[1]
        result.append((near[:, 128 * c : 128 * c + 128] + far).astype(BF16))
    return result


def store_heights(heights, out):
    at = 0
    for nodes in heights:
        for node in nodes:
            for part in node:
                out[at : at + 16, :] = part
                at += 16


def load_heights(source):
    heights, at = [], 0
    for count in NODES:
        heights.append([(source[b : b + 16, :], source[b + 16 : b + 32, :]) for b in range(at, at + 32 * count, 32)])
        at += 32 * count
    return heights


def store_local(near, couplings, near_out, couplings_out):
    for c in range(CHUNKS):
        near_out[:, 128 * c : 128 * c + 128] = near[c]
    at = 0
    for chunks in couplings:
        for chunk in chunks:
            couplings_out[at : at + 16, :] = chunk
            at += 16


def load_couplings(source):
    couplings, at = [], 0
    for count in (4, 2, 1, 1):
        couplings.append([source[b : b + 16, :] for b in range(at, at + 16 * count, 16)])
        at += 16 * count
    return couplings


def chunks_of(signal):
    return [signal[:, 128 * c : 128 * c + 128] for c in range(CHUNKS)]


def fetch(sources, targets, sems):
    copies = [pltpu.make_async_copy(s, t, sems.at[i]) for i, (s, t) in enumerate(zip(sources, targets, strict=True))]
    for copy in copies:
        copy.start()
    return copies


def first_kernel(
    vectors_hbm, points_hbm, basis_hbm, xfer_hbm, xfer_top_hbm, near, far, gather, heights_out, xfer_out, paths, weights,
    vectors, points, basis, xfer_low, xfer_top, wide_path, sems,
):
    copies = fetch(
        (xfer_top_hbm, xfer_hbm, vectors_hbm, basis_hbm, points_hbm), (xfer_top, xfer_low, vectors, basis, points), sems
    )
    place = lax.axis_index("leaf")
    m = Masks()
    xfer_out[960:1024, :] = jnp.zeros((64, 128), BF16)
    copies[1].wait()
    spread_table(xfer_low[...], xfer_out)
    copies[0].wait()
    copies[2].wait()
    copies[3].wait()
    signal = chunks_of(vectors)
    build_paths(place, xfer_top, wide_path, paths, weights)
    heights, root = up_pass(signal, basis, xfer_out, m)
    write_sends(place, signal, heights, root, weights, near, far, gather)
    store_heights(heights, heights_out)
    copies[4].wait()
    parts = chunks_of(point_parts(points[...]))
    exchange_rows(place, parts[:4], parts[4:], near, far, 320)


def table_kernel(
    couple_top_hbm, couple_hbm, paths, top, couple_wide, couple_top, couple, wide_couple, sems
):
    copies = fetch((couple_hbm, couple_top_hbm), (couple, couple_top), sems)
    copies[0].wait()
    spread_couple(couple, couple_wide)
    copies[1].wait()
    build_top(lax.axis_index("leaf"), couple, couple_top, paths, wide_couple, top)


def local_first_kernel(
    cols_hbm, counts_hbm, vectors_hbm, points_hbm, couple_wide, near, far, heights_in,
    tiles, near_out, couplings_out,
    cols, counts, vectors, points, from_left, from_right, places_left, places_right, near_left, near_right, sems,
):
    copies = fetch((cols_hbm, counts_hbm, vectors_hbm, points_hbm), (cols, counts, vectors, points), sems)
    m = Masks()
    place = lax.axis_index("leaf")
    sides(place, near, far, from_left, from_right)
    for copy in copies:
        copy.wait()
    build_tiles(
        place, point_parts(points[...]), cols, counts, from_left, from_right, places_left, places_right, tiles
    )
    couplings = couple_low(load_heights(heights_in), from_left, from_right, couple_wide, m)
    near = near_field(place, chunks_of(vectors), from_left, from_right, cols, tiles, near_left, near_right, m)
    store_local(near, couplings, near_out, couplings_out)


def spread_kernel(couple_hbm, basis_hbm, vectors, xfer, couple_wide, heights_out, couple, basis, sems):
    copies = fetch((couple_hbm, basis_hbm), (couple, basis), sems)
    m = Masks()
    copies[0].wait()
    copies[1].wait()
    spread_couple(couple, couple_wide)
    store_heights(up_pass(chunks_of(vectors), basis, xfer, m)[0], heights_out)


def local_next_kernel(
    cols_hbm, couple_wide, vectors, tiles, near, far, heights_in, near_out, couplings_out,
    cols, from_left, from_right, near_left, near_right, sems,
):
    copies = fetch((cols_hbm,), (cols,), sems)
    m = Masks()
    place = lax.axis_index("leaf")
    sides(place, near, far, from_left, from_right)
    couplings = couple_low(load_heights(heights_in), from_left, from_right, couple_wide, m)
    copies[0].wait()
    near = near_field(place, chunks_of(vectors), from_left, from_right, cols, tiles, near_left, near_right, m)
    store_local(near, couplings, near_out, couplings_out)


def down_up_kernel(
    basis_hbm, gathered, top, xfer, near, couplings, weights, near_pack, far_pack, gather, signal_out, basis, sems
):
    copies = fetch((basis_hbm,), (basis,), sems)
    m = Masks()
    place = lax.axis_index("leaf")
    down = down_pass(top_apply(place, gathered, top), load_couplings(couplings), xfer, m)
    copies[0].wait()
    signal = far_field(down, basis, near, m)
    for c in range(CHUNKS):
        signal_out[:, 128 * c : 128 * c + 128] = signal[c]
    heights, root = up_pass(signal, basis, xfer, m)
    write_sends(place, signal, heights, root, weights, near_pack, far_pack, gather)


def down_last_kernel(basis_hbm, gathered, top, xfer, near, couplings, out, basis, sems):
    copies = fetch((basis_hbm,), (basis,), sems)
    m = Masks()
    place = lax.axis_index("leaf")
    down = down_pass(top_apply(place, gathered, top), load_couplings(couplings), xfer, m)
    copies[0].wait()
    signal = far_field(down, basis, near, m)
    for c in range(CHUNKS):
        out[:, 128 * c : 128 * c + 128] = signal[c]


def call(kernel, name, arguments, arrays, outputs, scratch, flops, pinned=False):
    if pinned:
        arguments = [pltpu.with_memory_space_constraint(a, pltpu.HBM) for a in arguments]
    inputs = tuple(arguments) + tuple(arrays)
    in_specs = [pl.BlockSpec(memory_space=pltpu.HBM)] * len(arguments)
    in_specs += [pl.BlockSpec(memory_space=pltpu.VMEM)] * len(arrays)
    return pl.pallas_call(
        kernel,
        out_shape=[jax.ShapeDtypeStruct(shape, dtype) for shape, dtype in outputs],
        in_specs=in_specs,
        out_specs=[pl.BlockSpec(memory_space=pltpu.VMEM)] * len(outputs),
        scratch_shapes=scratch,
        compiler_params=pltpu.CompilerParams(vmem_limit_bytes=VMEM_LIMIT),
        cost_estimate=pl.CostEstimate(flops=flops, bytes_accessed=1 << 20, transcendentals=0),
        name=name,
    )(*inputs)


def exchange(near, far, gather):
    count = lax.axis_size("leaf")
    blocks = gather.reshape(count, 4, 128)
    gathered = lax.all_to_all(blocks, "leaf", 0, 0, tiled=True)
    near = lax.ppermute(near, "leaf", [(i, i ^ 1) for i in range(count)])
    far = lax.ppermute(far, "leaf", [(i, ((i + 1) ^ 1) - 1) for i in range(1, count - 1)])
    return near, far, gathered.reshape(count * 4, 128)


def body(vectors, points, near_cols, near_count, basis, xfer_low, couple, xfer_top, couple_top):
    vm, sm = pltpu.VMEM, pltpu.SMEM
    sems = pltpu.SemaphoreType.DMA
    signal_buf, basis_buf, points_buf = vm((16, 1024), BF16), vm((32, 1024), BF16), vm((3, 1024), F32)
    couple_buf = vm((3, 31, 1024), BF16)
    blocks = [vm((32, 16, 128), BF16)] * 2
    sends = [((512, 128), BF16), ((960, 128), BF16)]
    local = [((16, 1024), F32), ((128, 128), F32)]
    near, far, gather, heights, xfer, paths, weights = call(
        first_kernel, "up_first", (vectors, points, basis, xfer_low, xfer_top), (),
        [((384, 128), BF16)] * 2 + sends + [((1024, 128), BF16), ((192, 128), F32), ((64, 768), BF16)],
        [signal_buf, points_buf, basis_buf, vm((30, 1024), BF16), vm((254, 1024), BF16), vm((160, 128), BF16), sems((5,))],
        1 << 20, True,
    )
    near, far, gathered = exchange(near, far, gather)
    top, couple_wide = call(
        table_kernel, "tables", (couple_top, couple), (paths,), [((64, 2304), BF16), ((1024, 128), BF16)],
        [vm((3, 124, 1024), BF16), couple_buf, vm((576, 128), BF16), sems((2,))], 1 << 32, True,
    )
    tiles, near, couplings = call(
        local_first_kernel, "local_first", (near_cols, near_count, vectors, points),
        (couple_wide, near, far, heights), [((1024, 768), BF16)] + local,
        [sm((12, 16), jnp.int32), sm((16,), jnp.int32), signal_buf, points_buf] + [vm((384, 128), BF16)] * 2
        + [vm((32, 8, 128), F32)] * 2 + blocks + [sems((4,))], 1 << 32,
    )
    near, far, gather, signal = call(
        down_up_kernel, "down_up", (basis,), (gathered, top, xfer, near, couplings, weights),
        [((320, 128), BF16)] * 2 + [sends[0], ((16, 1024), BF16)], [basis_buf, sems((1,))], 1 << 20,
    )
    near, far, gathered = exchange(near, far, gather)
    couple_wide, heights = call(
        spread_kernel, "spread", (couple, basis), (signal, xfer), [((1024, 128), BF16), sends[1]],
        [couple_buf, basis_buf, sems((2,))], 1 << 32,
    )
    near, couplings = call(
        local_next_kernel, "local_next", (near_cols,), (couple_wide, signal, tiles, near, far, heights), local,
        [sm((12, 16), jnp.int32)] + [vm((320, 128), BF16)] * 2 + blocks + [sems((1,))], 1 << 32,
    )
    (result,) = call(
        down_last_kernel, "down_last", (basis,), (gathered, top, xfer, near, couplings), [((16, 1024), BF16)],
        [basis_buf, sems((1,))], 1 << 20,
    )
    return result


def solution(mesh):
    placed = (
        P("vec", "leaf"),
        P(None, "leaf"),
        P(None, "leaf"),
        P("leaf"),
        P(None, "leaf"),
        P("leaf", None),
        P(None, "leaf", None),
        P(),
        P(),
    )
    return jax.shard_map(body, mesh=mesh, in_specs=placed, out_specs=P("vec", "leaf"), check_vma=False)
```

time: 81.6 us -> 66.8 us (0.82)
  Pallas kernels: 24.7 us -> 17.2 us
  waiting for transfers between devices: 10.1 us -> 5.79 us
  starting transfers between devices: 45.9 us -> 43.3 us
    pallas_call x6 -> x7, Pallas kernels: 24.7 us -> 17.2 us  [call(): pl.pallas_call(kernel, out_shape=[jax.ShapeDtypeStruct(shape, dtype) for...]
    all_to_all x2, waiting for transfers between devices: 10.1 us -> 2.83 us  [exchange(): gathered = lax.all_to_all(blocks, 'leaf', 0, 0, tiled=True)]
    ppermute x4, waiting for transfers between devices: 0.01 us -> 2.96 us  [the longest x2 2.95 us: exchange(): lax.ppermute(far, 'leaf', [(i, (i + 1 ^ 1) - 1) for i in range(1, count -...]
    all_to_all x2, starting transfers between devices: 34.7 us -> 32.1 us  [exchange(): gathered = lax.all_to_all(blocks, 'leaf', 0, 0, tiled=True)]
  transfers between devices with their start and end apart: 6 -> 6, of which waited for: 1 -> 4; matrix products, arithmetic and copies ran while one was open for 0% -> 0% of each run, Pallas kernels for 20% -> 12%
where the time goes in v4:
time: 66.8 us; the launch traced here: 66.4 us
  starting transfers between devices  43.3 us (65%)
  Pallas kernels  17.2 us (26%)
  waiting for transfers between devices  5.79 us (9%)
    all_to_all x2, starting transfers between devices, exchange(): gathered = lax.all_to_all(blocks, 'leaf', 0, 0, tiled=True)  32.1 us
    pallas_call x7, Pallas kernels, call(): pl.pallas_call(kernel, out_shape=[jax.ShapeDtypeStruct(shape, dtype) for...  17.2 us
    ppermute x2, starting transfers between devices, exchange(): near = lax.ppermute(near, 'leaf', [(i, i ^ 1) for i in range(count)])  5.6 us
    ppermute x2, starting transfers between devices, exchange(): lax.ppermute(far, 'leaf', [(i, (i + 1 ^ 1) - 1) for i in range(1, count -...  5.59 us
    ppermute x2, waiting for transfers between devices, exchange(): lax.ppermute(far, 'leaf', [(i, (i + 1 ^ 1) - 1) for i in range(1, count -...  2.95 us
    all_to_all x2, waiting for transfers between devices, exchange(): gathered = lax.all_to_all(blocks, 'leaf', 0, 0, tiled=True)  2.83 us
  transfers between devices with their start and end apart: 6, of which 4 were waited for; matrix products, arithmetic and copies ran while one was open for 0% of the time, Pallas kernels for 12%

profile of v4, /device:TPU:1, one launch (start us, length us, event | category | flops | bytes accessed | tf_op | source)
XLA Modules:
  0.0 66.4 jit_solution(4711412923901231110)
XLA Ops:
  0.0 3.6 %up_first.1 = (bf16[384,128]{1,0:T(8,128)(2,1)S(1)}, bf16[384,128]{1,0:T(8,128)(2,1)S(1)}, bf16[512,128]{1,0:T(8,128)(2,1)}, bf16[960,128]{1,0:T(8,128)(2,1)S(1)...) custom-call(bf16[16,1024]{1,0:T(8,128)(2,1)} %vectors_hbm.3, ...), custom_call_target="tpu_custom_call" | custom-call | flops 1048576 | bytes 1048576 | tf_op jit(solution)/shard_map/up_first/pallas_call | solution.py:539
  3.7 18.4 %all-to-all-start = ((bf16[128,4,128]{2,1,0:T(4,128)(2,1)}), bf16[128,4,128]{2,1,0:T(4,128)(2,1)S(1)}, u32[]{:S(2)}, u32[]{:S(2)}) async-start(bf16[128,4,128]{2,1,0:T(4,128)(2,1)} %bitcast), calls=%async_computation | async-start | bytes 262144 | tf_op jit(solution)/shard_map/all_to_all | solution.py:554
  22.1 2.8 %collective-permute-start = (bf16[384,128]{1,0:T(8,128)(2,1)S(1)}, bf16[384,128]{1,0:T(8,128)(2,1)S(1)}, u32[]{:S(2)}, u32[]{:S(2)}) collective-permute-start(bf16[384,128]{1,0:T(8,128)(2,1)S(1)} %get-tuple-element.30), channel_id=1, source_target_pairs={{0,4},{4,0},{8,12},{12,8},{16,20},{20,16},{24,28},{28,24},{32,36},... | collective-permute-start | bytes 294920 | tf_op jit(solution)/shard_map/ppermute | solution.py:555
  24.9 2.8 %collective-permute-start.1 = (bf16[384,128]{1,0:T(8,128)(2,1)S(1)}, bf16[384,128]{1,0:T(8,128)(2,1)S(1)}, u32[]{:S(2)}, u32[]{:S(2)}) collective-permute-start(bf16[384,128]{1,0:T(8,128)(2,1)S(1)} %get-tuple-element.31), channel_id=1, source_target_pairs={{4,8},{8,4},{12,16},{16,12},{20,24},{24,20},{28,32},{32,28},{36,40... | collective-permute-start | bytes 294920 | tf_op jit(solution)/shard_map/ppermute | solution.py:556
  27.7 0.0 copy-start.1
  27.7 0.0 copy-start.2
  27.7 0.0 copy-start.4
  27.7 0.0 copy-start.5
  27.8 2.3 %tables.1 = (bf16[64,2304]{1,0:T(8,128)(2,1)S(1)}, bf16[1024,128]{1,0:T(8,128)(2,1)S(1)}) custom-call(bf16[3,124,1024]{2,1,0:T(8,128)(2,1)} %couple_top_hbm.1, bf16[3,31,1024]{2,1,0:T(8,128)(2,1)} %couple_hbm.3, f32[192,128]{1,0:T(8,128)S(1)} %get-tuple-element.26.paths), custom_call_target="tpu_custom_call" | custom-call | flops 4294967296 | bytes 1048576 | tf_op jit(solution)/shard_map/tables/pallas_call | solution.py:539
  30.1 0.0 collective-permute-done.near
  30.1 1.0 %collective-permute-done.1.far = bf16[384,128]{1,0:T(8,128)(2,1)S(1)} collective-permute-done((bf16[384,128]{1,0:T(8,128)(2,1)S(1)}, bf16[384,128]{1,0:T(8,128)(2,1)S(1)}, u32[]{:S(2)}, u32[]{:S(2)}) %collective-permute-start.1) | collective-permute-done | bytes 98336 | tf_op jit(solution)/shard_map/ppermute | solution.py:556
  31.1 0.0 copy-done.1
  31.1 0.0 copy-done.2
  31.1 0.0 copy-done.4
  31.1 0.0 copy-done.5
  31.2 0.0 copy-start
  31.2 0.0 copy-start.3
  31.2 3.3 %local_first.1 = (bf16[1024,768]{1,0:T(8,128)(2,1)S(1)}, f32[16,1024]{1,0:T(8,128)S(1)}, f32[128,128]{1,0:T(8,128)S(1)}) custom-call(s32[12,16]{1,0:T(8,128)S(1)} %copy-done.4, s32[16]{0:T(128)S(1)} %copy-done.5, bf16[16,1024]{1,0:T(8,128)(2,1)S(1)} %copy-done.1, f32[3,1024]{1,0:T(4,128)S(1)} %copy-done.2, ...), custom_call_target="tpu_custom_call" | custom-call | flops 4294967296 | bytes 1048576 | tf_op jit(solution)/shard_map/local_first/pallas_call | solution.py:539
  34.5 0.3 all-to-all-done
  34.8 0.0 copy-done
  34.8 3.1 %down_up.1 = (bf16[320,128]{1,0:T(8,128)(2,1)S(1)}, bf16[320,128]{1,0:T(8,128)(2,1)S(1)}, bf16[512,128]{1,0:T(8,128)(2,1)}, bf16[16,1024]{1,0:T(8,128)(2,1)S(1)}) custom-call(bf16[32,1024]{1,0:T(8,128)(2,1)S(1)} %copy-done, bf16[512,128]{1,0:T(8,128)(2,1)S(1)} %bitcast.4, bf16[64,2304]{1,0:T(8,128)(2,1)S(1)} %get-tuple-element.27.top, ...), custom_call_target="tpu_custom_call" | custom-call | flops 1048576 | bytes 1048576 | tf_op jit(solution)/shard_map/down_up/pallas_call | solution.py:539
  38.0 13.6 %all-to-all-start.1 = ((bf16[128,4,128]{2,1,0:T(4,128)(2,1)}), bf16[128,4,128]{2,1,0:T(4,128)(2,1)S(1)}, u32[]{:S(2)}, u32[]{:S(2)}) async-start(bf16[128,4,128]{2,1,0:T(4,128)(2,1)} %bitcast.2), calls=%async_computation.1 | async-start | bytes 262144 | tf_op jit(solution)/shard_map/all_to_all | solution.py:554
  51.6 2.8 %collective-permute-start.2 = (bf16[320,128]{1,0:T(8,128)(2,1)S(1)}, bf16[320,128]{1,0:T(8,128)(2,1)S(1)}, u32[]{:S(2)}, u32[]{:S(2)}) collective-permute-start(bf16[320,128]{1,0:T(8,128)(2,1)S(1)} %get-tuple-element.40), channel_id=1, source_target_pairs={{0,4},{4,0},{8,12},{12,8},{16,20},{20,16},{24,28},{28,24},{32,36},... | collective-permute-start | bytes 245768 | tf_op jit(solution)/shard_map/ppermute | solution.py:555
  54.4 2.8 %collective-permute-start.3 = (bf16[320,128]{1,0:T(8,128)(2,1)S(1)}, bf16[320,128]{1,0:T(8,128)(2,1)S(1)}, u32[]{:S(2)}, u32[]{:S(2)}) collective-permute-start(bf16[320,128]{1,0:T(8,128)(2,1)S(1)} %get-tuple-element.41), channel_id=1, source_target_pairs={{4,8},{8,4},{12,16},{16,12},{20,24},{24,20},{28,32},{32,28},{36,40... | collective-permute-start | bytes 245768 | tf_op jit(solution)/shard_map/ppermute | solution.py:556
  57.2 0.0 copy-done.3
  57.2 1.3 %spread.1 = (bf16[1024,128]{1,0:T(8,128)(2,1)S(1)}, bf16[960,128]{1,0:T(8,128)(2,1)S(1)}) custom-call(bf16[3,31,1024]{2,1,0:T(8,128)(2,1)S(1)} %copy-done.3, bf16[32,1024]{1,0:T(8,128)(2,1)S(1)} %copy-done, bf16[16,1024]{1,0:T(8,128)(2,1)S(1)} %get-tuple-element.37.vectors, bf16[1024,128]{1,0:T(8,128)(2,1)S(1)} %get-tuple-element.28.xfer), custom_call_target="tpu_custom_call" | custom-call | flops 4294967296 | bytes 1048576 | tf_op jit(solution)/shard_map/spread/pallas_call | solution.py:539
  58.6 0.0 collective-permute-done.2.near
  58.6 1.9 %collective-permute-done.3.far = bf16[320,128]{1,0:T(8,128)(2,1)S(1)} collective-permute-done((bf16[320,128]{1,0:T(8,128)(2,1)S(1)}, bf16[320,128]{1,0:T(8,128)(2,1)S(1)}, u32[]{:S(2)}, u32[]{:S(2)}) %collective-permute-start.3) | collective-permute-done | bytes 81952 | tf_op jit(solution)/shard_map/ppermute | solution.py:556
  60.5 1.3 %local_next.1 = (f32[16,1024]{1,0:T(8,128)S(1)}, f32[128,128]{1,0:T(8,128)S(1)}) custom-call(s32[12,16]{1,0:T(8,128)S(1)} %copy-done.4, bf16[1024,128]{1,0:T(8,128)(2,1)S(1)} %get-tuple-element.38.couple_wide, bf16[16,1024]{1,0:T(8,128)(2,1)S(1)} %get-tuple-element.37.vectors, bf16[1024,768]{1,0:T(8,128)(2,1)S(1)} %get-tuple-element.39.tiles, ...), custom_call_target="tpu_custom_call" | custom-call | flops 4294967296 | bytes 1048576 | tf_op jit(solution)/shard_map/local_next/pallas_call | solution.py:539
  61.8 2.5 %all-to-all-done.1 = bf16[128,4,128]{2,1,0:T(4,128)(2,1)S(1)} async-done(((bf16[128,4,128]{2,1,0:T(4,128)(2,1)}), bf16[128,4,128]{2,1,0:T(4,128)(2,1)S(1)}, u32[]{:S(2)}, u32[]{:S(2)}) %all-to-all-start.1) | async-done | bytes 131104 | tf_op jit(solution)/shard_map/all_to_all | solution.py:554
  64.3 2.1 %down_last.1 = bf16[16,1024]{1,0:T(8,128)(2,1)} custom-call(bf16[32,1024]{1,0:T(8,128)(2,1)S(1)} %copy-done, bf16[512,128]{1,0:T(8,128)(2,1)S(1)} %bitcast.5, bf16[64,2304]{1,0:T(8,128)(2,1)S(1)} %get-tuple-element.27.top, bf16[1024,128]{1,0:T(8,128)(2,1)S(1)} %get-tuple-element.28.xfer, f32[16,1024]{1,0:T(8,128)S(1)} %get-tuple-element.43.near, ...), custom_call_target="tpu_custom_call" | custom-call | flops 1048576 | bytes 1048576 | tf_op jit(solution)/shard_map/down_last/pallas_call | solution.py:539
Async XLA Ops:
  3.7 31.2 %all-to-all-start = ((bf16[128,4,128]{2,1,0:T(4,128)(2,1)}), bf16[128,4,128]{2,1,0:T(4,128)(2,1)S(1)}, u32[]{:S(2)}, u32[]{:S(2)}) async-start(bf16[128,4,128]{2,1,0:T(4,128)(2,1)} %bitcast), calls=%async_computation | async-start | bytes 262144 | tf_op jit(solution)/shard_map/all_to_all | solution.py:554
  22.1 8.0 %collective-permute-start = (bf16[384,128]{1,0:T(8,128)(2,1)S(1)}, bf16[384,128]{1,0:T(8,128)(2,1)S(1)}, u32[]{:S(2)}, u32[]{:S(2)}) collective-permute-start(bf16[384,128]{1,0:T(8,128)(2,1)S(1)} %get-tuple-element.30), channel_id=1, source_target_pairs={{0,4},{4,0},{8,12},{12,8},{16,20},{20,16},{24,28},{28,24},{32,36},... | collective-permute-start | bytes 294920 | tf_op jit(solution)/shard_map/ppermute | solution.py:555
  24.9 6.2 %collective-permute-start.1 = (bf16[384,128]{1,0:T(8,128)(2,1)S(1)}, bf16[384,128]{1,0:T(8,128)(2,1)S(1)}, u32[]{:S(2)}, u32[]{:S(2)}) collective-permute-start(bf16[384,128]{1,0:T(8,128)(2,1)S(1)} %get-tuple-element.31), channel_id=1, source_target_pairs={{4,8},{8,4},{12,16},{16,12},{20,24},{24,20},{28,32},{32,28},{36,40... | collective-permute-start | bytes 294920 | tf_op jit(solution)/shard_map/ppermute | solution.py:556
  27.7 3.4 %copy-start.1 = (bf16[16,1024]{1,0:T(8,128)(2,1)S(1)}, bf16[16,1024]{1,0:T(8,128)(2,1)}, u32[]{:S(2)}) copy-start(bf16[16,1024]{1,0:T(8,128)(2,1)} %vectors_hbm.3) | copy-start | bytes 98308
  27.7 3.4 %copy-start.2 = (f32[3,1024]{1,0:T(4,128)S(1)}, f32[3,1024]{1,0:T(4,128)}, u32[]{:S(2)}) copy-start(f32[3,1024]{1,0:T(4,128)} %points_hbm.3) | copy-start | bytes 36868
  27.7 3.4 %copy-start.4 = (s32[12,16]{1,0:T(8,128)S(1)}, s32[12,16]{1,0:T(8,128)}, u32[]{:S(2)}) copy-start(s32[12,16]{1,0:T(8,128)} %cols_hbm.3) | copy-start | bytes 2308
  27.7 3.4 %copy-start.5 = (s32[16]{0:T(128)S(1)}, s32[16]{0:T(128)}, u32[]{:S(2)}) copy-start(s32[16]{0:T(128)} %counts_hbm.1) | copy-start | bytes 196
  31.2 3.7 %copy-start = (bf16[32,1024]{1,0:T(8,128)(2,1)S(1)}, bf16[32,1024]{1,0:T(8,128)(2,1)}, u32[]{:S(2)}) copy-start(bf16[32,1024]{1,0:T(8,128)(2,1)} %basis_hbm.7) | copy-start | bytes 196612
  31.2 26.1 %copy-start.3 = (bf16[3,31,1024]{2,1,0:T(8,128)(2,1)S(1)}, bf16[3,31,1024]{2,1,0:T(8,128)(2,1)}, u32[]{:S(2)}) copy-start(bf16[3,31,1024]{2,1,0:T(8,128)(2,1)} %couple_hbm.3) | copy-start | bytes 571396
  38.0 26.4 %all-to-all-start.1 = ((bf16[128,4,128]{2,1,0:T(4,128)(2,1)}), bf16[128,4,128]{2,1,0:T(4,128)(2,1)S(1)}, u32[]{:S(2)}, u32[]{:S(2)}) async-start(bf16[128,4,128]{2,1,0:T(4,128)(2,1)} %bitcast.2), calls=%async_computation.1 | async-start | bytes 262144 | tf_op jit(solution)/shard_map/all_to_all | solution.py:554
  51.6 6.9 %collective-permute-start.2 = (bf16[320,128]{1,0:T(8,128)(2,1)S(1)}, bf16[320,128]{1,0:T(8,128)(2,1)S(1)}, u32[]{:S(2)}, u32[]{:S(2)}) collective-permute-start(bf16[320,128]{1,0:T(8,128)(2,1)S(1)} %get-tuple-element.40), channel_id=1, source_target_pairs={{0,4},{4,0},{8,12},{12,8},{16,20},{20,16},{24,28},{28,24},{32,36},... | collective-permute-start | bytes 245768 | tf_op jit(solution)/shard_map/ppermute | solution.py:555
  54.4 6.1 %collective-permute-start.3 = (bf16[320,128]{1,0:T(8,128)(2,1)S(1)}, bf16[320,128]{1,0:T(8,128)(2,1)S(1)}, u32[]{:S(2)}, u32[]{:S(2)}) collective-permute-start(bf16[320,128]{1,0:T(8,128)(2,1)S(1)} %get-tuple-element.41), channel_id=1, source_target_pairs={{4,8},{8,4},{12,16},{16,12},{20,24},{24,20},{28,32},{32,28},{36,40... | collective-permute-start | bytes 245768 | tf_op jit(solution)/shard_map/ppermute | solution.py:556

commit v5 on v4

--- a/solution.py
+++ b/solution.py
@@ -49,11 +49,12 @@
 
 
 class Masks:
-    def __init__(self):
-        self.group = [lanes_in(16, 32 * g, 32, BF16) for g in range(4)]
-        self.groupf = [lanes_in(16, 32 * g, 32, F32) for g in range(4)]
-        self.half = [lanes_in(16, 64 * g, 64, BF16) for g in range(2)]
-        self.halff = [lanes_in(16, 64 * g, 64, F32) for g in range(2)]
+    def __init__(self, rows=16):
+        self.rows = rows
+        self.group = [lanes_in(rows, 32 * g, 32, BF16) for g in range(4)]
+        self.groupf = [lanes_in(rows, 32 * g, 32, F32) for g in range(4)]
+        self.half = [lanes_in(rows, 64 * g, 64, BF16) for g in range(2)]
+        self.halff = [lanes_in(rows, 64 * g, 64, F32) for g in range(2)]
 
 
 def repeat_matrix():
@@ -139,11 +140,14 @@
         right[at : at + 16, :] = jnp.where(even, one, two)
 
 
-def write_sends(place, signal, heights, root, weights, near, far, gather):
+def write_halo(place, signal, heights, near, far):
     exchange_rows(place, signal[:4], signal[4:], near, far, 0)
     to_left = [heights[h][i][part] for h in range(4) for i in (0, 1) for part in range(2)]
     to_right = [heights[h][i][part] for h in range(4) for i in (-2, -1) for part in range(2)]
     exchange_rows(place, to_left, to_right, near, far, 64)
+
+
+def write_sends(place, root, weights, gather):
     both = nn(jnp.concatenate([part[:, 0:64] for part in halves(root)], axis=0), weights[...])
     both = both[:16] + both[16:]
     row = lax.broadcasted_iota(jnp.int32, (16, 128), 0)
@@ -199,16 +203,17 @@
     left = [jnp.concatenate([sums[4 * i : 4 * i + 4]] * 4, axis=0) * mine for i in range(18)]
     left = halves(jnp.concatenate(left, axis=1))
     total = nt(jnp.concatenate(left, axis=0), top[...])
-    total = jnp.concatenate([total[:16] + total[16:], jnp.zeros((16, 64), F32)], axis=1)
-    total = total + pltpu.roll(total, 64, 1)
-    return total + pltpu.roll(total, 32, 1)
+    return everywhere(total[:16] + total[16:])
 
 
 def down_pass(root, couplings, xfer, m):
-    high, low = halves(root)
-    first = LOW[3] * 32
-    both = nt(jnp.concatenate([high * m.group[0], low * m.group[0]], axis=0), xfer[first : first + 128, :])
-    down = [couplings[3][0] + both[:16] + both[16:]]
+    n = m.rows
+    down = [0.0] if couplings is None else couplings[3]
+    if root is not None:
+        high, low = halves(root)
+        first = LOW[3] * 32
+        both = nt(jnp.concatenate([high * m.group[0], low * m.group[0]], axis=0), xfer[first : first + 128, :])
+        down = [down[0] + both[:n] + both[n:]]
     for h in (2, 1, 0):
         first = LOW[h] * 32
         split = [halves(d) for d in down]
@@ -218,14 +223,10 @@
             g = (2 * t) % 4
             left = [high * m.group[g], high * m.group[g + 1], low * m.group[g], low * m.group[g + 1]]
             both = nt(jnp.concatenate(left, axis=0), xfer[first + 128 * t : first + 128 * t + 128, :])
-            both = both[:32] + both[32:]
-            down.append(couplings[h][t] + both[:16] * m.halff[0] + both[16:] * m.halff[1])
+            both = both[: 2 * n] + both[2 * n :]
+            both = both[:n] * m.halff[0] + both[n:] * m.halff[1]
+            down.append(both if couplings is None else couplings[h][t] + both)
     return down
-
-
-def one_hot(wanted, count):
-    col = lax.broadcasted_iota(jnp.int32, wanted.shape, 1)
-    return (col == wanted).astype(F32).astype(BF16)
 
 
 def pick_rows(table, level_rows):
@@ -366,7 +367,8 @@
     return result
 
 
-def far_field(down, basis, near, m):
+def far_field(down, basis, m):
+    n = m.rows
     result = []
     split = [halves(d) for d in down]
     for c in range(CHUNKS):
@@ -375,10 +377,30 @@
         left = [high * m.group[g], high * m.group[g + 1], low * m.group[g], low * m.group[g + 1]]
         wide = jnp.concatenate([basis[:, 128 * c : 128 * c + 128]] * 4, axis=0)
         far = nn(jnp.concatenate(left, axis=0), wide)
-        far = far[:32] + far[32:]
-        far = far[:16] * m.halff[0] + far[16:] * m.halff[1]
-        result.append((near[:, 128 * c : 128 * c + 128] + far).astype(BF16))
+        far = far[: 2 * n] + far[2 * n :]
+        result.append(far[:n] * m.halff[0] + far[n:] * m.halff[1])
     return result
+
+
+def build_root_basis(basis, xfer, root_basis):
+    row = lax.broadcasted_iota(jnp.int32, (32, 128), 0)
+    one = (row == (lax.broadcasted_iota(jnp.int32, (32, 128), 1) & 31)).astype(F32)
+    m = Masks(32)
+    for c, far in enumerate(far_field(down_pass(one, None, xfer, m), basis, m)):
+        high, low = halves(far)
+        root_basis[0:32, 128 * c : 128 * c + 128] = high
+        root_basis[32:64, 128 * c : 128 * c + 128] = low
+
+
+def finish(down, local, root_basis):
+    both = nn(jnp.concatenate([part[:, 0:64] for part in halves(down)], axis=0), root_basis[...])
+    return (local[...] + both[:16] + both[16:]).astype(BF16)
+
+
+def everywhere(parts):
+    total = jnp.concatenate([parts, jnp.zeros((16, 64), F32)], axis=1)
+    total = total + pltpu.roll(total, 64, 1)
+    return total + pltpu.roll(total, 32, 1)
 
 
 def store_heights(heights, out):
@@ -398,22 +420,10 @@
     return heights
 
 
-def store_local(near, couplings, near_out, couplings_out):
+def store_local(near, couplings, basis, xfer, local_out, m):
+    far = far_field(down_pass(None, couplings, xfer, m), basis, m)
     for c in range(CHUNKS):
-        near_out[:, 128 * c : 128 * c + 128] = near[c]
-    at = 0
-    for chunks in couplings:
-        for chunk in chunks:
-            couplings_out[at : at + 16, :] = chunk
-            at += 16
-
-
-def load_couplings(source):
-    couplings, at = [], 0
-    for count in (4, 2, 1, 1):
-        couplings.append([source[b : b + 16, :] for b in range(at, at + 16 * count, 16)])
-        at += 16 * count
-    return couplings
+        local_out[:, 128 * c : 128 * c + 128] = near[c] + far[c]
 
 
 def chunks_of(signal):
@@ -445,7 +455,8 @@
     signal = chunks_of(vectors)
     build_paths(place, xfer_top, wide_path, paths, weights)
     heights, root = up_pass(signal, basis, xfer_out, m)
-    write_sends(place, signal, heights, root, weights, near, far, gather)
+    write_halo(place, signal, heights, near, far)
+    write_sends(place, root, weights, gather)
     store_heights(heights, heights_out)
     copies[4].wait()
     parts = chunks_of(point_parts(points[...]))
@@ -453,21 +464,26 @@
 
 
 def table_kernel(
-    couple_top_hbm, couple_hbm, paths, top, couple_wide, couple_top, couple, wide_couple, sems
+    couple_top_hbm, couple_hbm, basis_hbm, paths, xfer, top, couple_wide, root_basis,
+    couple_top, couple, basis, wide_couple, sems,
 ):
-    copies = fetch((couple_hbm, couple_top_hbm), (couple, couple_top), sems)
+    copies = fetch((couple_top_hbm, couple_hbm, basis_hbm), (couple_top, couple, basis), sems)
+    copies[2].wait()
+    build_root_basis(basis, xfer, root_basis)
+    copies[1].wait()
+    spread_couple(couple, couple_wide)
     copies[0].wait()
-    spread_couple(couple, couple_wide)
-    copies[1].wait()
     build_top(lax.axis_index("leaf"), couple, couple_top, paths, wide_couple, top)
 
 
 def local_first_kernel(
-    cols_hbm, counts_hbm, vectors_hbm, points_hbm, couple_wide, near, far, heights_in,
-    tiles, near_out, couplings_out,
-    cols, counts, vectors, points, from_left, from_right, places_left, places_right, near_left, near_right, sems,
+    cols_hbm, counts_hbm, vectors_hbm, points_hbm, basis_hbm, couple_wide, xfer, far, near, heights_in,
+    tiles, local_out,
+    cols, counts, vectors, points, basis, from_left, from_right, places_left, places_right, near_left, near_right, sems,
 ):
-    copies = fetch((cols_hbm, counts_hbm, vectors_hbm, points_hbm), (cols, counts, vectors, points), sems)
+    copies = fetch(
+        (cols_hbm, counts_hbm, vectors_hbm, points_hbm, basis_hbm), (cols, counts, vectors, points, basis), sems
+    )
     m = Masks()
     place = lax.axis_index("leaf")
     sides(place, near, far, from_left, from_right)
@@ -478,56 +494,49 @@
     )
     couplings = couple_low(load_heights(heights_in), from_left, from_right, couple_wide, m)
     near = near_field(place, chunks_of(vectors), from_left, from_right, cols, tiles, near_left, near_right, m)
-    store_local(near, couplings, near_out, couplings_out)
-
-
-def spread_kernel(couple_hbm, basis_hbm, vectors, xfer, couple_wide, heights_out, couple, basis, sems):
-    copies = fetch((couple_hbm, basis_hbm), (couple, basis), sems)
+    store_local(near, couplings, basis, xfer, local_out, m)
+
+
+def pack_kernel(basis_hbm, vectors, xfer, near, far, heights_out, basis, sems):
+    copies = fetch((basis_hbm,), (basis,), sems)
     m = Masks()
+    signal = chunks_of(vectors)
     copies[0].wait()
-    copies[1].wait()
+    heights, _ = up_pass(signal, basis, xfer, m)
+    write_halo(lax.axis_index("leaf"), signal, heights, near, far)
+    store_heights(heights, heights_out)
+
+
+def spread_kernel(couple_hbm, after, couple_wide, couple, sems):
+    del after
+    fetch((couple_hbm,), (couple,), sems)[0].wait()
     spread_couple(couple, couple_wide)
-    store_heights(up_pass(chunks_of(vectors), basis, xfer, m)[0], heights_out)
 
 
 def local_next_kernel(
-    cols_hbm, couple_wide, vectors, tiles, near, far, heights_in, near_out, couplings_out,
-    cols, from_left, from_right, near_left, near_right, sems,
+    cols_hbm, basis_hbm, couple_wide, xfer, vectors, tiles, far, near, heights_in, local_out,
+    cols, basis, from_left, from_right, near_left, near_right, sems,
 ):
-    copies = fetch((cols_hbm,), (cols,), sems)
+    copies = fetch((cols_hbm, basis_hbm), (cols, basis), sems)
     m = Masks()
     place = lax.axis_index("leaf")
     sides(place, near, far, from_left, from_right)
     couplings = couple_low(load_heights(heights_in), from_left, from_right, couple_wide, m)
     copies[0].wait()
+    copies[1].wait()
     near = near_field(place, chunks_of(vectors), from_left, from_right, cols, tiles, near_left, near_right, m)
-    store_local(near, couplings, near_out, couplings_out)
-
-
-def down_up_kernel(
-    basis_hbm, gathered, top, xfer, near, couplings, weights, near_pack, far_pack, gather, signal_out, basis, sems
-):
-    copies = fetch((basis_hbm,), (basis,), sems)
-    m = Masks()
+    store_local(near, couplings, basis, xfer, local_out, m)
+
+
+def down_up_kernel(gathered, top, root_basis, local, weights, gather, signal_out):
     place = lax.axis_index("leaf")
-    down = down_pass(top_apply(place, gathered, top), load_couplings(couplings), xfer, m)
-    copies[0].wait()
-    signal = far_field(down, basis, near, m)
-    for c in range(CHUNKS):
-        signal_out[:, 128 * c : 128 * c + 128] = signal[c]
-    heights, root = up_pass(signal, basis, xfer, m)
-    write_sends(place, signal, heights, root, weights, near_pack, far_pack, gather)
-
-
-def down_last_kernel(basis_hbm, gathered, top, xfer, near, couplings, out, basis, sems):
-    copies = fetch((basis_hbm,), (basis,), sems)
-    m = Masks()
-    place = lax.axis_index("leaf")
-    down = down_pass(top_apply(place, gathered, top), load_couplings(couplings), xfer, m)
-    copies[0].wait()
-    signal = far_field(down, basis, near, m)
-    for c in range(CHUNKS):
-        out[:, 128 * c : 128 * c + 128] = signal[c]
+    signal = finish(top_apply(place, gathered, top), local, root_basis)
+    signal_out[...] = signal
+    write_sends(place, everywhere(nt(signal, root_basis[...])), weights, gather)
+
+
+def down_last_kernel(gathered, top, root_basis, local, out):
+    out[...] = finish(top_apply(lax.axis_index("leaf"), gathered, top), local, root_basis)
 
 
 def call(kernel, name, arguments, arrays, outputs, scratch, flops, pinned=False):
@@ -548,13 +557,16 @@
     )(*inputs)
 
 
-def exchange(near, far, gather):
+def to_all(gather):
     count = lax.axis_size("leaf")
     blocks = gather.reshape(count, 4, 128)
-    gathered = lax.all_to_all(blocks, "leaf", 0, 0, tiled=True)
-    near = lax.ppermute(near, "leaf", [(i, i ^ 1) for i in range(count)])
+    return lax.all_to_all(blocks, "leaf", 0, 0, tiled=True).reshape(count * 4, 128)
+
+
+def swap(near, far):
+    count = lax.axis_size("leaf")
     far = lax.ppermute(far, "leaf", [(i, ((i + 1) ^ 1) - 1) for i in range(1, count - 1)])
-    return near, far, gathered.reshape(count * 4, 128)
+    return far, lax.ppermute(near, "leaf", [(i, i ^ 1) for i in range(count)])
 
 
 def body(vectors, points, near_cols, near_count, basis, xfer_low, couple, xfer_top, couple_top):
@@ -564,40 +576,46 @@
     couple_buf = vm((3, 31, 1024), BF16)
     blocks = [vm((32, 16, 128), BF16)] * 2
     sends = [((512, 128), BF16), ((960, 128), BF16)]
-    local = [((16, 1024), F32), ((128, 128), F32)]
+    local_out, root_out = ((16, 1024), F32), ((64, 1024), BF16)
     near, far, gather, heights, xfer, paths, weights = call(
         first_kernel, "up_first", (vectors, points, basis, xfer_low, xfer_top), (),
         [((384, 128), BF16)] * 2 + sends + [((1024, 128), BF16), ((192, 128), F32), ((64, 768), BF16)],
         [signal_buf, points_buf, basis_buf, vm((30, 1024), BF16), vm((254, 1024), BF16), vm((160, 128), BF16), sems((5,))],
         1 << 20, True,
     )
-    near, far, gathered = exchange(near, far, gather)
-    top, couple_wide = call(
-        table_kernel, "tables", (couple_top, couple), (paths,), [((64, 2304), BF16), ((1024, 128), BF16)],
-        [vm((3, 124, 1024), BF16), couple_buf, vm((576, 128), BF16), sems((2,))], 1 << 32, True,
-    )
-    tiles, near, couplings = call(
-        local_first_kernel, "local_first", (near_cols, near_count, vectors, points),
-        (couple_wide, near, far, heights), [((1024, 768), BF16)] + local,
-        [sm((12, 16), jnp.int32), sm((16,), jnp.int32), signal_buf, points_buf] + [vm((384, 128), BF16)] * 2
-        + [vm((32, 8, 128), F32)] * 2 + blocks + [sems((4,))], 1 << 32,
-    )
-    near, far, gather, signal = call(
-        down_up_kernel, "down_up", (basis,), (gathered, top, xfer, near, couplings, weights),
-        [((320, 128), BF16)] * 2 + [sends[0], ((16, 1024), BF16)], [basis_buf, sems((1,))], 1 << 20,
-    )
-    near, far, gathered = exchange(near, far, gather)
-    couple_wide, heights = call(
-        spread_kernel, "spread", (couple, basis), (signal, xfer), [((1024, 128), BF16), sends[1]],
-        [couple_buf, basis_buf, sems((2,))], 1 << 32,
-    )
-    near, couplings = call(
-        local_next_kernel, "local_next", (near_cols,), (couple_wide, signal, tiles, near, far, heights), local,
-        [sm((12, 16), jnp.int32)] + [vm((320, 128), BF16)] * 2 + blocks + [sems((1,))], 1 << 32,
+    gathered = to_all(gather)
+    far, near = swap(near, far)
+    top, couple_wide, root_basis = call(
+        table_kernel, "tables", (couple_top, couple, basis), (paths, xfer),
+        [((64, 2304), BF16), ((1024, 128), BF16), root_out],
+        [vm((3, 124, 1024), BF16), couple_buf, basis_buf, vm((576, 128), BF16), sems((3,))], 1 << 32, True,
+    )
+    tiles, local = call(
+        local_first_kernel, "local_first", (near_cols, near_count, vectors, points, basis),
+        (couple_wide, xfer, far, near, heights), [((1024, 768), BF16), local_out],
+        [sm((12, 16), jnp.int32), sm((16,), jnp.int32), signal_buf, points_buf, basis_buf] + [vm((384, 128), BF16)] * 2
+        + [vm((32, 8, 128), F32)] * 2 + blocks + [sems((5,))], 1 << 32,
+    )
+    gather, signal = call(
+        down_up_kernel, "down_up", (), (gathered, top, root_basis, local, weights), [sends[0], ((16, 1024), BF16)], [],
+        1 << 20,
+    )
+    gathered = to_all(gather)
+    near, far, heights = call(
+        pack_kernel, "pack", (basis,), (signal, xfer), [((320, 128), BF16)] * 2 + [sends[1]], [basis_buf, sems((1,))],
+        1 << 32,
+    )
+    far, near = swap(near, far)
+    (couple_wide,) = call(
+        spread_kernel, "spread", (couple,), (heights,), [((1024, 128), BF16)], [couple_buf, sems((1,))], 1 << 32
+    )
+    (local,) = call(
+        local_next_kernel, "local_next", (near_cols, basis), (couple_wide, xfer, signal, tiles, far, near, heights),
+        [local_out],
+        [sm((12, 16), jnp.int32), basis_buf] + [vm((320, 128), BF16)] * 2 + blocks + [sems((2,))], 1 << 32,
     )
     (result,) = call(
-        down_last_kernel, "down_last", (basis,), (gathered, top, xfer, near, couplings), [((16, 1024), BF16)],
-        [basis_buf, sems((1,))], 1 << 20,
+        down_last_kernel, "down_last", (), (gathered, top, root_basis, local), [((16, 1024), BF16)], [], 1 << 20
     )
     return result
 

time: 66.8 us -> 64.3 us (0.963)
  waiting for transfers between devices: 5.79 us -> 3.89 us
  starting transfers between devices: 43.3 us -> 42.1 us
    ppermute x4, waiting for transfers between devices: 2.96 us -> 0.51 us  [the longest x2 0.5 us: swap(): return (far, lax.ppermute(near, 'leaf', [(i, i ^ 1) for i in range(count)]))]
    all_to_all x2, starting transfers between devices: 32.1 us -> 31.2 us  [to_all(): lax.all_to_all(blocks, 'leaf', 0, 0, tiled=True).reshape(count * 4, 128)]
    pallas_call x7 -> x8, Pallas kernels: 17.2 us -> 17.7 us  [call(): pl.pallas_call(kernel, out_shape=[jax.ShapeDtypeStruct(shape, dtype) for...]
  transfers between devices with their start and end apart: 6 -> 6, of which waited for: 4 -> 2; matrix products, arithmetic and copies ran while one was open for 0% -> 0% of each run, Pallas kernels for 12% -> 16%
where the time goes in v5:
time: 64.3 us; the launch traced here: 64 us
  starting transfers between devices  42.1 us (65%)
  Pallas kernels  17.7 us (28%)
  waiting for transfers between devices  3.89 us (6%)
    all_to_all x2, starting transfers between devices, to_all(): lax.all_to_all(blocks, 'leaf', 0, 0, tiled=True).reshape(count * 4, 128)  31.2 us
    pallas_call x8, Pallas kernels, call(): pl.pallas_call(kernel, out_shape=[jax.ShapeDtypeStruct(shape, dtype) for...  17.7 us
    ppermute x2, starting transfers between devices, swap(): lax.ppermute(far, 'leaf', [(i, (i + 1 ^ 1) - 1) for i in range(1, count -...  7.08 us
    ppermute x2, starting transfers between devices, swap(): return (far, lax.ppermute(near, 'leaf', [(i, i ^ 1) for i in range(count)]))  3.84 us
    all_to_all x2, waiting for transfers between devices, to_all(): lax.all_to_all(blocks, 'leaf', 0, 0, tiled=True).reshape(count * 4, 128)  3.38 us
  transfers between devices with their start and end apart: 6, of which 2 were waited for; matrix products, arithmetic and copies ran while one was open for 0% of the time, Pallas kernels for 16%

profile of v5, /device:TPU:1, one launch (start us, length us, event | category | flops | bytes accessed | tf_op | source)
XLA Modules:
  0.0 64.0 jit_solution(8730473771342676738)
XLA Ops:
  0.0 3.7 %up_first.1 = (bf16[384,128]{1,0:T(8,128)(2,1)S(1)}, bf16[384,128]{1,0:T(8,128)(2,1)S(1)}, bf16[512,128]{1,0:T(8,128)(2,1)}, bf16[960,128]{1,0:T(8,128)(2,1)S(1)...) custom-call(bf16[16,1024]{1,0:T(8,128)(2,1)} %vectors_hbm.3, ...), custom_call_target="tpu_custom_call" | custom-call | flops 1048576 | bytes 1048576 | tf_op jit(solution)/shard_map/up_first/pallas_call | solution.py:548
  3.7 18.4 %all-to-all-start = ((bf16[128,4,128]{2,1,0:T(4,128)(2,1)}), bf16[128,4,128]{2,1,0:T(4,128)(2,1)S(1)}, u32[]{:S(2)}, u32[]{:S(2)}) async-start(bf16[128,4,128]{2,1,0:T(4,128)(2,1)} %bitcast), calls=%async_computation | async-start | bytes 262144 | tf_op jit(solution)/shard_map/all_to_all | solution.py:563
  22.1 3.5 %collective-permute-start = (bf16[384,128]{1,0:T(8,128)(2,1)S(1)}, bf16[384,128]{1,0:T(8,128)(2,1)S(1)}, u32[]{:S(2)}, u32[]{:S(2)}) collective-permute-start(bf16[384,128]{1,0:T(8,128)(2,1)S(1)} %get-tuple-element.28), channel_id=1, source_target_pairs={{4,8},{8,4},{12,16},{16,12},{20,24},{24,20},{28,32},{32,28},{36,40... | collective-permute-start | bytes 294920 | tf_op jit(solution)/shard_map/ppermute | solution.py:568
  25.7 1.9 %collective-permute-start.1 = (bf16[384,128]{1,0:T(8,128)(2,1)S(1)}, bf16[384,128]{1,0:T(8,128)(2,1)S(1)}, u32[]{:S(2)}, u32[]{:S(2)}) collective-permute-start(bf16[384,128]{1,0:T(8,128)(2,1)S(1)} %get-tuple-element.29), channel_id=1, source_target_pairs={{0,4},{4,0},{8,12},{12,8},{16,20},{20,16},{24,28},{28,24},{32,36},... | collective-permute-start | bytes 294920 | tf_op jit(solution)/shard_map/ppermute | solution.py:569
  27.6 0.0 copy-start
  27.6 0.0 copy-start.1
  27.6 0.0 copy-start.2
  27.6 0.0 copy-start.4
  27.6 0.0 copy-start.5
  27.6 3.4 %tables.1 = (bf16[64,2304]{1,0:T(8,128)(2,1)S(1)}, bf16[1024,128]{1,0:T(8,128)(2,1)S(1)}, bf16[64,1024]{1,0:T(8,128)(2,1)S(1)}) custom-call(bf16[3,124,1024]{2,1,0:T(8,128)(2,1)} %couple_top_hbm.1, bf16[3,31,1024]{2,1,0:T(8,128)(2,1)} %couple_hbm.3, bf16[32,1024]{1,0:T(8,128)(2,1)} %basis_hbm.9, f32[192,128]{1,0:T(8,128)S(1)} %get-tuple-element.23.paths, ...), custom_call_target="tpu_custom_call" | custom-call | flops 4294967296 | bytes 1048576 | tf_op jit(solution)/shard_map/tables/pallas_call | solution.py:548
  31.0 0.0 collective-permute-done.far
  31.0 0.0 collective-permute-done.1.near
  31.0 0.0 copy-done
  31.0 0.0 copy-done.1
  31.0 0.0 copy-done.2
  31.1 0.0 copy-done.4
  31.1 0.0 copy-done.5
  31.1 3.9 %local_first.1 = (bf16[1024,768]{1,0:T(8,128)(2,1)S(1)}, f32[16,1024]{1,0:T(8,128)S(1)}) custom-call(s32[12,16]{1,0:T(8,128)S(1)} %copy-done.4, s32[16]{0:T(128)S(1)} %copy-done.5, bf16[16,1024]{1,0:T(8,128)(2,1)S(1)} %copy-done.1, f32[3,1024]{1,0:T(4,128)S(1)} %copy-done.2, bf16[32,1024]{1,0:T(8,128)(2,1)S(1)} %copy-done, ...), custom_call_target="tpu_custom_call" | custom-call | flops 4294967296 | bytes 1048576 | tf_op jit(solution)/shard_map/local_first/pallas_call | solution.py:548
  35.0 0.0 all-to-all-done
  35.0 2.1 %down_up.1 = (bf16[512,128]{1,0:T(8,128)(2,1)}, bf16[16,1024]{1,0:T(8,128)(2,1)S(1)}) custom-call(bf16[512,128]{1,0:T(8,128)(2,1)S(1)} %bitcast.5, bf16[64,2304]{1,0:T(8,128)(2,1)S(1)} %get-tuple-element.25.top, bf16[64,1024]{1,0:T(8,128)(2,1)S(1)} %get-tuple-element.26.root_basis, f32[16,1024]{1,0:T(8,128)S(1)} %get-tuple-element.31.local, ...), custom_call_target="tpu_custom_call" | custom-call | flops 1048576 | bytes 1048576 | tf_op jit(solution)/shard_map/down_up/pallas_call | solution.py:548
  37.1 12.8 %all-to-all-start.1 = ((bf16[128,4,128]{2,1,0:T(4,128)(2,1)}), bf16[128,4,128]{2,1,0:T(4,128)(2,1)S(1)}, u32[]{:S(2)}, u32[]{:S(2)}) async-start(bf16[128,4,128]{2,1,0:T(4,128)(2,1)} %bitcast.2), calls=%async_computation.1 | async-start | bytes 262144 | tf_op jit(solution)/shard_map/all_to_all | solution.py:563
  49.9 0.0 copy-start.3
  49.9 0.7 %pack.1 = (bf16[320,128]{1,0:T(8,128)(2,1)S(1)}, bf16[320,128]{1,0:T(8,128)(2,1)S(1)}, bf16[960,128]{1,0:T(8,128)(2,1)S(1)}) custom-call(bf16[32,1024]{1,0:T(8,128)(2,1)S(1)} %copy-done, bf16[16,1024]{1,0:T(8,128)(2,1)S(1)} %get-tuple-element.34.vectors, bf16[1024,128]{1,0:T(8,128)(2,1)S(1)} %get-tuple-element.24.xfer), custom_call_target="tpu_custom_call" | custom-call | flops 4294967296 | bytes 1048576 | tf_op jit(solution)/shard_map/pack/pallas_call | solution.py:548
  50.6 3.5 %collective-permute-start.2 = (bf16[320,128]{1,0:T(8,128)(2,1)S(1)}, bf16[320,128]{1,0:T(8,128)(2,1)S(1)}, u32[]{:S(2)}, u32[]{:S(2)}) collective-permute-start(bf16[320,128]{1,0:T(8,128)(2,1)S(1)} %get-tuple-element.37), channel_id=1, source_target_pairs={{4,8},{8,4},{12,16},{16,12},{20,24},{24,20},{28,32},{32,28},{36,40... | collective-permute-start | bytes 245768 | tf_op jit(solution)/shard_map/ppermute | solution.py:568
  54.2 1.9 %collective-permute-start.3 = (bf16[320,128]{1,0:T(8,128)(2,1)S(1)}, bf16[320,128]{1,0:T(8,128)(2,1)S(1)}, u32[]{:S(2)}, u32[]{:S(2)}) collective-permute-start(bf16[320,128]{1,0:T(8,128)(2,1)S(1)} %get-tuple-element.38), channel_id=1, source_target_pairs={{0,4},{4,0},{8,12},{12,8},{16,20},{20,16},{24,28},{28,24},{32,36},... | collective-permute-start | bytes 245768 | tf_op jit(solution)/shard_map/ppermute | solution.py:569
  56.1 0.0 copy-done.3
  56.1 0.7 %spread.1.couple_wide = bf16[1024,128]{1,0:T(8,128)(2,1)S(1)} custom-call(bf16[3,31,1024]{2,1,0:T(8,128)(2,1)S(1)} %copy-done.3, bf16[960,128]{1,0:T(8,128)(2,1)S(1)} %get-tuple-element.35.after.heights_in), custom_call_target="tpu_custom_call" | custom-call | flops 4294967296 | bytes 1048576 | tf_op jit(solution)/shard_map/spread/pallas_call | solution.py:548
  56.8 0.0 collective-permute-done.2.far
  56.8 0.5 collective-permute-done.3.near
  57.3 1.9 %local_next.1.local = f32[16,1024]{1,0:T(8,128)S(1)} custom-call(s32[12,16]{1,0:T(8,128)S(1)} %copy-done.4, bf16[32,1024]{1,0:T(8,128)(2,1)S(1)} %copy-done, bf16[1024,128]{1,0:T(8,128)(2,1)S(1)} %spread.1.couple_wide, bf16[1024,128]{1,0:T(8,128)(2,1)S(1)} %get-tuple-element.24.xfer, bf16[16,1024]{1,0:T(8,128)(2,1)S(1)} %get-tuple-element.34.vectors, ...), custom_call_target="tpu_custom_call" | custom-call | flops 4294967296 | bytes 1048576 | tf_op jit(solution)/shard_map/local_next/pallas_call | solution.py:548
  59.2 3.4 %all-to-all-done.1 = bf16[128,4,128]{2,1,0:T(4,128)(2,1)S(1)} async-done(((bf16[128,4,128]{2,1,0:T(4,128)(2,1)}), bf16[128,4,128]{2,1,0:T(4,128)(2,1)S(1)}, u32[]{:S(2)}, u32[]{:S(2)}) %all-to-all-start.1) | async-done | bytes 131104 | tf_op jit(solution)/shard_map/all_to_all | solution.py:563
  62.6 1.4 %down_last.1 = bf16[16,1024]{1,0:T(8,128)(2,1)} custom-call(bf16[512,128]{1,0:T(8,128)(2,1)S(1)} %bitcast.4, bf16[64,2304]{1,0:T(8,128)(2,1)S(1)} %get-tuple-element.25.top, bf16[64,1024]{1,0:T(8,128)(2,1)S(1)} %get-tuple-element.26.root_basis, f32[16,1024]{1,0:T(8,128)S(1)} %local_next.1.local), custom_call_target="tpu_custom_call" | custom-call | flops 1048576 | bytes 1048576 | tf_op jit(solution)/shard_map/down_last/pallas_call | solution.py:548
Async XLA Ops:
  3.7 31.3 %all-to-all-start = ((bf16[128,4,128]{2,1,0:T(4,128)(2,1)}), bf16[128,4,128]{2,1,0:T(4,128)(2,1)S(1)}, u32[]{:S(2)}, u32[]{:S(2)}) async-start(bf16[128,4,128]{2,1,0:T(4,128)(2,1)} %bitcast), calls=%async_computation | async-start | bytes 262144 | tf_op jit(solution)/shard_map/all_to_all | solution.py:563
  22.1 8.9 %collective-permute-start = (bf16[384,128]{1,0:T(8,128)(2,1)S(1)}, bf16[384,128]{1,0:T(8,128)(2,1)S(1)}, u32[]{:S(2)}, u32[]{:S(2)}) collective-permute-start(bf16[384,128]{1,0:T(8,128)(2,1)S(1)} %get-tuple-element.28), channel_id=1, source_target_pairs={{4,8},{8,4},{12,16},{16,12},{20,24},{24,20},{28,32},{32,28},{36,40... | collective-permute-start | bytes 294920 | tf_op jit(solution)/shard_map/ppermute | solution.py:568
  25.7 5.4 %collective-permute-start.1 = (bf16[384,128]{1,0:T(8,128)(2,1)S(1)}, bf16[384,128]{1,0:T(8,128)(2,1)S(1)}, u32[]{:S(2)}, u32[]{:S(2)}) collective-permute-start(bf16[384,128]{1,0:T(8,128)(2,1)S(1)} %get-tuple-element.29), channel_id=1, source_target_pairs={{0,4},{4,0},{8,12},{12,8},{16,20},{20,16},{24,28},{28,24},{32,36},... | collective-permute-start | bytes 294920 | tf_op jit(solution)/shard_map/ppermute | solution.py:569
  27.6 3.4 %copy-start = (bf16[32,1024]{1,0:T(8,128)(2,1)S(1)}, bf16[32,1024]{1,0:T(8,128)(2,1)}, u32[]{:S(2)}) copy-start(bf16[32,1024]{1,0:T(8,128)(2,1)} %basis_hbm.9) | copy-start | bytes 196612
  27.6 3.4 %copy-start.1 = (bf16[16,1024]{1,0:T(8,128)(2,1)S(1)}, bf16[16,1024]{1,0:T(8,128)(2,1)}, u32[]{:S(2)}) copy-start(bf16[16,1024]{1,0:T(8,128)(2,1)} %vectors_hbm.3) | copy-start | bytes 98308
  27.6 3.4 %copy-start.2 = (f32[3,1024]{1,0:T(4,128)S(1)}, f32[3,1024]{1,0:T(4,128)}, u32[]{:S(2)}) copy-start(f32[3,1024]{1,0:T(4,128)} %points_hbm.3) | copy-start | bytes 36868
  27.6 3.4 %copy-start.4 = (s32[12,16]{1,0:T(8,128)S(1)}, s32[12,16]{1,0:T(8,128)}, u32[]{:S(2)}) copy-start(s32[12,16]{1,0:T(8,128)} %cols_hbm.3) | copy-start | bytes 2308
  27.6 3.4 %copy-start.5 = (s32[16]{0:T(128)S(1)}, s32[16]{0:T(128)}, u32[]{:S(2)}) copy-start(s32[16]{0:T(128)} %counts_hbm.1) | copy-start | bytes 196
  37.1 25.5 %all-to-all-start.1 = ((bf16[128,4,128]{2,1,0:T(4,128)(2,1)}), bf16[128,4,128]{2,1,0:T(4,128)(2,1)S(1)}, u32[]{:S(2)}, u32[]{:S(2)}) async-start(bf16[128,4,128]{2,1,0:T(4,128)(2,1)} %bitcast.2), calls=%async_computation.1 | async-start | bytes 262144 | tf_op jit(solution)/shard_map/all_to_all | solution.py:563
  49.9 6.2 %copy-start.3 = (bf16[3,31,1024]{2,1,0:T(8,128)(2,1)S(1)}, bf16[3,31,1024]{2,1,0:T(8,128)(2,1)}, u32[]{:S(2)}) copy-start(bf16[3,31,1024]{2,1,0:T(8,128)(2,1)} %couple_hbm.3) | copy-start | bytes 571396
  50.6 6.2 %collective-permute-start.2 = (bf16[320,128]{1,0:T(8,128)(2,1)S(1)}, bf16[320,128]{1,0:T(8,128)(2,1)S(1)}, u32[]{:S(2)}, u32[]{:S(2)}) collective-permute-start(bf16[320,128]{1,0:T(8,128)(2,1)S(1)} %get-tuple-element.37), channel_id=1, source_target_pairs={{4,8},{8,4},{12,16},{16,12},{20,24},{24,20},{28,32},{32,28},{36,40... | collective-permute-start | bytes 245768 | tf_op jit(solution)/shard_map/ppermute | solution.py:568
  54.2 3.2 %collective-permute-start.3 = (bf16[320,128]{1,0:T(8,128)(2,1)S(1)}, bf16[320,128]{1,0:T(8,128)(2,1)S(1)}, u32[]{:S(2)}, u32[]{:S(2)}) collective-permute-start(bf16[320,128]{1,0:T(8,128)(2,1)S(1)} %get-tuple-element.38), channel_id=1, source_target_pairs={{0,4},{4,0},{8,12},{12,8},{16,20},{20,16},{24,28},{28,24},{32,36},... | collective-permute-start | bytes 245768 | tf_op jit(solution)/shard_map/ppermute | solution.py:569

commit v6 on v5

--- a/solution.py
+++ b/solution.py
@@ -442,24 +442,24 @@
     vectors, points, basis, xfer_low, xfer_top, wide_path, sems,
 ):
     copies = fetch(
-        (xfer_top_hbm, xfer_hbm, vectors_hbm, basis_hbm, points_hbm), (xfer_top, xfer_low, vectors, basis, points), sems
+        (xfer_hbm, vectors_hbm, basis_hbm, points_hbm, xfer_top_hbm), (xfer_low, vectors, basis, points, xfer_top), sems
     )
     place = lax.axis_index("leaf")
     m = Masks()
     xfer_out[960:1024, :] = jnp.zeros((64, 128), BF16)
+    copies[0].wait()
+    spread_table(xfer_low[...], xfer_out)
     copies[1].wait()
-    spread_table(xfer_low[...], xfer_out)
-    copies[0].wait()
     copies[2].wait()
-    copies[3].wait()
     signal = chunks_of(vectors)
-    build_paths(place, xfer_top, wide_path, paths, weights)
     heights, root = up_pass(signal, basis, xfer_out, m)
     write_halo(place, signal, heights, near, far)
+    store_heights(heights, heights_out)
+    copies[3].wait()
+    parts = chunks_of(point_parts(points[...]))
+    copies[4].wait()
+    build_paths(place, xfer_top, wide_path, paths, weights)
     write_sends(place, root, weights, gather)
-    store_heights(heights, heights_out)
-    copies[4].wait()
-    parts = chunks_of(point_parts(points[...]))
     exchange_rows(place, parts[:4], parts[4:], near, far, 320)
 
 
@@ -467,13 +467,13 @@
     couple_top_hbm, couple_hbm, basis_hbm, paths, xfer, top, couple_wide, root_basis,
     couple_top, couple, basis, wide_couple, sems,
 ):
-    copies = fetch((couple_top_hbm, couple_hbm, basis_hbm), (couple_top, couple, basis), sems)
-    copies[2].wait()
-    build_root_basis(basis, xfer, root_basis)
+    copies = fetch((basis_hbm, couple_hbm, couple_top_hbm), (basis, couple, couple_top), sems)
     copies[1].wait()
     spread_couple(couple, couple_wide)
     copies[0].wait()
+    copies[2].wait()
     build_top(lax.axis_index("leaf"), couple, couple_top, paths, wide_couple, top)
+    build_root_basis(basis, xfer, root_basis)
 
 
 def local_first_kernel(

time: 64.3 us -> 64 us (level)
  transfers between devices with their start and end apart: 6 -> 6, of which waited for: 2 -> 3; matrix products, arithmetic and copies ran while one was open for 0% -> 0% of each run, Pallas kernels for 16% -> 16%
where the time goes in v6:
time: 64 us; the launch traced here: 63.7 us
  starting transfers between devices  42 us (66%)
  Pallas kernels  17.4 us (27%)
  waiting for transfers between devices  4.07 us (6%)
    all_to_all x2, starting transfers between devices, to_all(): lax.all_to_all(blocks, 'leaf', 0, 0, tiled=True).reshape(count * 4, 128)  31 us
    pallas_call x8, Pallas kernels, call(): pl.pallas_call(kernel, out_shape=[jax.ShapeDtypeStruct(shape, dtype) for...  17.4 us
    ppermute x2, starting transfers between devices, swap(): lax.ppermute(far, 'leaf', [(i, (i + 1 ^ 1) - 1) for i in range(1, count -...  7.08 us
    ppermute x2, starting transfers between devices, swap(): return (far, lax.ppermute(near, 'leaf', [(i, i ^ 1) for i in range(count)]))  3.84 us
    all_to_all x2, waiting for transfers between devices, to_all(): lax.all_to_all(blocks, 'leaf', 0, 0, tiled=True).reshape(count * 4, 128)  3.56 us
  transfers between devices with their start and end apart: 6, of which 3 were waited for; matrix products, arithmetic and copies ran while one was open for 0% of the time, Pallas kernels for 16%

profile of v6, /device:TPU:1, one launch (start us, length us, event | category | flops | bytes accessed | tf_op | source)
XLA Modules:
  0.0 63.7 jit_solution(8643212266572853317)
XLA Ops:
  0.0 3.6 %up_first.1 = (bf16[384,128]{1,0:T(8,128)(2,1)S(1)}, bf16[384,128]{1,0:T(8,128)(2,1)S(1)}, bf16[512,128]{1,0:T(8,128)(2,1)}, bf16[960,128]{1,0:T(8,128)(2,1)S(1)...) custom-call(bf16[16,1024]{1,0:T(8,128)(2,1)} %vectors_hbm.3, ...), custom_call_target="tpu_custom_call" | custom-call | flops 1048576 | bytes 1048576 | tf_op jit(solution)/shard_map/up_first/pallas_call | solution.py:548
  3.6 18.4 %all-to-all-start = ((bf16[128,4,128]{2,1,0:T(4,128)(2,1)}), bf16[128,4,128]{2,1,0:T(4,128)(2,1)S(1)}, u32[]{:S(2)}, u32[]{:S(2)}) async-start(bf16[128,4,128]{2,1,0:T(4,128)(2,1)} %bitcast), calls=%async_computation | async-start | bytes 262144 | tf_op jit(solution)/shard_map/all_to_all | solution.py:563
  22.1 3.5 %collective-permute-start = (bf16[384,128]{1,0:T(8,128)(2,1)S(1)}, bf16[384,128]{1,0:T(8,128)(2,1)S(1)}, u32[]{:S(2)}, u32[]{:S(2)}) collective-permute-start(bf16[384,128]{1,0:T(8,128)(2,1)S(1)} %get-tuple-element.28), channel_id=1, source_target_pairs={{4,8},{8,4},{12,16},{16,12},{20,24},{24,20},{28,32},{32,28},{36,40... | collective-permute-start | bytes 294920 | tf_op jit(solution)/shard_map/ppermute | solution.py:568
  25.6 1.9 %collective-permute-start.1 = (bf16[384,128]{1,0:T(8,128)(2,1)S(1)}, bf16[384,128]{1,0:T(8,128)(2,1)S(1)}, u32[]{:S(2)}, u32[]{:S(2)}) collective-permute-start(bf16[384,128]{1,0:T(8,128)(2,1)S(1)} %get-tuple-element.29), channel_id=1, source_target_pairs={{0,4},{4,0},{8,12},{12,8},{16,20},{20,16},{24,28},{28,24},{32,36},... | collective-permute-start | bytes 294920 | tf_op jit(solution)/shard_map/ppermute | solution.py:569
  27.6 0.0 copy-start
  27.6 0.0 copy-start.1
  27.6 0.0 copy-start.2
  27.6 0.0 copy-start.4
  27.6 0.0 copy-start.5
  27.6 3.0 %tables.1 = (bf16[64,2304]{1,0:T(8,128)(2,1)S(1)}, bf16[1024,128]{1,0:T(8,128)(2,1)S(1)}, bf16[64,1024]{1,0:T(8,128)(2,1)S(1)}) custom-call(bf16[3,124,1024]{2,1,0:T(8,128)(2,1)} %couple_top_hbm.1, bf16[3,31,1024]{2,1,0:T(8,128)(2,1)} %couple_hbm.3, bf16[32,1024]{1,0:T(8,128)(2,1)} %basis_hbm.9, f32[192,128]{1,0:T(8,128)S(1)} %get-tuple-element.23.paths, ...), custom_call_target="tpu_custom_call" | custom-call | flops 4294967296 | bytes 1048576 | tf_op jit(solution)/shard_map/tables/pallas_call | solution.py:548
  30.7 0.0 collective-permute-done.far
  30.7 0.0 collective-permute-done.1.near
  30.7 0.0 copy-done
  30.7 0.0 copy-done.1
  30.7 0.0 copy-done.2
  30.7 0.0 copy-done.4
  30.7 0.0 copy-done.5
  30.7 3.9 %local_first.1 = (bf16[1024,768]{1,0:T(8,128)(2,1)S(1)}, f32[16,1024]{1,0:T(8,128)S(1)}) custom-call(s32[12,16]{1,0:T(8,128)S(1)} %copy-done.4, s32[16]{0:T(128)S(1)} %copy-done.5, bf16[16,1024]{1,0:T(8,128)(2,1)S(1)} %copy-done.1, f32[3,1024]{1,0:T(4,128)S(1)} %copy-done.2, bf16[32,1024]{1,0:T(8,128)(2,1)S(1)} %copy-done, ...), custom_call_target="tpu_custom_call" | custom-call | flops 4294967296 | bytes 1048576 | tf_op jit(solution)/shard_map/local_first/pallas_call | solution.py:548
  34.6 0.2 all-to-all-done
  34.8 2.1 %down_up.1 = (bf16[512,128]{1,0:T(8,128)(2,1)}, bf16[16,1024]{1,0:T(8,128)(2,1)S(1)}) custom-call(bf16[512,128]{1,0:T(8,128)(2,1)S(1)} %bitcast.5, bf16[64,2304]{1,0:T(8,128)(2,1)S(1)} %get-tuple-element.25.top, bf16[64,1024]{1,0:T(8,128)(2,1)S(1)} %get-tuple-element.26.root_basis, f32[16,1024]{1,0:T(8,128)S(1)} %get-tuple-element.31.local, ...), custom_call_target="tpu_custom_call" | custom-call | flops 1048576 | bytes 1048576 | tf_op jit(solution)/shard_map/down_up/pallas_call | solution.py:548
  36.9 12.6 %all-to-all-start.1 = ((bf16[128,4,128]{2,1,0:T(4,128)(2,1)}), bf16[128,4,128]{2,1,0:T(4,128)(2,1)S(1)}, u32[]{:S(2)}, u32[]{:S(2)}) async-start(bf16[128,4,128]{2,1,0:T(4,128)(2,1)} %bitcast.2), calls=%async_computation.1 | async-start | bytes 262144 | tf_op jit(solution)/shard_map/all_to_all | solution.py:563
  49.5 0.0 copy-start.3
  49.5 0.7 %pack.1 = (bf16[320,128]{1,0:T(8,128)(2,1)S(1)}, bf16[320,128]{1,0:T(8,128)(2,1)S(1)}, bf16[960,128]{1,0:T(8,128)(2,1)S(1)}) custom-call(bf16[32,1024]{1,0:T(8,128)(2,1)S(1)} %copy-done, bf16[16,1024]{1,0:T(8,128)(2,1)S(1)} %get-tuple-element.34.vectors, bf16[1024,128]{1,0:T(8,128)(2,1)S(1)} %get-tuple-element.24.xfer), custom_call_target="tpu_custom_call" | custom-call | flops 4294967296 | bytes 1048576 | tf_op jit(solution)/shard_map/pack/pallas_call | solution.py:548
  50.3 3.5 %collective-permute-start.2 = (bf16[320,128]{1,0:T(8,128)(2,1)S(1)}, bf16[320,128]{1,0:T(8,128)(2,1)S(1)}, u32[]{:S(2)}, u32[]{:S(2)}) collective-permute-start(bf16[320,128]{1,0:T(8,128)(2,1)S(1)} %get-tuple-element.37), channel_id=1, source_target_pairs={{4,8},{8,4},{12,16},{16,12},{20,24},{24,20},{28,32},{32,28},{36,40... | collective-permute-start | bytes 245768 | tf_op jit(solution)/shard_map/ppermute | solution.py:568
  53.8 1.9 %collective-permute-start.3 = (bf16[320,128]{1,0:T(8,128)(2,1)S(1)}, bf16[320,128]{1,0:T(8,128)(2,1)S(1)}, u32[]{:S(2)}, u32[]{:S(2)}) collective-permute-start(bf16[320,128]{1,0:T(8,128)(2,1)S(1)} %get-tuple-element.38), channel_id=1, source_target_pairs={{0,4},{4,0},{8,12},{12,8},{16,20},{20,16},{24,28},{28,24},{32,36},... | collective-permute-start | bytes 245768 | tf_op jit(solution)/shard_map/ppermute | solution.py:569
  55.8 0.0 copy-done.3
  55.8 0.7 %spread.1.couple_wide = bf16[1024,128]{1,0:T(8,128)(2,1)S(1)} custom-call(bf16[3,31,1024]{2,1,0:T(8,128)(2,1)S(1)} %copy-done.3, bf16[960,128]{1,0:T(8,128)(2,1)S(1)} %get-tuple-element.35.after.heights_in), custom_call_target="tpu_custom_call" | custom-call | flops 4294967296 | bytes 1048576 | tf_op jit(solution)/shard_map/spread/pallas_call | solution.py:548
  56.5 0.0 collective-permute-done.2.far
  56.5 0.5 collective-permute-done.3.near
  57.0 1.9 %local_next.1.local = f32[16,1024]{1,0:T(8,128)S(1)} custom-call(s32[12,16]{1,0:T(8,128)S(1)} %copy-done.4, bf16[32,1024]{1,0:T(8,128)(2,1)S(1)} %copy-done, bf16[1024,128]{1,0:T(8,128)(2,1)S(1)} %spread.1.couple_wide, bf16[1024,128]{1,0:T(8,128)(2,1)S(1)} %get-tuple-element.24.xfer, bf16[16,1024]{1,0:T(8,128)(2,1)S(1)} %get-tuple-element.34.vectors, ...), custom_call_target="tpu_custom_call" | custom-call | flops 4294967296 | bytes 1048576 | tf_op jit(solution)/shard_map/local_next/pallas_call | solution.py:548
  58.9 3.4 %all-to-all-done.1 = bf16[128,4,128]{2,1,0:T(4,128)(2,1)S(1)} async-done(((bf16[128,4,128]{2,1,0:T(4,128)(2,1)}), bf16[128,4,128]{2,1,0:T(4,128)(2,1)S(1)}, u32[]{:S(2)}, u32[]{:S(2)}) %all-to-all-start.1) | async-done | bytes 131104 | tf_op jit(solution)/shard_map/all_to_all | solution.py:563
  62.3 1.4 %down_last.1 = bf16[16,1024]{1,0:T(8,128)(2,1)} custom-call(bf16[512,128]{1,0:T(8,128)(2,1)S(1)} %bitcast.4, bf16[64,2304]{1,0:T(8,128)(2,1)S(1)} %get-tuple-element.25.top, bf16[64,1024]{1,0:T(8,128)(2,1)S(1)} %get-tuple-element.26.root_basis, f32[16,1024]{1,0:T(8,128)S(1)} %local_next.1.local), custom_call_target="tpu_custom_call" | custom-call | flops 1048576 | bytes 1048576 | tf_op jit(solution)/shard_map/down_last/pallas_call | solution.py:548
Async XLA Ops:
  3.6 31.2 %all-to-all-start = ((bf16[128,4,128]{2,1,0:T(4,128)(2,1)}), bf16[128,4,128]{2,1,0:T(4,128)(2,1)S(1)}, u32[]{:S(2)}, u32[]{:S(2)}) async-start(bf16[128,4,128]{2,1,0:T(4,128)(2,1)} %bitcast), calls=%async_computation | async-start | bytes 262144 | tf_op jit(solution)/shard_map/all_to_all | solution.py:563
  22.1 8.6 %collective-permute-start = (bf16[384,128]{1,0:T(8,128)(2,1)S(1)}, bf16[384,128]{1,0:T(8,128)(2,1)S(1)}, u32[]{:S(2)}, u32[]{:S(2)}) collective-permute-start(bf16[384,128]{1,0:T(8,128)(2,1)S(1)} %get-tuple-element.28), channel_id=1, source_target_pairs={{4,8},{8,4},{12,16},{16,12},{20,24},{24,20},{28,32},{32,28},{36,40... | collective-permute-start | bytes 294920 | tf_op jit(solution)/shard_map/ppermute | solution.py:568
  25.6 5.1 %collective-permute-start.1 = (bf16[384,128]{1,0:T(8,128)(2,1)S(1)}, bf16[384,128]{1,0:T(8,128)(2,1)S(1)}, u32[]{:S(2)}, u32[]{:S(2)}) collective-permute-start(bf16[384,128]{1,0:T(8,128)(2,1)S(1)} %get-tuple-element.29), channel_id=1, source_target_pairs={{0,4},{4,0},{8,12},{12,8},{16,20},{20,16},{24,28},{28,24},{32,36},... | collective-permute-start | bytes 294920 | tf_op jit(solution)/shard_map/ppermute | solution.py:569
  27.6 3.1 %copy-start = (bf16[32,1024]{1,0:T(8,128)(2,1)S(1)}, bf16[32,1024]{1,0:T(8,128)(2,1)}, u32[]{:S(2)}) copy-start(bf16[32,1024]{1,0:T(8,128)(2,1)} %basis_hbm.9) | copy-start | bytes 196612
  27.6 3.1 %copy-start.1 = (bf16[16,1024]{1,0:T(8,128)(2,1)S(1)}, bf16[16,1024]{1,0:T(8,128)(2,1)}, u32[]{:S(2)}) copy-start(bf16[16,1024]{1,0:T(8,128)(2,1)} %vectors_hbm.3) | copy-start | bytes 98308
  27.6 3.1 %copy-start.2 = (f32[3,1024]{1,0:T(4,128)S(1)}, f32[3,1024]{1,0:T(4,128)}, u32[]{:S(2)}) copy-start(f32[3,1024]{1,0:T(4,128)} %points_hbm.3) | copy-start | bytes 36868
  27.6 3.1 %copy-start.4 = (s32[12,16]{1,0:T(8,128)S(1)}, s32[12,16]{1,0:T(8,128)}, u32[]{:S(2)}) copy-start(s32[12,16]{1,0:T(8,128)} %cols_hbm.3) | copy-start | bytes 2308
  27.6 3.1 %copy-start.5 = (s32[16]{0:T(128)S(1)}, s32[16]{0:T(128)}, u32[]{:S(2)}) copy-start(s32[16]{0:T(128)} %counts_hbm.1) | copy-start | bytes 196
  36.9 25.3 %all-to-all-start.1 = ((bf16[128,4,128]{2,1,0:T(4,128)(2,1)}), bf16[128,4,128]{2,1,0:T(4,128)(2,1)S(1)}, u32[]{:S(2)}, u32[]{:S(2)}) async-start(bf16[128,4,128]{2,1,0:T(4,128)(2,1)} %bitcast.2), calls=%async_computation.1 | async-start | bytes 262144 | tf_op jit(solution)/shard_map/all_to_all | solution.py:563
  49.5 6.2 %copy-start.3 = (bf16[3,31,1024]{2,1,0:T(8,128)(2,1)S(1)}, bf16[3,31,1024]{2,1,0:T(8,128)(2,1)}, u32[]{:S(2)}) copy-start(bf16[3,31,1024]{2,1,0:T(8,128)(2,1)} %couple_hbm.3) | copy-start | bytes 571396
  50.3 6.2 %collective-permute-start.2 = (bf16[320,128]{1,0:T(8,128)(2,1)S(1)}, bf16[320,128]{1,0:T(8,128)(2,1)S(1)}, u32[]{:S(2)}, u32[]{:S(2)}) collective-permute-start(bf16[320,128]{1,0:T(8,128)(2,1)S(1)} %get-tuple-element.37), channel_id=1, source_target_pairs={{4,8},{8,4},{12,16},{16,12},{20,24},{24,20},{28,32},{32,28},{36,40... | collective-permute-start | bytes 245768 | tf_op jit(solution)/shard_map/ppermute | solution.py:568
  53.8 3.2 %collective-permute-start.3 = (bf16[320,128]{1,0:T(8,128)(2,1)S(1)}, bf16[320,128]{1,0:T(8,128)(2,1)S(1)}, u32[]{:S(2)}, u32[]{:S(2)}) collective-permute-start(bf16[320,128]{1,0:T(8,128)(2,1)S(1)} %get-tuple-element.38), channel_id=1, source_target_pairs={{0,4},{4,0},{8,12},{12,8},{16,20},{20,16},{24,28},{28,24},{32,36},... | collective-permute-start | bytes 245768 | tf_op jit(solution)/shard_map/ppermute | solution.py:569

commit v7 on v6

--- a/solution.py
+++ b/solution.py
@@ -438,8 +438,8 @@
 
 
 def first_kernel(
-    vectors_hbm, points_hbm, basis_hbm, xfer_hbm, xfer_top_hbm, near, far, gather, heights_out, xfer_out, paths, weights,
-    vectors, points, basis, xfer_low, xfer_top, wide_path, sems,
+    vectors_hbm, points_hbm, basis_hbm, xfer_hbm, xfer_top_hbm, near, far, gather, heights_out, xfer_out, paths, weights, basis,
+    vectors, points, xfer_low, xfer_top, wide_path, sems,
 ):
     copies = fetch(
         (xfer_hbm, vectors_hbm, basis_hbm, points_hbm, xfer_top_hbm), (xfer_low, vectors, basis, points, xfer_top), sems
@@ -463,35 +463,30 @@
     exchange_rows(place, parts[:4], parts[4:], near, far, 320)
 
 
-def table_kernel(
-    couple_top_hbm, couple_hbm, basis_hbm, paths, xfer, top, couple_wide, root_basis,
-    couple_top, couple, basis, wide_couple, sems,
-):
-    copies = fetch((basis_hbm, couple_hbm, couple_top_hbm), (basis, couple, couple_top), sems)
-    copies[1].wait()
-    spread_couple(couple, couple_wide)
-    copies[0].wait()
-    copies[2].wait()
-    build_top(lax.axis_index("leaf"), couple, couple_top, paths, wide_couple, top)
-    build_root_basis(basis, xfer, root_basis)
-
-
 def local_first_kernel(
-    cols_hbm, counts_hbm, vectors_hbm, points_hbm, basis_hbm, couple_wide, xfer, far, near, heights_in,
-    tiles, local_out,
-    cols, counts, vectors, points, basis, from_left, from_right, places_left, places_right, near_left, near_right, sems,
+    cols_hbm, counts_hbm, vectors_hbm, points_hbm, couple_hbm, couple_top_hbm,
+    couple_wide, basis, paths, xfer, far, near, heights_in,
+    tiles, local_out, top, root_basis,
+    cols, counts, vectors, points, couple, couple_top, wide_couple, from_left, from_right,
+    places_left, places_right, near_left, near_right, sems,
 ):
     copies = fetch(
-        (cols_hbm, counts_hbm, vectors_hbm, points_hbm, basis_hbm), (cols, counts, vectors, points, basis), sems
+        (cols_hbm, counts_hbm, vectors_hbm, points_hbm, couple_hbm, couple_top_hbm),
+        (cols, counts, vectors, points, couple, couple_top),
+        sems,
     )
     m = Masks()
     place = lax.axis_index("leaf")
+    build_root_basis(basis, xfer, root_basis)
     sides(place, near, far, from_left, from_right)
-    for copy in copies:
+    for copy in copies[:4]:
         copy.wait()
     build_tiles(
         place, point_parts(points[...]), cols, counts, from_left, from_right, places_left, places_right, tiles
     )
+    copies[4].wait()
+    copies[5].wait()
+    build_top(place, couple, couple_top, paths, wide_couple, top)
     couplings = couple_low(load_heights(heights_in), from_left, from_right, couple_wide, m)
     near = near_field(place, chunks_of(vectors), from_left, from_right, cols, tiles, near_left, near_right, m)
     store_local(near, couplings, basis, xfer, local_out, m)
@@ -577,24 +572,25 @@
     blocks = [vm((32, 16, 128), BF16)] * 2
     sends = [((512, 128), BF16), ((960, 128), BF16)]
     local_out, root_out = ((16, 1024), F32), ((64, 1024), BF16)
-    near, far, gather, heights, xfer, paths, weights = call(
+    near, far, gather, heights, xfer, paths, weights, basis_near = call(
         first_kernel, "up_first", (vectors, points, basis, xfer_low, xfer_top), (),
-        [((384, 128), BF16)] * 2 + sends + [((1024, 128), BF16), ((192, 128), F32), ((64, 768), BF16)],
-        [signal_buf, points_buf, basis_buf, vm((30, 1024), BF16), vm((254, 1024), BF16), vm((160, 128), BF16), sems((5,))],
+        [((384, 128), BF16)] * 2 + sends + [((1024, 128), BF16), ((192, 128), F32), ((64, 768), BF16)]
+        + [((32, 1024), BF16)],
+        [signal_buf, points_buf, vm((30, 1024), BF16), vm((254, 1024), BF16), vm((160, 128), BF16), sems((5,))],
         1 << 20, True,
     )
     gathered = to_all(gather)
     far, near = swap(near, far)
-    top, couple_wide, root_basis = call(
-        table_kernel, "tables", (couple_top, couple, basis), (paths, xfer),
-        [((64, 2304), BF16), ((1024, 128), BF16), root_out],
-        [vm((3, 124, 1024), BF16), couple_buf, basis_buf, vm((576, 128), BF16), sems((3,))], 1 << 32, True,
-    )
-    tiles, local = call(
-        local_first_kernel, "local_first", (near_cols, near_count, vectors, points, basis),
-        (couple_wide, xfer, far, near, heights), [((1024, 768), BF16), local_out],
-        [sm((12, 16), jnp.int32), sm((16,), jnp.int32), signal_buf, points_buf, basis_buf] + [vm((384, 128), BF16)] * 2
-        + [vm((32, 8, 128), F32)] * 2 + blocks + [sems((5,))], 1 << 32,
+    (couple_wide,) = call(
+        spread_kernel, "spread", (couple,), (heights,), [((1024, 128), BF16)], [couple_buf, sems((1,))], 1 << 32, True
+    )
+    tiles, local, top, root_basis = call(
+        local_first_kernel, "local_first", (near_cols, near_count, vectors, points, couple, couple_top),
+        (couple_wide, basis_near, paths, xfer, far, near, heights),
+        [((1024, 768), BF16), local_out, ((64, 2304), BF16), root_out],
+        [sm((12, 16), jnp.int32), sm((16,), jnp.int32), signal_buf, points_buf, couple_buf, vm((3, 124, 1024), BF16),
+         vm((576, 128), BF16)] + [vm((384, 128), BF16)] * 2 + [vm((32, 8, 128), F32)] * 2 + blocks
+        + [sems((6,))], 1 << 33, True,
     )
     gather, signal = call(
         down_up_kernel, "down_up", (), (gathered, top, root_basis, local, weights), [sends[0], ((16, 1024), BF16)], [],

time: 64 us -> 64.6 us (level)
  transfers between devices with their start and end apart: 6 -> 6, of which waited for: 3 -> 3; matrix products, arithmetic and copies ran while one was open for 0% -> 0% of each run, Pallas kernels for 16% -> 15%
where the time goes in v7:
time: 64.6 us; the launch traced here: 64.2 us
  starting transfers between devices  42.6 us (66%)
  Pallas kernels  16.8 us (26%)
  waiting for transfers between devices  4.65 us (7%)
    all_to_all x2, starting transfers between devices, to_all(): lax.all_to_all(blocks, 'leaf', 0, 0, tiled=True).reshape(count * 4, 128)  31.6 us
    pallas_call x8, Pallas kernels, call(): pl.pallas_call(kernel, out_shape=[jax.ShapeDtypeStruct(shape, dtype) for...  16.8 us
    ppermute x2, starting transfers between devices, swap(): lax.ppermute(far, 'leaf', [(i, (i + 1 ^ 1) - 1) for i in range(1, count -...  7.08 us
    all_to_all x2, waiting for transfers between devices, to_all(): lax.all_to_all(blocks, 'leaf', 0, 0, tiled=True).reshape(count * 4, 128)  4.15 us
    ppermute x2, starting transfers between devices, swap(): return (far, lax.ppermute(near, 'leaf', [(i, i ^ 1) for i in range(count)]))  3.84 us
  transfers between devices with their start and end apart: 6, of which 3 were waited for; matrix products, arithmetic and copies ran while one was open for 0% of the time, Pallas kernels for 15%

profile of v7, /device:TPU:1, one launch (start us, length us, event | category | flops | bytes accessed | tf_op | source)
XLA Modules:
  0.0 64.2 jit_solution(7356891211976832370)
XLA Ops:
  0.0 3.6 %up_first.1 = (bf16[384,128]{1,0:T(8,128)(2,1)S(1)}, bf16[384,128]{1,0:T(8,128)(2,1)S(1)}, bf16[512,128]{1,0:T(8,128)(2,1)}, bf16[960,128]{1,0:T(8,128)(2,1)S(1)...) custom-call(bf16[16,1024]{1,0:T(8,128)(2,1)} %vectors_hbm.3, ...), custom_call_target="tpu_custom_call" | custom-call | flops 1048576 | bytes 1048576 | tf_op jit(solution)/shard_map/up_first/pallas_call | solution.py:543
  3.6 18.4 %all-to-all-start = ((bf16[128,4,128]{2,1,0:T(4,128)(2,1)}), bf16[128,4,128]{2,1,0:T(4,128)(2,1)S(1)}, u32[]{:S(2)}, u32[]{:S(2)}) async-start(bf16[128,4,128]{2,1,0:T(4,128)(2,1)} %bitcast), calls=%async_computation | async-start | bytes 262144 | tf_op jit(solution)/shard_map/all_to_all | solution.py:558
  22.1 3.5 %collective-permute-start = (bf16[384,128]{1,0:T(8,128)(2,1)S(1)}, bf16[384,128]{1,0:T(8,128)(2,1)S(1)}, u32[]{:S(2)}, u32[]{:S(2)}) collective-permute-start(bf16[384,128]{1,0:T(8,128)(2,1)S(1)} %get-tuple-element.27), channel_id=1, source_target_pairs={{4,8},{8,4},{12,16},{16,12},{20,24},{24,20},{28,32},{32,28},{36,40... | collective-permute-start | bytes 294920 | tf_op jit(solution)/shard_map/ppermute | solution.py:563
  25.6 1.9 %collective-permute-start.1 = (bf16[384,128]{1,0:T(8,128)(2,1)S(1)}, bf16[384,128]{1,0:T(8,128)(2,1)S(1)}, u32[]{:S(2)}, u32[]{:S(2)}) collective-permute-start(bf16[384,128]{1,0:T(8,128)(2,1)S(1)} %get-tuple-element.28), channel_id=1, source_target_pairs={{0,4},{4,0},{8,12},{12,8},{16,20},{20,16},{24,28},{28,24},{32,36},... | collective-permute-start | bytes 294920 | tf_op jit(solution)/shard_map/ppermute | solution.py:564
  27.5 1.4 %spread.2.couple_wide = bf16[1024,128]{1,0:T(8,128)(2,1)S(1)} custom-call(bf16[3,31,1024]{2,1,0:T(8,128)(2,1)} %couple_hbm.5, bf16[960,128]{1,0:T(8,128)(2,1)S(1)} %get-tuple-element.23.after.heights_in), custom_call_target="tpu_custom_call" | custom-call | flops 4294967296 | bytes 1048576 | tf_op jit(solution)/shard_map/spread/pallas_call | solution.py:543
  28.9 0.0 collective-permute-done.far
  29.0 0.0 collective-permute-done.1.near
  29.0 0.0 copy-start
  29.0 5.0 %local_first.1 = (bf16[1024,768]{1,0:T(8,128)(2,1)S(1)}, f32[16,1024]{1,0:T(8,128)S(1)}, bf16[64,2304]{1,0:T(8,128)(2,1)S(1)}, bf16[64,1024]{1,0:T(8,128)(2,1)S(1)}) custom-call(s32[12,16]{1,0:T(8,128)} %cols_hbm.3, s32[16]{0:T(128)} %counts_hbm.1, bf16[16,1024]{1,0:T(8,128)(2,1)} %vectors_hbm.3, f32[3,1024]{1,0:T(4,128)} %points_hbm.3, ...), custom_call_target="tpu_custom_call" | custom-call | flops 8589934592 | bytes 1048576 | tf_op jit(solution)/shard_map/local_first/pallas_call | solution.py:543
  34.0 0.8 %all-to-all-done = bf16[128,4,128]{2,1,0:T(4,128)(2,1)S(1)} async-done(((bf16[128,4,128]{2,1,0:T(4,128)(2,1)}), bf16[128,4,128]{2,1,0:T(4,128)(2,1)S(1)}, u32[]{:S(2)}, u32[]{:S(2)}) %all-to-all-start) | async-done | bytes 131104 | tf_op jit(solution)/shard_map/all_to_all | solution.py:558
  34.8 2.1 %down_up.1 = (bf16[512,128]{1,0:T(8,128)(2,1)}, bf16[16,1024]{1,0:T(8,128)(2,1)S(1)}) custom-call(bf16[512,128]{1,0:T(8,128)(2,1)S(1)} %bitcast.5, bf16[64,2304]{1,0:T(8,128)(2,1)S(1)} %get-tuple-element.29.top, bf16[64,1024]{1,0:T(8,128)(2,1)S(1)} %get-tuple-element.30.root_basis, f32[16,1024]{1,0:T(8,128)S(1)} %get-tuple-element.31.local, ...), custom_call_target="tpu_custom_call" | custom-call | flops 1048576 | bytes 1048576 | tf_op jit(solution)/shard_map/down_up/pallas_call | solution.py:543
  36.9 13.2 %all-to-all-start.1 = ((bf16[128,4,128]{2,1,0:T(4,128)(2,1)}), bf16[128,4,128]{2,1,0:T(4,128)(2,1)S(1)}, u32[]{:S(2)}, u32[]{:S(2)}) async-start(bf16[128,4,128]{2,1,0:T(4,128)(2,1)} %bitcast.2), calls=%async_computation.1 | async-start | bytes 262144 | tf_op jit(solution)/shard_map/all_to_all | solution.py:558
  50.1 0.0 copy-done
  50.1 0.0 copy-start.1
  50.1 0.7 %pack.1 = (bf16[320,128]{1,0:T(8,128)(2,1)S(1)}, bf16[320,128]{1,0:T(8,128)(2,1)S(1)}, bf16[960,128]{1,0:T(8,128)(2,1)S(1)}) custom-call(bf16[32,1024]{1,0:T(8,128)(2,1)S(1)} %copy-done, bf16[16,1024]{1,0:T(8,128)(2,1)S(1)} %get-tuple-element.34.vectors, bf16[1024,128]{1,0:T(8,128)(2,1)S(1)} %get-tuple-element.26.xfer), custom_call_target="tpu_custom_call" | custom-call | flops 4294967296 | bytes 1048576 | tf_op jit(solution)/shard_map/pack/pallas_call | solution.py:543
  50.8 3.5 %collective-permute-start.2 = (bf16[320,128]{1,0:T(8,128)(2,1)S(1)}, bf16[320,128]{1,0:T(8,128)(2,1)S(1)}, u32[]{:S(2)}, u32[]{:S(2)}) collective-permute-start(bf16[320,128]{1,0:T(8,128)(2,1)S(1)} %get-tuple-element.37), channel_id=1, source_target_pairs={{4,8},{8,4},{12,16},{16,12},{20,24},{24,20},{28,32},{32,28},{36,40... | collective-permute-start | bytes 245768 | tf_op jit(solution)/shard_map/ppermute | solution.py:563
  54.4 1.9 %collective-permute-start.3 = (bf16[320,128]{1,0:T(8,128)(2,1)S(1)}, bf16[320,128]{1,0:T(8,128)(2,1)S(1)}, u32[]{:S(2)}, u32[]{:S(2)}) collective-permute-start(bf16[320,128]{1,0:T(8,128)(2,1)S(1)} %get-tuple-element.38), channel_id=1, source_target_pairs={{0,4},{4,0},{8,12},{12,8},{16,20},{20,16},{24,28},{28,24},{32,36},... | collective-permute-start | bytes 245768 | tf_op jit(solution)/shard_map/ppermute | solution.py:564
  56.3 0.0 copy-done.1
  56.3 0.0 copy-start.2
  56.3 0.7 %spread.3.couple_wide = bf16[1024,128]{1,0:T(8,128)(2,1)S(1)} custom-call(bf16[3,31,1024]{2,1,0:T(8,128)(2,1)S(1)} %copy-done.1, bf16[960,128]{1,0:T(8,128)(2,1)S(1)} %get-tuple-element.35.after.heights_in), custom_call_target="tpu_custom_call" | custom-call | flops 4294967296 | bytes 1048576 | tf_op jit(solution)/shard_map/spread/pallas_call | solution.py:543
  57.1 0.0 collective-permute-done.2.far
  57.1 0.5 collective-permute-done.3.near
  57.6 0.0 copy-done.2
  57.6 1.9 %local_next.1.local = f32[16,1024]{1,0:T(8,128)S(1)} custom-call(s32[12,16]{1,0:T(8,128)S(1)} %copy-done.2, bf16[32,1024]{1,0:T(8,128)(2,1)S(1)} %copy-done, bf16[1024,128]{1,0:T(8,128)(2,1)S(1)} %spread.3.couple_wide, bf16[1024,128]{1,0:T(8,128)(2,1)S(1)} %get-tuple-element.26.xfer, bf16[16,1024]{1,0:T(8,128)(2,1)S(1)} %get-tuple-element.34.vectors, ...), custom_call_target="tpu_custom_call" | custom-call | flops 4294967296 | bytes 1048576 | tf_op jit(solution)/shard_map/local_next/pallas_call | solution.py:543
  59.4 3.4 %all-to-all-done.1 = bf16[128,4,128]{2,1,0:T(4,128)(2,1)S(1)} async-done(((bf16[128,4,128]{2,1,0:T(4,128)(2,1)}), bf16[128,4,128]{2,1,0:T(4,128)(2,1)S(1)}, u32[]{:S(2)}, u32[]{:S(2)}) %all-to-all-start.1) | async-done | bytes 131104 | tf_op jit(solution)/shard_map/all_to_all | solution.py:558
  62.8 1.4 %down_last.1 = bf16[16,1024]{1,0:T(8,128)(2,1)} custom-call(bf16[512,128]{1,0:T(8,128)(2,1)S(1)} %bitcast.4, bf16[64,2304]{1,0:T(8,128)(2,1)S(1)} %get-tuple-element.29.top, bf16[64,1024]{1,0:T(8,128)(2,1)S(1)} %get-tuple-element.30.root_basis, f32[16,1024]{1,0:T(8,128)S(1)} %local_next.1.local), custom_call_target="tpu_custom_call" | custom-call | flops 1048576 | bytes 1048576 | tf_op jit(solution)/shard_map/down_last/pallas_call | solution.py:543
Async XLA Ops:
  3.6 31.2 %all-to-all-start = ((bf16[128,4,128]{2,1,0:T(4,128)(2,1)}), bf16[128,4,128]{2,1,0:T(4,128)(2,1)S(1)}, u32[]{:S(2)}, u32[]{:S(2)}) async-start(bf16[128,4,128]{2,1,0:T(4,128)(2,1)} %bitcast), calls=%async_computation | async-start | bytes 262144 | tf_op jit(solution)/shard_map/all_to_all | solution.py:558
  22.1 6.9 %collective-permute-start = (bf16[384,128]{1,0:T(8,128)(2,1)S(1)}, bf16[384,128]{1,0:T(8,128)(2,1)S(1)}, u32[]{:S(2)}, u32[]{:S(2)}) collective-permute-start(bf16[384,128]{1,0:T(8,128)(2,1)S(1)} %get-tuple-element.27), channel_id=1, source_target_pairs={{4,8},{8,4},{12,16},{16,12},{20,24},{24,20},{28,32},{32,28},{36,40... | collective-permute-start | bytes 294920 | tf_op jit(solution)/shard_map/ppermute | solution.py:563
  25.6 3.3 %collective-permute-start.1 = (bf16[384,128]{1,0:T(8,128)(2,1)S(1)}, bf16[384,128]{1,0:T(8,128)(2,1)S(1)}, u32[]{:S(2)}, u32[]{:S(2)}) collective-permute-start(bf16[384,128]{1,0:T(8,128)(2,1)S(1)} %get-tuple-element.28), channel_id=1, source_target_pairs={{0,4},{4,0},{8,12},{12,8},{16,20},{20,16},{24,28},{28,24},{32,36},... | collective-permute-start | bytes 294920 | tf_op jit(solution)/shard_map/ppermute | solution.py:564
  29.0 21.1 %copy-start = (bf16[32,1024]{1,0:T(8,128)(2,1)S(1)}, bf16[32,1024]{1,0:T(8,128)(2,1)}, u32[]{:S(2)}) copy-start(bf16[32,1024]{1,0:T(8,128)(2,1)} %basis_hbm.5) | copy-start | bytes 196612
  36.9 25.9 %all-to-all-start.1 = ((bf16[128,4,128]{2,1,0:T(4,128)(2,1)}), bf16[128,4,128]{2,1,0:T(4,128)(2,1)S(1)}, u32[]{:S(2)}, u32[]{:S(2)}) async-start(bf16[128,4,128]{2,1,0:T(4,128)(2,1)} %bitcast.2), calls=%async_computation.1 | async-start | bytes 262144 | tf_op jit(solution)/shard_map/all_to_all | solution.py:558
  50.1 6.2 %copy-start.1 = (bf16[3,31,1024]{2,1,0:T(8,128)(2,1)S(1)}, bf16[3,31,1024]{2,1,0:T(8,128)(2,1)}, u32[]{:S(2)}) copy-start(bf16[3,31,1024]{2,1,0:T(8,128)(2,1)} %couple_hbm.5) | copy-start | bytes 571396
  50.8 6.2 %collective-permute-start.2 = (bf16[320,128]{1,0:T(8,128)(2,1)S(1)}, bf16[320,128]{1,0:T(8,128)(2,1)S(1)}, u32[]{:S(2)}, u32[]{:S(2)}) collective-permute-start(bf16[320,128]{1,0:T(8,128)(2,1)S(1)} %get-tuple-element.37), channel_id=1, source_target_pairs={{4,8},{8,4},{12,16},{16,12},{20,24},{24,20},{28,32},{32,28},{36,40... | collective-permute-start | bytes 245768 | tf_op jit(solution)/shard_map/ppermute | solution.py:563
  54.4 3.2 %collective-permute-start.3 = (bf16[320,128]{1,0:T(8,128)(2,1)S(1)}, bf16[320,128]{1,0:T(8,128)(2,1)S(1)}, u32[]{:S(2)}, u32[]{:S(2)}) collective-permute-start(bf16[320,128]{1,0:T(8,128)(2,1)S(1)} %get-tuple-element.38), channel_id=1, source_target_pairs={{0,4},{4,0},{8,12},{12,8},{16,20},{20,16},{24,28},{28,24},{32,36},... | collective-permute-start | bytes 245768 | tf_op jit(solution)/shard_map/ppermute | solution.py:564
  56.3 1.2 %copy-start.2 = (s32[12,16]{1,0:T(8,128)S(1)}, s32[12,16]{1,0:T(8,128)}, u32[]{:S(2)}) copy-start(s32[12,16]{1,0:T(8,128)} %cols_hbm.3) | copy-start | bytes 2308
